TPU v7x, 32 devices: a whole 2x2x4 slice. The times are simulated.
32 devices in a mesh: row: 8 (over z, core), col: 4 (over y, x).
Axes of the slice: x: 2, y: 2, z: 4, core: 2. Of those that a mesh axis runs over, the one named last changes fastest.
Arguments:
- tiles: bfloat16 [8, 4, 16, 512, 512], P('row', 'col'), as said below
- tile_rows: int32 [8, 4, 16], P('row', 'col'), may hold values from 0 to 11, as said below
- tile_cols: int32 [8, 4, 16], P('row', 'col'), may hold values from 0 to 11
- tile_counts: int32 [8, 4], P('row', 'col'), may hold values from 4 to 16, as said below
- sketch: bfloat16 [49152, 256], P(('row', 'col')), as said below
Outputs:
- basis: float32 [49152, 256], P(('row', 'col'))
- factor: float32 [256, 256], replicated
Inputs may be any that keep to these rules, and one draw needn't show every extreme that they name: Within one device's slots the pairs (tile_rows, tile_cols) are all different. `tile_counts`: some device uses all 16 slots in every draw. `tiles`: real valued tile entries of order one over the square root of a row's fan-in. `sketch`: real valued entries of order one.
All inputs are finite; a program needn't handle non-finite values.
Results may differ from a plain program's by a relative error of at most 0.0023.
Values may be sent and summed in bfloat16 or wider, within the bound.
No kernel may reach another device: no remote copies, remote signals or barrier semaphores. Data moves between devices by JAX's collectives and lax.ppermute only.
A program may use at most 64 MiB of HBM per device.

v0:
```python
import jax
import jax.numpy as jnp
from jax import lax
from jax.sharding import PartitionSpec as P

BR = 12
BC = 12


def body(tiles, tile_rows, tile_cols, tile_counts, sketch):
    tile_size = tiles.shape[-1]
    sketch_width = sketch.shape[1]
    local_tiles = tiles[0, 0]
    row_ids = tile_rows[0, 0]
    col_ids = tile_cols[0, 0]
    live_count = tile_counts[0, 0]
    gathered = lax.all_gather(sketch, "col", axis=0, tiled=True)

    def transposed_step(slot_index, running):
        matrix = lax.dynamic_index_in_dim(local_tiles, slot_index, 0, keepdims=False)
        sketch_block = lax.dynamic_slice_in_dim(
            gathered, row_ids[slot_index] * tile_size, tile_size, 0
        )
        product = lax.dot_general(
            matrix, sketch_block, (((0,), (0,)), ((), ())), preferred_element_type=jnp.float32
        )
        target = col_ids[slot_index] * tile_size
        current = lax.dynamic_slice_in_dim(running, target, tile_size, 0)
        return lax.dynamic_update_slice_in_dim(running, current + product, target, 0)

    partial_cols = lax.fori_loop(
        0, live_count, transposed_step, jnp.zeros((BC * tile_size, sketch_width), jnp.float32)
    )
    shared = lax.psum_scatter(partial_cols, "row", scatter_dimension=0, tiled=True).astype(
        jnp.bfloat16
    )
    columns = lax.all_gather(shared, "row", axis=0, tiled=True)

    def forward_step(slot_index, running):
        matrix = lax.dynamic_index_in_dim(local_tiles, slot_index, 0, keepdims=False)
        column_block = lax.dynamic_slice_in_dim(
            columns, col_ids[slot_index] * tile_size, tile_size, 0
        )
        product = jnp.dot(matrix, column_block, preferred_element_type=jnp.float32)
        target = row_ids[slot_index] * tile_size
        current = lax.dynamic_slice_in_dim(running, target, tile_size, 0)
        return lax.dynamic_update_slice_in_dim(running, current + product, target, 0)

    partial_rows = lax.fori_loop(
        0, live_count, forward_step, jnp.zeros((BR * tile_size, sketch_width), jnp.float32)
    )
    owned_rows = lax.psum_scatter(partial_rows, "col", scatter_dimension=0, tiled=True)
    total_rows = BR * tile_size * lax.axis_size("row")
    local_gram = jnp.dot(
        owned_rows.T,
        owned_rows,
        precision=lax.Precision.HIGHEST,
        preferred_element_type=jnp.float32,
    )
    gram_matrix = lax.psum(local_gram, ("row", "col")) / total_rows
    cholesky_lower = jnp.linalg.cholesky(gram_matrix)
    basis_rows = lax.linalg.triangular_solve(
        cholesky_lower, owned_rows, left_side=False, lower=True, transpose_a=True
    )
    return (basis_rows, cholesky_lower.T)


def solution(mesh):
    return jax.shard_map(
        body,
        mesh=mesh,
        in_specs=(
            P("row", "col", None, None, None),
            P("row", "col", None),
            P("row", "col", None),
            P("row", "col"),
            P(("row", "col"), None),
        ),
        out_specs=(P(("row", "col"), None), P()),
        check_vma=False,
    )
```

profile of v0, /device:TPU:0, one launch (start us, length us, event | category | flops | bytes accessed | tf_op | source)
XLA Modules:
  0.0 624.3 jit_solution(2240724171948778964)
XLA Ops:
  7.9 48.6 %all-gather.3.cloned.1.call-done = bf16[6144,256]{1,0:T(8,128)(2,1)} async-done(((bf16[1536,256]{1,0:T(8,128)(2,1)}), bf16[6144,256]{1,0:T(8,128)(2,1)}) %all-gather.3.cloned.1.call-update) | async-done | bytes 3145744 | tf_op jit(solution)/shard_map/all_gather | solution.py:17
  56.6 3.1 broadcast.98.clone
  59.6 90.0 %while.21 = (s32[]{:T(128)}, f32[6144,256]{1,0:T(8,128)}, s32[]{:T(128)}, s32[16]{0:T(128)S(1)}, bf16[16,512,512]{2,1,0:T(8,128)(2,1)}, /*index=5*/s32[16]{0:T(1...) while((s32[]{:T(128)}, f32[6144,256]{1,0:T(8,128)}, ...), condition=%wide.region_1.2_spmd, body=%wide.region_0.1_spmd.sunk | while | flops 134348816 | bytes 1835287 | solution.py:31
  62.8 2.4 fusion.37
  68.4 2.4 fusion.37
  74.0 2.4 fusion.37
  79.6 2.4 fusion.37
  85.2 2.4 fusion.37
  90.7 2.4 fusion.37
  96.3 2.4 fusion.37
  101.9 2.4 fusion.37
  107.5 2.4 fusion.37
  113.1 2.4 fusion.37
  118.7 2.4 fusion.37
  124.3 2.4 fusion.37
  129.8 2.4 fusion.37
  135.4 2.4 fusion.37
  141.0 2.4 fusion.37
  146.6 2.4 fusion.37
  149.7 69.0 %reduce-scatter.3.cloned.1.call-done = f32[768,256]{1,0:T(8,128)} async-done(((f32[6144,256]{1,0:T(8,128)}), f32[768,256]{1,0:T(8,128)}) %reduce-scatter.3.cloned.1.call-update) | async-done | bytes 786448 | tf_op jit(solution)/shard_map/reduce_scatter | solution.py:34
  218.7 1.9 convert_element_type.3
  220.7 36.9 %all-gather.5.cloned.1.call-done = bf16[6144,256]{1,0:T(8,128)(2,1)} async-done(((bf16[768,256]{1,0:T(8,128)(2,1)}), bf16[6144,256]{1,0:T(8,128)(2,1)}) %all-gather.5.cloned.1.call-update) | async-done | bytes 3145744 | tf_op jit(solution)/shard_map/all_gather | solution.py:37
  257.6 3.1 broadcast.98
  260.7 89.3 %while.22 = (s32[]{:T(128)}, f32[6144,256]{1,0:T(8,128)}, s32[]{:T(128)}, s32[16]{0:T(128)S(1)}, bf16[16,512,512]{2,1,0:T(8,128)(2,1)}, /*index=5*/s32[16]{0:T(1...) while((s32[]{:T(128)}, f32[6144,256]{1,0:T(8,128)}, ...), condition=%wide.region_4.5_spmd, body=%wide.region_3.4_spmd.sunk | while | flops 134348816 | bytes 1835287 | solution.py:49
  263.8 2.4 fusion.40
  269.4 2.4 fusion.40
  274.9 2.4 fusion.40
  280.5 2.4 fusion.40
  286.0 2.4 fusion.40
  291.5 2.4 fusion.40
  297.1 2.4 fusion.40
  302.6 2.4 fusion.40
  308.2 2.4 fusion.40
  313.7 2.4 fusion.40
  319.3 2.4 fusion.40
  324.8 2.4 fusion.40
  330.4 2.4 fusion.40
  335.9 2.4 fusion.40
  341.4 2.4 fusion.40
  347.0 2.4 fusion.40
  350.1 69.2 %reduce-scatter.5.cloned.1.call-done = f32[1536,256]{1,0:T(8,128)} async-done(((f32[6144,256]{1,0:T(8,128)}), f32[1536,256]{1,0:T(8,128)}) %reduce-scatter.5.cloned.1.call-update) | async-done | bytes 1572880 | tf_op jit(solution)/shard_map/reduce_scatter | solution.py:52
  419.3 5.3 fusion.21
  424.6 125.6 %all-reduce.3.cloned.1.call-done = f32[256,256]{0,1:T(8,128)} async-done(((f32[256,256]{0,1:T(8,128)}), f32[256,256]{0,1:T(8,128)}) %all-reduce.3.cloned.1.call-update) | async-done | bytes 262160 | tf_op jit(solution)/shard_map/psum | solution.py:60
  552.3 11.7 %cholesky.50 = f32[128,128]{1,0:T(8,128)S(1)} custom-call(f32[128,128]{1,0:T(8,128)S(1)} %cholesky.118), custom_call_target="Cholesky" | custom-call | tf_op jit(solution)/shard_map/jit(cholesky)/cholesky | solution.py:61
  564.1 9.8 %custom-call.14 = f32[1,128,128]{1,2,0:T(8,128)S(1)} custom-call(f32[1,128,128]{2,1,0:T(8,128)S(1)} %get-tuple-element.133), custom_call_target="InvertDiagBlocksLowerTriangular" | custom-call | tf_op jit(solution)/shard_map/jit(cholesky)/cholesky | solution.py:61
  574.4 11.9 %cholesky.105 = f32[128,128]{1,0:T(8,128)S(1)} custom-call(f32[128,128]{1,0:T(8,128)S(1)} %convolution_subtract_fusion.1), custom_call_target="Cholesky" | custom-call | tf_op jit(solution)/shard_map/jit(cholesky)/cholesky | solution.py:61
  588.4 4.0 while.23
  592.4 19.7 %custom-call.15 = f32[2,128,128]{1,2,0:T(8,128)S(1)} custom-call(f32[2,128,128]{2,1,0:T(8,128)S(1)} %get-tuple-element.87), custom_call_target="InvertDiagBlocksLowerTriangular" | custom-call | tf_op jit(solution)/shard_map/triangular_solve | solution.py:62
  (106 shorter events, 51.6 us)
Async XLA Ops:
  7.2 49.4 %all-gather.3.cloned.1.call-start = ((), (), s32[]{:S(2)}) async-start(), calls=%async_computation.2 | async-start | bytes 3932160 | tf_op jit(solution)/shard_map/all_gather | solution.py:17
  7.9 210.8 %reduce-scatter.3.cloned.1.call-start = ((), (), s32[]{:S(2)}) async-start(), calls=%async_computation.3 | async-start | bytes 7077888 | tf_op jit(solution)/shard_map/reduce_scatter | solution.py:34
  56.5 3.1 copy-start.1
  56.6 3.1 copy-start.2
  149.7 107.9 %all-gather.5.cloned.1.call-start = ((), (), s32[]{:S(2)}) async-start(), calls=%async_computation.4 | async-start | bytes 3538944 | tf_op jit(solution)/shard_map/all_gather | solution.py:37
  220.7 198.6 %reduce-scatter.5.cloned.1.call-start = ((), (), s32[]{:S(2)}) async-start(), calls=%async_computation.5 | async-start | bytes 7864320 | tf_op jit(solution)/shard_map/reduce_scatter | solution.py:52
  350.0 200.2 %all-reduce.3.cloned.1.call-start = ((), (), s32[]{:S(2)}) async-start(), calls=%async_computation.6 | async-start | bytes 524288 | tf_op jit(solution)/shard_map/psum | solution.py:60
  424.6 187.5 %copy-start = (f32[1536,256]{1,0:T(8,128)S(1)}, f32[1536,256]{1,0:T(8,128)}, u32[]{:S(2)}) copy-start(f32[1536,256]{1,0:T(8,128)} %reduce-scatter.5.cloned.1.call-done) | copy-start | bytes 4718596
Sparse Core Ops, SparseCore 0:
  9.8 46.6 all-gather.2
  149.8 68.8 reduce-scatter.2
  220.9 36.6 all-gather.4
  350.1 69.0 reduce-scatter.4
  425.2 124.9 all-reduce.2
where the time goes:
time: 626 us; the launch traced here: 624 us
  waiting for transfers between devices  350 us (56%)
  matrix products  85.9 us (14%)
  loops' own time  64.7 us (10%)
  other arithmetic  57.8 us (9%)
  local copies, waits for them, and re-layouts  50.4 us (8%)
  between operations  15.2 us (2%)
    psum x1, waiting for transfers between devices, body(): gram_matrix = lax.psum(local_gram, ('row', 'col')) / total_rows  126 us
    reduce_scatter x1, waiting for transfers between devices, body(): lax.psum_scatter(partial_rows, 'col', scatter_dimension=0, tiled=True)  69.2 us
    reduce_scatter x1, waiting for transfers between devices, body(): lax.psum_scatter(partial_cols, 'row', scatter_dimension=0, tiled=True)  69 us
    all_gather x1, waiting for transfers between devices, body(): gathered = lax.all_gather(sketch, 'col', axis=0, tiled=True)  48.6 us
    dot_general x16, matrix products, transposed_step(): lax.dot_general(matrix, sketch_block, (((0,), (0,)), ((), ())), preferred...  38.9 us
    dot_general x16, matrix products, forward_step(): product = jnp.dot(matrix, column_block, preferred_element_type=jnp.float32)  38.2 us
    all_gather x1, waiting for transfers between devices, body(): columns = lax.all_gather(shared, 'row', axis=0, tiled=True)  36.9 us
    another operation x6, other arithmetic, body(): cholesky_lower = jnp.linalg.cholesky(gram_matrix)  34.1 us
  transfers between devices with their start and end apart: 5, of which 5 were waited for; matrix products, arithmetic and copies ran while one was open for 0% of the time, Pallas kernels for 0%

commit v1 on v0

v1 whole, which is shorter than its diff:
```python
import jax
import jax.numpy as jnp
from jax import lax
from jax.experimental import pallas as pl
from jax.experimental.pallas import tpu as pltpu
from jax.sharding import PartitionSpec as P

BR = 12
BC = 12
GROUP = 16
VMEM_LIMIT = 52 * 1024 * 1024


def swap(value, axis, offset):
    size = lax.axis_size(axis)
    return lax.ppermute(value, axis, [(i, i ^ offset) for i in range(size)])


def fetch_tiles(count, tiles_ref, tile_buf, sems):
    slots = tiles_ref.shape[0]
    for slot in range(slots):
        @pl.when(slot < count)
        def _():
            pltpu.make_async_copy(tiles_ref.at[slot], tile_buf.at[slot], sems.at[slot]).start()


def wait_tile(slot, tiles_ref, tile_buf, sems):
    pltpu.make_async_copy(tiles_ref.at[slot], tile_buf.at[slot], sems.at[slot]).wait()


def transposed_kernel(count_ref, rows_ref, cols_ref, tiles_ref, *refs):
    pieces, (mine_ref, other_ref, sketch_buf, tile_buf, sems) = refs[:-5], refs[-5:]
    count = count_ref[0, 0]
    fetch_tiles(count, tiles_ref, tile_buf, sems)
    row_index, col_index = lax.axis_index("row"), lax.axis_index("col")
    tile_size = tiles_ref.shape[1]
    width = pieces[0].shape[1]
    groups = pieces[0].shape[0] // GROUP
    half = groups // 2
    core, place = row_index % 2, row_index // 2
    for offset, piece in enumerate(pieces):
        lanes = pl.ds(pl.multiple_of((col_index ^ offset) * width, 128), width)
        for group in range(groups):
            source = (core ^ (group // half)) * half + (place ^ (group % half))
            sketch_buf[pl.ds(group * GROUP, GROUP), lanes] = piece[
                pl.ds(pl.multiple_of(source * GROUP, GROUP), GROUP), :
            ]
    mine_ref[...] = jnp.zeros_like(mine_ref)
    other_ref[...] = jnp.zeros_like(other_ref)
    split = mine_ref.shape[0]

    def step(slot, carry):
        wait_tile(slot, tiles_ref, tile_buf, sems)
        block = sketch_buf[:, pl.ds(pl.multiple_of(rows_ref[0, 0, slot] * tile_size, 128), tile_size)]
        product = jnp.dot(block, tile_buf[slot], preferred_element_type=jnp.float32)
        lanes = pl.ds(pl.multiple_of(cols_ref[0, 0, slot] * tile_size, 128), tile_size)
        mine_ref[:, lanes] += product[:split]
        other_ref[:, lanes] += product[split:]
        return carry

    lax.fori_loop(0, count, step, 0)


def forward_kernel(count_ref, rows_ref, cols_ref, tiles_ref, *refs):
    pieces, (out_ref, column_buf, total, tile_buf, sems) = refs[:-5], refs[-5:]
    count = count_ref[0, 0]
    fetch_tiles(count, tiles_ref, tile_buf, sems)
    row_index, col_index = lax.axis_index("row"), lax.axis_index("col")
    tile_size = tiles_ref.shape[1]
    half = len(pieces) // 2
    core, place = row_index % 2, row_index // 2
    for offset, piece in enumerate(pieces):
        target = (core ^ (offset // half)) * half + (place ^ (offset % half))
        column_buf[pl.ds(pl.multiple_of(target * GROUP, GROUP), GROUP), :] = piece[...]
    total[...] = jnp.zeros_like(total)

    def step(slot, carry):
        wait_tile(slot, tiles_ref, tile_buf, sems)
        block = column_buf[:, pl.ds(pl.multiple_of(cols_ref[0, 0, slot] * tile_size, 128), tile_size)]
        product = lax.dot_general(
            tile_buf[slot], block, (((1,), (1,)), ((), ())), preferred_element_type=jnp.float32
        )
        total[pl.ds(pl.multiple_of(rows_ref[0, 0, slot] * tile_size, 128), tile_size), :] += product
        return carry

    lax.fori_loop(0, count, step, 0)
    width = out_ref.shape[1]
    for offset in range(out_ref.shape[0]):
        start = pl.multiple_of((col_index ^ offset) * width, 128)
        out_ref[offset] = total[pl.ds(start, width), :]


def tile_call(kernel, out_shape, scratch, counts, rows, cols, tiles, pieces):
    slots, tile_size, _ = tiles.shape
    smem = pl.BlockSpec(memory_space=pltpu.SMEM)
    vmem = pl.BlockSpec(memory_space=pltpu.VMEM)
    width = sum(p.shape[0] * p.shape[1] for p in pieces)
    return pl.pallas_call(
        kernel,
        out_shape=out_shape,
        in_specs=[smem, smem, smem, pl.BlockSpec(memory_space=pl.ANY)] + [vmem] * len(pieces),
        out_specs=jax.tree.map(lambda _: vmem, out_shape),
        scratch_shapes=scratch
        + [
            pltpu.VMEM((slots, tile_size, tile_size), jnp.bfloat16),
            pltpu.SemaphoreType.DMA((slots,)),
        ],
        compiler_params=pltpu.CompilerParams(vmem_limit_bytes=VMEM_LIMIT),
        cost_estimate=pl.CostEstimate(
            flops=2 * slots * tile_size * width // BR, bytes_accessed=2 * tiles.size, transcendentals=0
        ),
    )(counts, rows, cols, tiles, *pieces)


def gather_sketch(shard):
    return [shard] + [swap(shard, "col", d) for d in range(1, lax.axis_size("col"))]


def sum_columns(mine, other):
    places = lax.axis_size("row") // 2
    low = lambda d: d & -d
    arrived = swap(other.astype(jnp.float16), "row", 1)
    mine = mine + arrived.astype(jnp.float32)
    parts = {d: mine[d * GROUP : (d + 1) * GROUP] for d in range(places)}
    for d in range(places - 1, 0, -1):
        parts[d ^ low(d)] = parts[d ^ low(d)] + swap(
            parts[d].astype(jnp.float16), "row", 2 * low(d)
        ).astype(jnp.float32)
    whole = {0: parts[0].astype(jnp.bfloat16)}
    for d in sorted(range(1, places), key=lambda d: (bin(d).count("1"), -d)):
        whole[d] = swap(whole[d ^ low(d)], "row", 2 * low(d))
    near = [whole[d] for d in range(places)]
    return near + [swap(v, "row", 1) for v in near]


def sum_rows(parts):
    sent = parts[1:].astype(jnp.float16)
    total = parts[0]
    for d in range(1, parts.shape[0]):
        total = total + swap(sent[d - 1], "col", d).astype(jnp.float32)
    return total


def sum_everywhere(value):
    half = value.shape[0] // 2
    core = lax.axis_index("row") % 2
    mine = lax.dynamic_slice_in_dim(value, core * half, half, 0)
    other = lax.dynamic_slice_in_dim(value, (1 - core) * half, half, 0)
    mine = mine + swap(other, "row", 1)
    arrived = [swap(mine, "col", d) for d in range(1, lax.axis_size("col"))]
    stack = jnp.stack([mine] + arrived)
    mine = sum(
        lax.dynamic_index_in_dim(stack, lax.axis_index("col") ^ d, 0, keepdims=False)
        for d in range(lax.axis_size("col"))
    )
    bit = 2
    while bit < lax.axis_size("row"):
        mine = mine + swap(mine, "row", bit)
        bit *= 2
    other = swap(mine, "row", 1)
    return jnp.where(
        core == 0, jnp.concatenate([mine, other]), jnp.concatenate([other, mine])
    )


def body(tiles, tile_rows, tile_cols, tile_counts, sketch):
    tiles = tiles[0, 0]
    slots, tile_size, _ = tiles.shape
    width, sketch_width = sketch.shape
    chunk = min(sketch_width, GROUP * lax.axis_size("row"))
    group_rows, group_cols = BR * tile_size, BC * tile_size
    shard = sketch.T
    owned = []
    for start in range(0, sketch_width, chunk):
        pieces = gather_sketch(shard[start : start + chunk])
        half = jax.ShapeDtypeStruct((chunk // 2, group_cols), jnp.float32)
        mine, other = tile_call(
            transposed_kernel,
            (half, half),
            [pltpu.VMEM((chunk, group_rows), jnp.bfloat16)],
            tile_counts, tile_rows, tile_cols, tiles, pieces,
        )
        columns = sum_columns(mine, other)
        parts = tile_call(
            forward_kernel,
            jax.ShapeDtypeStruct((group_rows // width, width, chunk), jnp.float32),
            [pltpu.VMEM((chunk, group_cols), jnp.bfloat16), pltpu.VMEM((group_rows, chunk), jnp.float32)],
            tile_counts, tile_rows, tile_cols, tiles, columns,
        )
        owned.append(sum_rows(parts))
    owned_rows = jnp.concatenate(owned, axis=1)
    total_rows = group_rows * lax.axis_size("row")
    local_gram = jnp.dot(
        owned_rows.T, owned_rows, precision=lax.Precision.HIGHEST, preferred_element_type=jnp.float32
    )
    gram_matrix = sum_everywhere(local_gram) / total_rows
    cholesky_lower = jnp.linalg.cholesky(gram_matrix)
    basis_rows = lax.linalg.triangular_solve(
        cholesky_lower, owned_rows, left_side=False, lower=True, transpose_a=True
    )
    return (basis_rows, cholesky_lower.T)


def solution(mesh):
    return jax.shard_map(
        body,
        mesh=mesh,
        in_specs=(
            P("row", "col", None, None, None),
            P("row", "col", None),
            P("row", "col", None),
            P("row", "col"),
            P(("row", "col"), None),
        ),
        out_specs=(P(("row", "col"), None), P()),
        check_vma=False,
    )
```

time: 626 us -> 266 us (0.42)
  waiting for transfers between devices: 350 us -> 120 us
  matrix products: 85.9 us -> 6.21 us
  loops' own time: 64.7 us -> 0.03 us
  starting transfers between devices: 0.2 us -> 45.1 us
  local copies, waits for them, and re-layouts: 50.4 us -> 8.72 us
  Pallas kernels: 0 us -> 18.4 us
  between operations: 15.2 us -> 2.98 us
  other arithmetic: 57.8 us -> 64.8 us
    reduce_scatter x2 -> x0, waiting for transfers between devices: 138 us -> none  [the longest x1 69.2 us: body(): lax.psum_scatter(partial_rows, 'col', scatter_dimension=0, tiled=True)]
    psum x1 -> x0, waiting for transfers between devices: 126 us -> none  [body(): gram_matrix = lax.psum(local_gram, ('row', 'col')) / total_rows]
    ppermute x0 -> x41, waiting for transfers between devices: none -> 120 us  [swap(): return lax.ppermute(value, axis, [(i, i ^ offset) for i in range(size)])]
    all_gather x2 -> x0, waiting for transfers between devices: 85.5 us -> none  [the longest x1 48.6 us: body(): gathered = lax.all_gather(sketch, 'col', axis=0, tiled=True)]
    dot_general x32 -> x0, matrix products: 77.1 us -> none  [the longest x16 38.9 us: transposed_step(): lax.dot_general(matrix, sketch_block, (((0,), (0,)), ((), ())), preferred...]
    another operation x2 -> x0, loops' own time: 64.7 us -> none  [the longest x1 32.3 us: body(): lax.fori_loop(0, live_count, transposed_step, jnp.zeros((BC * tile_size,...]
    ppermute x0 -> x41, starting transfers between devices: none -> 45.1 us  [swap(): return lax.ppermute(value, axis, [(i, i ^ offset) for i in range(size)])]
    dynamic_slice x64 -> x1, local copies, waits for them, and re-layouts: 37.6 us -> 0.02 us  [sum_everywhere(): other = lax.dynamic_slice_in_dim(value, (1 - core) * half, half, 0)]
  transfers between devices with their start and end apart: 5 -> 41, of which waited for: 5 -> 21; matrix products, arithmetic and copies ran while one was open for 0% -> 3% of each run, Pallas kernels for 0% -> 5%
where the time goes in v1:
time: 266 us
  waiting for transfers between devices  120 us (45%)
  other arithmetic  64.8 us (24%)
  starting transfers between devices  45.1 us (17%)
  Pallas kernels  18.4 us (7%)
  local copies, waits for them, and re-layouts  8.72 us (3%)
  matrix products  6.21 us (2%)
  between operations  2.98 us (1%)
    ppermute x41, waiting for transfers between devices, swap(): return lax.ppermute(value, axis, [(i, i ^ offset) for i in range(size)])  120 us
    ppermute x41, starting transfers between devices, swap(): return lax.ppermute(value, axis, [(i, i ^ offset) for i in range(size)])  45.1 us
    another operation x6, other arithmetic, body(): cholesky_lower = jnp.linalg.cholesky(gram_matrix)  34.2 us
    another operation x3, other arithmetic, body(): lax.linalg.triangular_solve(cholesky_lower, owned_rows, left_side=False,...  19.8 us
    pallas_call x4, Pallas kernels, tile_call(): pl.pallas_call(kernel, out_shape=out_shape, in_specs=[smem, smem, smem, p...  18.4 us
  transfers between devices with their start and end apart: 41, of which 21 were waited for; matrix products, arithmetic and copies ran while one was open for 3% of the time, Pallas kernels for 5%

profile of v1, /device:TPU:0, one launch (start us, length us, event | category | flops | bytes accessed | tf_op | source)
XLA Modules:
  0.0 266.1 jit_solution(5508639089535909594)
XLA Ops:
  2.1 3.0 %collective-permute-start = (bf16[128,1536]{1,0:T(8,128)(2,1)S(1)}, bf16[128,1536]{1,0:T(8,128)(2,1)S(1)}, u32[]{:S(2)}, u32[]{:S(2)}) collective-permute-start(bf16[128,1536]{1,0:T(8,128)(2,1)S(1)} %get-tuple-element.42.refs_0_), channel_id=1, source_target_pairs={{0,1},{1,0},{2,3},{3,2},{4,5},{5,4},{6,7},{7,6},{8,9},{9,8},{10,11... | collective-permute-start | bytes 1179656 | tf_op jit(solution)/shard_map/ppermute | solution.py:16
  5.1 1.5 collective-permute-start.1
  7.3 7.7 %collective-permute-done.refs_1_ = bf16[128,1536]{1,0:T(8,128)(2,1)S(1)} collective-permute-done((bf16[128,1536]{1,0:T(8,128)(2,1)S(1)}, bf16[128,1536]{1,0:T(8,128)(2,1)S(1)}, u32[]{:S(2)}, u32[]{:S(2)}) %collective-permute-start) | collective-permute-done | bytes 393248 | tf_op jit(solution)/shard_map/ppermute | solution.py:16
  15.1 9.1 %collective-permute-done.1.refs_2_ = bf16[128,1536]{1,0:T(8,128)(2,1)S(1)} collective-permute-done((bf16[128,1536]{1,0:T(8,128)(2,1)S(1)}, bf16[128,1536]{1,0:T(8,128)(2,1)S(1)}, u32[]{:S(2)}, u32[]{:S(2)}) %collective-permute-start.1) | collective-permute-done | bytes 393248 | tf_op jit(solution)/shard_map/ppermute | solution.py:16
  24.1 4.3 %shard_map.68 = (f32[64,6144]{1,0:T(8,128)}, f32[64,6144]{1,0:T(8,128)}) custom-call(s32[1,1]{1,0:T(1,128)S(6)} %copy.24.count_ref, s32[1,1,16]{2,1,0:T(1,128)S(1)} %copy-done, s32[1,1,16]{2,1,0:T(1,128)S(1)} %copy-done.1, bf16[16,512,512]{2,1,0:T(8,128)(2,1)} %bitcast.72, bf16[128,1536]{1,0:T(8,128)(2,1)S(1)} %get-tuple-element.42.refs_0_, ...), custom_call_target="tpu_custom_call" | custom-call | flops 1073741824 | bytes 8388608 | tf_op jit(solution)/shard_map/pallas_call | solution.py:98
  28.5 1.5 convert_element_type.66
  31.2 2.3 collective-permute-start.17
  35.0 8.4 %collective-permute-done.17.refs_1_ = bf16[128,1536]{1,0:T(8,128)(2,1)S(1)} collective-permute-done((bf16[128,1536]{1,0:T(8,128)(2,1)S(1)}, bf16[128,1536]{1,0:T(8,128)(2,1)S(1)}, u32[]{:S(2)}, u32[]{:S(2)}) %collective-permute-start.17) | collective-permute-done | bytes 393248 | tf_op jit(solution)/shard_map/ppermute | solution.py:16
  43.4 9.6 %collective-permute-done.18.refs_2_ = bf16[128,1536]{1,0:T(8,128)(2,1)S(1)} collective-permute-done((bf16[128,1536]{1,0:T(8,128)(2,1)S(1)}, bf16[128,1536]{1,0:T(8,128)(2,1)S(1)}, u32[]{:S(2)}, u32[]{:S(2)}) %collective-permute-start.18) | collective-permute-done | bytes 393248 | tf_op jit(solution)/shard_map/ppermute | solution.py:16
  53.1 4.3 %shard_map.70 = (f32[64,6144]{1,0:T(8,128)}, f32[64,6144]{1,0:T(8,128)}) custom-call(s32[1,1]{1,0:T(1,128)S(6)} %copy.24.count_ref, s32[1,1,16]{2,1,0:T(1,128)S(1)} %copy-done, s32[1,1,16]{2,1,0:T(1,128)S(1)} %copy-done.1, bf16[16,512,512]{2,1,0:T(8,128)(2,1)} %bitcast.73, bf16[128,1536]{1,0:T(8,128)(2,1)S(1)} %get-tuple-element.43.refs_0_, ...), custom_call_target="tpu_custom_call" | custom-call | flops 1073741824 | bytes 8388608 | tf_op jit(solution)/shard_map/pallas_call | solution.py:98
  57.5 1.6 convert_element_type.76
  59.1 1.9 collective-permute-start.20
  65.8 3.3 %collective-permute-done.4 = f16[16,6144]{1,0:T(8,128)(2,1)S(1)} collective-permute-done((f16[16,6144]{1,0:T(8,128)(2,1)S(1)}, f16[16,6144]{1,0:T(8,128)(2,1)S(1)}, u32[]{:S(2)}, u32[]{:S(2)}) %collective-permute-start.4) | collective-permute-done | bytes 196640 | tf_op jit(solution)/shard_map/ppermute | solution.py:16
  69.2 3.1 %collective-permute-start.5 = (f16[16,6144]{1,0:T(8,128)(2,1)S(1)}, f16[16,6144]{1,0:T(8,128)(2,1)S(1)}, u32[]{:S(2)}, u32[]{:S(2)}) collective-permute-start(f16[16,6144]{1,0:T(8,128)(2,1)S(1)} %fusion.13), channel_id=1, source_target_pairs={{0,16},{4,20},{8,24},{12,28},{16,0},{20,4},{24,8},{28,12},{1,17},{... | collective-permute-start | bytes 589832 | tf_op jit(solution)/shard_map/ppermute | solution.py:16
  72.3 9.5 %collective-permute-done.21 = f16[16,6144]{1,0:T(8,128)(2,1)S(1)} collective-permute-done((f16[16,6144]{1,0:T(8,128)(2,1)S(1)}, f16[16,6144]{1,0:T(8,128)(2,1)S(1)}, u32[]{:S(2)}, u32[]{:S(2)}) %collective-permute-start.21) | collective-permute-done | bytes 196640 | tf_op jit(solution)/shard_map/ppermute | solution.py:16
  81.8 2.7 %collective-permute-start.22 = (f16[16,6144]{1,0:T(8,128)(2,1)S(1)}, f16[16,6144]{1,0:T(8,128)(2,1)S(1)}, u32[]{:S(2)}, u32[]{:S(2)}) collective-permute-start(f16[16,6144]{1,0:T(8,128)(2,1)S(1)} %fusion.10), channel_id=1, source_target_pairs={{0,16},{4,20},{8,24},{12,28},{16,0},{20,4},{24,8},{28,12},{1,17},{... | collective-permute-start | bytes 589832 | tf_op jit(solution)/shard_map/ppermute | solution.py:16
  84.6 2.8 %collective-permute-start.8 = (bf16[16,6144]{1,0:T(8,128)(2,1)S(1)}, bf16[16,6144]{1,0:T(8,128)(2,1)S(1)}, u32[]{:S(2)}, u32[]{:S(2)}) collective-permute-start(bf16[16,6144]{1,0:T(8,128)(2,1)S(1)} %fusion.15.refs_0_), channel_id=1, source_target_pairs={{0,16},{4,20},{8,24},{12,28},{16,0},{20,4},{24,8},{28,12},{1,17},{... | collective-permute-start | bytes 589832 | tf_op jit(solution)/shard_map/ppermute | solution.py:16
  87.4 1.9 collective-permute-start.7
  89.3 11.6 %collective-permute-done.22 = f16[16,6144]{1,0:T(8,128)(2,1)S(1)} collective-permute-done((f16[16,6144]{1,0:T(8,128)(2,1)S(1)}, f16[16,6144]{1,0:T(8,128)(2,1)S(1)}, u32[]{:S(2)}, u32[]{:S(2)}) %collective-permute-start.22) | collective-permute-done | bytes 196640 | tf_op jit(solution)/shard_map/ppermute | solution.py:16
  101.1 8.3 %collective-permute-done.8.refs_2_ = bf16[16,6144]{1,0:T(8,128)(2,1)S(1)} collective-permute-done((bf16[16,6144]{1,0:T(8,128)(2,1)S(1)}, bf16[16,6144]{1,0:T(8,128)(2,1)S(1)}, u32[]{:S(2)}, u32[]{:S(2)}) %collective-permute-start.8) | collective-permute-done | bytes 196640 | tf_op jit(solution)/shard_map/ppermute | solution.py:16
  109.4 2.0 collective-permute-start.24
  111.9 1.7 collective-permute-done.25.refs_2_
  113.6 4.2 %collective-permute-done.9.refs_3_ = bf16[16,6144]{1,0:T(8,128)(2,1)S(1)} collective-permute-done((bf16[16,6144]{1,0:T(8,128)(2,1)S(1)}, bf16[16,6144]{1,0:T(8,128)(2,1)S(1)}, u32[]{:S(2)}, u32[]{:S(2)}) %collective-permute-start.9) | collective-permute-done | bytes 196640 | tf_op jit(solution)/shard_map/ppermute | solution.py:16
  117.8 4.2 %collective-permute-done.24.refs_1_ = bf16[16,6144]{1,0:T(8,128)(2,1)S(1)} collective-permute-done((bf16[16,6144]{1,0:T(8,128)(2,1)S(1)}, bf16[16,6144]{1,0:T(8,128)(2,1)S(1)}, u32[]{:S(2)}, u32[]{:S(2)}) %collective-permute-start.24) | collective-permute-done | bytes 196640 | tf_op jit(solution)/shard_map/ppermute | solution.py:16
  122.6 3.5 %collective-permute-done.26.refs_3_ = bf16[16,6144]{1,0:T(8,128)(2,1)S(1)} collective-permute-done((bf16[16,6144]{1,0:T(8,128)(2,1)S(1)}, bf16[16,6144]{1,0:T(8,128)(2,1)S(1)}, u32[]{:S(2)}, u32[]{:S(2)}) %collective-permute-start.26) | collective-permute-done | bytes 196640 | tf_op jit(solution)/shard_map/ppermute | solution.py:16
  126.1 4.8 %shard_map.69 = f32[4,1536,128]{2,1,0:T(8,128)} custom-call(s32[1,1]{1,0:T(1,128)S(6)} %copy.24.count_ref, s32[1,1,16]{2,1,0:T(1,128)S(1)} %copy-done, s32[1,1,16]{2,1,0:T(1,128)S(1)} %copy-done.1, bf16[16,512,512]{2,1,0:T(8,128)(2,1)} %bitcast.74, bf16[16,6144]{1,0:T(8,128)(2,1)S(1)} %fusion.15.refs_0_, ...), custom_call_target="tpu_custom_call" | custom-call | flops 1073741824 | bytes 8388608 | tf_op jit(solution)/shard_map/pallas_call | solution.py:98
  130.9 2.1 convert.15
  133.3 3.3 %collective-permute-start.14 = (f16[1536,128]{1,0:T(8,128)(2,1)S(1)}, f16[1536,128]{1,0:T(8,128)(2,1)S(1)}, u32[]{:S(2)}, u32[]{:S(2)}) collective-permute-start(f16[1536,128]{1,0:T(8,128)(2,1)S(1)} %get-tuple-element.34), channel_id=1, source_target_pairs={{0,1},{1,0},{2,3},{3,2},{4,5},{5,4},{6,7},{7,6},{8,9},{9,8},{10,11... | collective-permute-start | bytes 1179656 | tf_op jit(solution)/shard_map/ppermute | solution.py:16
  136.6 1.5 collective-permute-start.15
  138.1 4.9 %shard_map.71 = f32[4,1536,128]{2,1,0:T(8,128)} custom-call(s32[1,1]{1,0:T(1,128)S(6)} %copy.24.count_ref, s32[1,1,16]{2,1,0:T(1,128)S(1)} %copy-done, s32[1,1,16]{2,1,0:T(1,128)S(1)} %copy-done.1, bf16[16,512,512]{2,1,0:T(8,128)(2,1)} %bitcast.75, bf16[16,6144]{1,0:T(8,128)(2,1)S(1)} %fusion.12.refs_0_, ...), custom_call_target="tpu_custom_call" | custom-call | flops 1073741824 | bytes 8388608 | tf_op jit(solution)/shard_map/pallas_call | solution.py:98
  143.0 2.1 convert.17
  145.4 4.7 %collective-permute-start.31 = (f16[1536,128]{1,0:T(8,128)(2,1)S(1)}, f16[1536,128]{1,0:T(8,128)(2,1)S(1)}, u32[]{:S(2)}, u32[]{:S(2)}) collective-permute-start(f16[1536,128]{1,0:T(8,128)(2,1)S(1)} %get-tuple-element.37), channel_id=1, source_target_pairs={{0,1},{1,0},{2,3},{3,2},{4,5},{5,4},{6,7},{7,6},{8,9},{9,8},{10,11... | collective-permute-start | bytes 1179656 | tf_op jit(solution)/shard_map/ppermute | solution.py:16
  151.6 5.3 %collective-permute-done.15 = f16[1536,128]{1,0:T(8,128)(2,1)S(1)} collective-permute-done((f16[1536,128]{1,0:T(8,128)(2,1)S(1)}, f16[1536,128]{1,0:T(8,128)(2,1)S(1)}, u32[]{:S(2)}, u32[]{:S(2)}) %collective-permute-start.15) | collective-permute-done | bytes 393248 | tf_op jit(solution)/shard_map/ppermute | solution.py:16
  158.2 4.7 %collective-permute-done.31 = f16[1536,128]{1,0:T(8,128)(2,1)S(1)} collective-permute-done((f16[1536,128]{1,0:T(8,128)(2,1)S(1)}, f16[1536,128]{1,0:T(8,128)(2,1)S(1)}, u32[]{:S(2)}, u32[]{:S(2)}) %collective-permute-start.31) | collective-permute-done | bytes 393248 | tf_op jit(solution)/shard_map/ppermute | solution.py:16
  162.9 10.3 %collective-permute-done.32 = f16[1536,128]{1,0:T(8,128)(2,1)S(1)} collective-permute-done((f16[1536,128]{1,0:T(8,128)(2,1)S(1)}, f16[1536,128]{1,0:T(8,128)(2,1)S(1)}, u32[]{:S(2)}, u32[]{:S(2)}) %collective-permute-start.32) | collective-permute-done | bytes 393248 | tf_op jit(solution)/shard_map/ppermute | solution.py:16
  174.5 2.6 fusion
  179.0 1.6 collective-permute-start.36
  180.6 1.5 collective-permute-start.37
  182.2 2.9 %collective-permute-done.35 = f32[128,256]{0,1:T(8,128)S(1)} collective-permute-done((f32[128,256]{0,1:T(8,128)S(1)}, f32[128,256]{0,1:T(8,128)S(1)}, u32[]{:S(2)}, u32[]{:S(2)}) %collective-permute-start.35) | collective-permute-done | bytes 131104 | tf_op jit(solution)/shard_map/ppermute | solution.py:16
  185.0 2.1 collective-permute-done.36
  187.3 5.0 %collective-permute-done.38 = f32[128,256]{0,1:T(8,128)S(1)} collective-permute-done((f32[128,256]{0,1:T(8,128)S(1)}, f32[128,256]{0,1:T(8,128)S(1)}, u32[]{:S(2)}, u32[]{:S(2)}) %collective-permute-start.38) | collective-permute-done | bytes 131104 | tf_op jit(solution)/shard_map/ppermute | solution.py:16
  193.1 5.9 %collective-permute-done.39 = f32[128,256]{0,1:T(8,128)S(1)} collective-permute-done((f32[128,256]{0,1:T(8,128)S(1)}, f32[128,256]{0,1:T(8,128)S(1)}, u32[]{:S(2)}, u32[]{:S(2)}) %collective-permute-start.39) | collective-permute-done | bytes 131104 | tf_op jit(solution)/shard_map/ppermute | solution.py:16
  200.7 11.7 %cholesky.50 = f32[128,128]{1,0:T(8,128)S(1)} custom-call(f32[128,128]{1,0:T(8,128)S(1)} %cholesky.118), custom_call_target="Cholesky" | custom-call | tf_op jit(solution)/shard_map/jit(cholesky)/cholesky | solution.py:197
  212.5 9.8 %custom-call.14 = f32[1,128,128]{1,2,0:T(8,128)S(1)} custom-call(f32[1,128,128]{2,1,0:T(8,128)S(1)} %get-tuple-element.51), custom_call_target="InvertDiagBlocksLowerTriangular" | custom-call | tf_op jit(solution)/shard_map/jit(cholesky)/cholesky | solution.py:197
  222.8 11.9 %cholesky.105 = f32[128,128]{1,0:T(8,128)S(1)} custom-call(f32[128,128]{1,0:T(8,128)S(1)} %convolution_subtract_fusion.1), custom_call_target="Cholesky" | custom-call | tf_op jit(solution)/shard_map/jit(cholesky)/cholesky | solution.py:197
  236.8 4.0 %while.1 = (s32[]{:T(128)}, f32[256,256]{1,0:T(8,128)S(1)}, s32[2,2]{1,0:T(2,128)S(1)}, f32[2,128,128]{2,1,0:T(8,128)S(1)}, s32[]{:T(128)}) while((s32[]{:T(128)}, f32[256,256]{1,0:T(8,128)S(1)}, s32[2,2]{1,0:T(2,128)S(1)}, f32[2,128,128]{2,1,0:T(8,128)S(1)}, s32[]{:T(128)}) %tuple.38), condition=%wide.while_cond, body=%wide.while_body.sunk | while | flops 2 | bytes 131181 | solution.py:198
  240.8 19.7 %custom-call.15 = f32[2,128,128]{1,2,0:T(8,128)S(1)} custom-call(f32[2,128,128]{2,1,0:T(8,128)S(1)} %get-tuple-element.17), custom_call_target="InvertDiagBlocksLowerTriangular" | custom-call | tf_op jit(solution)/shard_map/triangular_solve | solution.py:198
  263.7 1.6 copy.11
  (102 shorter events, 28.9 us)
Async XLA Ops:
  0.6 23.5 %copy-start = (s32[1,1,16]{2,1,0:T(1,128)S(1)}, s32[1,1,16]{2,1,0:T(1,128)}, u32[]{:S(2)}) copy-start(s32[1,1,16]{2,1,0:T(1,128)} %rows_ref.7) | copy-start | bytes 196
  0.6 23.5 %copy-start.1 = (s32[1,1,16]{2,1,0:T(1,128)S(1)}, s32[1,1,16]{2,1,0:T(1,128)}, u32[]{:S(2)}) copy-start(s32[1,1,16]{2,1,0:T(1,128)} %cols_ref.7) | copy-start | bytes 196
  2.1 12.9 %collective-permute-start = (bf16[128,1536]{1,0:T(8,128)(2,1)S(1)}, bf16[128,1536]{1,0:T(8,128)(2,1)S(1)}, u32[]{:S(2)}, u32[]{:S(2)}) collective-permute-start(bf16[128,1536]{1,0:T(8,128)(2,1)S(1)} %get-tuple-element.42.refs_0_), channel_id=1, source_target_pairs={{0,1},{1,0},{2,3},{3,2},{4,5},{5,4},{6,7},{7,6},{8,9},{9,8},{10,11... | collective-permute-start | bytes 1179656 | tf_op jit(solution)/shard_map/ppermute | solution.py:16
  5.1 19.0 %collective-permute-start.1 = (bf16[128,1536]{1,0:T(8,128)(2,1)S(1)}, bf16[128,1536]{1,0:T(8,128)(2,1)S(1)}, u32[]{:S(2)}, u32[]{:S(2)}) collective-permute-start(bf16[128,1536]{1,0:T(8,128)(2,1)S(1)} %get-tuple-element.42.refs_0_), channel_id=1, source_target_pairs={{0,2},{1,3},{2,0},{3,1},{4,6},{5,7},{6,4},{7,5},{8,10},{9,11},{10,... | collective-permute-start | bytes 1179656 | tf_op jit(solution)/shard_map/ppermute | solution.py:16
  6.7 17.5 %collective-permute-start.2 = (bf16[128,1536]{1,0:T(8,128)(2,1)S(1)}, bf16[128,1536]{1,0:T(8,128)(2,1)S(1)}, u32[]{:S(2)}, u32[]{:S(2)}) collective-permute-start(bf16[128,1536]{1,0:T(8,128)(2,1)S(1)} %get-tuple-element.42.refs_0_), channel_id=1, source_target_pairs={{0,3},{1,2},{2,1},{3,0},{4,7},{5,6},{6,5},{7,4},{8,11},{9,10},{10,... | collective-permute-start | bytes 1179656 | tf_op jit(solution)/shard_map/ppermute | solution.py:16
  30.0 31.0 %collective-permute-start.3 = (f16[64,6144]{1,0:T(8,128)(2,1)S(1)}, f16[64,6144]{1,0:T(8,128)(2,1)S(1)}, u32[]{:S(2)}, u32[]{:S(2)}) collective-permute-start(f16[64,6144]{1,0:T(8,128)(2,1)S(1)} %convert_element_type.66), channel_id=1, source_target_pairs={{0,4},{4,0},{8,12},{12,8},{16,20},{20,16},{24,28},{28,24},{1,5},{5... | collective-permute-start | bytes 2359304 | tf_op jit(solution)/shard_map/ppermute | solution.py:16
  31.2 12.3 %collective-permute-start.17 = (bf16[128,1536]{1,0:T(8,128)(2,1)S(1)}, bf16[128,1536]{1,0:T(8,128)(2,1)S(1)}, u32[]{:S(2)}, u32[]{:S(2)}) collective-permute-start(bf16[128,1536]{1,0:T(8,128)(2,1)S(1)} %get-tuple-element.43.refs_0_), channel_id=1, source_target_pairs={{0,1},{1,0},{2,3},{3,2},{4,5},{5,4},{6,7},{7,6},{8,9},{9,8},{10,11... | collective-permute-start | bytes 1179656 | tf_op jit(solution)/shard_map/ppermute | solution.py:16
  33.5 19.6 %collective-permute-start.18 = (bf16[128,1536]{1,0:T(8,128)(2,1)S(1)}, bf16[128,1536]{1,0:T(8,128)(2,1)S(1)}, u32[]{:S(2)}, u32[]{:S(2)}) collective-permute-start(bf16[128,1536]{1,0:T(8,128)(2,1)S(1)} %get-tuple-element.43.refs_0_), channel_id=1, source_target_pairs={{0,2},{1,3},{2,0},{3,1},{4,6},{5,7},{6,4},{7,5},{8,10},{9,11},{10,... | collective-permute-start | bytes 1179656 | tf_op jit(solution)/shard_map/ppermute | solution.py:16
  34.3 18.8 %collective-permute-start.19 = (bf16[128,1536]{1,0:T(8,128)(2,1)S(1)}, bf16[128,1536]{1,0:T(8,128)(2,1)S(1)}, u32[]{:S(2)}, u32[]{:S(2)}) collective-permute-start(bf16[128,1536]{1,0:T(8,128)(2,1)S(1)} %get-tuple-element.43.refs_0_), channel_id=1, source_target_pairs={{0,3},{1,2},{2,1},{3,0},{4,7},{5,6},{6,5},{7,4},{8,11},{9,10},{10,... | collective-permute-start | bytes 1179656 | tf_op jit(solution)/shard_map/ppermute | solution.py:16
  57.4 3.5 %copy-start.2 = (f32[64,6144]{1,0:T(8,128)S(1)}, f32[64,6144]{1,0:T(8,128)}, u32[]{:S(2)}) copy-start(f32[64,6144]{1,0:T(8,128)} %get-tuple-element.6) | copy-start | bytes 4718596
  59.1 4.3 %collective-permute-start.20 = (f16[64,6144]{1,0:T(8,128)(2,1)S(1)}, f16[64,6144]{1,0:T(8,128)(2,1)S(1)}, u32[]{:S(2)}, u32[]{:S(2)}) collective-permute-start(f16[64,6144]{1,0:T(8,128)(2,1)S(1)} %convert_element_type.76), channel_id=1, source_target_pairs={{0,4},{4,0},{8,12},{12,8},{16,20},{20,16},{24,28},{28,24},{1,5},{5... | collective-permute-start | bytes 2359304 | tf_op jit(solution)/shard_map/ppermute | solution.py:16
  61.0 2.4 copy-start.3
  61.3 7.8 %collective-permute-start.4 = (f16[16,6144]{1,0:T(8,128)(2,1)S(1)}, f16[16,6144]{1,0:T(8,128)(2,1)S(1)}, u32[]{:S(2)}, u32[]{:S(2)}) collective-permute-start(f16[16,6144]{1,0:T(8,128)(2,1)S(1)} %get-tuple-element.40), channel_id=1, source_target_pairs={{0,8},{4,12},{8,0},{12,4},{16,24},{20,28},{24,16},{28,20},{1,9},{5... | collective-permute-start | bytes 589832 | tf_op jit(solution)/shard_map/ppermute | solution.py:16
  62.3 22.3 %collective-permute-start.6 = (f16[16,6144]{1,0:T(8,128)(2,1)S(1)}, f16[16,6144]{1,0:T(8,128)(2,1)S(1)}, u32[]{:S(2)}, u32[]{:S(2)}) collective-permute-start(f16[16,6144]{1,0:T(8,128)(2,1)S(1)} %get-tuple-element.41), channel_id=1, source_target_pairs={{0,8},{4,12},{8,0},{12,4},{16,24},{20,28},{24,16},{28,20},{1,9},{5... | collective-permute-start | bytes 589832 | tf_op jit(solution)/shard_map/ppermute | solution.py:16
  63.7 18.0 %collective-permute-start.21 = (f16[16,6144]{1,0:T(8,128)(2,1)S(1)}, f16[16,6144]{1,0:T(8,128)(2,1)S(1)}, u32[]{:S(2)}, u32[]{:S(2)}) collective-permute-start(f16[16,6144]{1,0:T(8,128)(2,1)S(1)} %get-tuple-element.44), channel_id=1, source_target_pairs={{0,8},{4,12},{8,0},{12,4},{16,24},{20,28},{24,16},{28,20},{1,9},{5... | collective-permute-start | bytes 589832 | tf_op jit(solution)/shard_map/ppermute | solution.py:16
  64.7 24.7 %collective-permute-start.23 = (f16[16,6144]{1,0:T(8,128)(2,1)S(1)}, f16[16,6144]{1,0:T(8,128)(2,1)S(1)}, u32[]{:S(2)}, u32[]{:S(2)}) collective-permute-start(f16[16,6144]{1,0:T(8,128)(2,1)S(1)} %get-tuple-element.45), channel_id=1, source_target_pairs={{0,8},{4,12},{8,0},{12,4},{16,24},{20,28},{24,16},{28,20},{1,9},{5... | collective-permute-start | bytes 589832 | tf_op jit(solution)/shard_map/ppermute | solution.py:16
  69.2 15.4 %collective-permute-start.5 = (f16[16,6144]{1,0:T(8,128)(2,1)S(1)}, f16[16,6144]{1,0:T(8,128)(2,1)S(1)}, u32[]{:S(2)}, u32[]{:S(2)}) collective-permute-start(f16[16,6144]{1,0:T(8,128)(2,1)S(1)} %fusion.13), channel_id=1, source_target_pairs={{0,16},{4,20},{8,24},{12,28},{16,0},{20,4},{24,8},{28,12},{1,17},{... | collective-permute-start | bytes 589832 | tf_op jit(solution)/shard_map/ppermute | solution.py:16
  81.8 19.1 %collective-permute-start.22 = (f16[16,6144]{1,0:T(8,128)(2,1)S(1)}, f16[16,6144]{1,0:T(8,128)(2,1)S(1)}, u32[]{:S(2)}, u32[]{:S(2)}) collective-permute-start(f16[16,6144]{1,0:T(8,128)(2,1)S(1)} %fusion.10), channel_id=1, source_target_pairs={{0,16},{4,20},{8,24},{12,28},{16,0},{20,4},{24,8},{28,12},{1,17},{... | collective-permute-start | bytes 589832 | tf_op jit(solution)/shard_map/ppermute | solution.py:16
  84.6 24.8 %collective-permute-start.8 = (bf16[16,6144]{1,0:T(8,128)(2,1)S(1)}, bf16[16,6144]{1,0:T(8,128)(2,1)S(1)}, u32[]{:S(2)}, u32[]{:S(2)}) collective-permute-start(bf16[16,6144]{1,0:T(8,128)(2,1)S(1)} %fusion.15.refs_0_), channel_id=1, source_target_pairs={{0,16},{4,20},{8,24},{12,28},{16,0},{20,4},{24,8},{28,12},{1,17},{... | collective-permute-start | bytes 589832 | tf_op jit(solution)/shard_map/ppermute | solution.py:16
  87.4 24.0 %collective-permute-start.7 = (bf16[16,6144]{1,0:T(8,128)(2,1)S(1)}, bf16[16,6144]{1,0:T(8,128)(2,1)S(1)}, u32[]{:S(2)}, u32[]{:S(2)}) collective-permute-start(bf16[16,6144]{1,0:T(8,128)(2,1)S(1)} %fusion.15.refs_0_), channel_id=1, source_target_pairs={{0,8},{4,12},{8,0},{12,4},{16,24},{20,28},{24,16},{28,20},{1,9},{5... | collective-permute-start | bytes 589832 | tf_op jit(solution)/shard_map/ppermute | solution.py:16
  89.3 22.0 %collective-permute-start.10 = (bf16[16,6144]{1,0:T(8,128)(2,1)S(1)}, bf16[16,6144]{1,0:T(8,128)(2,1)S(1)}, u32[]{:S(2)}, u32[]{:S(2)}) collective-permute-start(bf16[16,6144]{1,0:T(8,128)(2,1)S(1)} %fusion.15.refs_0_), channel_id=1, source_target_pairs={{0,4},{4,0},{8,12},{12,8},{16,20},{20,16},{24,28},{28,24},{1,5},{5... | collective-permute-start | bytes 589832 | tf_op jit(solution)/shard_map/ppermute | solution.py:16
  101.0 12.6 %collective-permute-start.25 = (bf16[16,6144]{1,0:T(8,128)(2,1)S(1)}, bf16[16,6144]{1,0:T(8,128)(2,1)S(1)}, u32[]{:S(2)}, u32[]{:S(2)}) collective-permute-start(bf16[16,6144]{1,0:T(8,128)(2,1)S(1)} %fusion.12.refs_0_), channel_id=1, source_target_pairs={{0,16},{4,20},{8,24},{12,28},{16,0},{20,4},{24,8},{28,12},{1,17},{... | collective-permute-start | bytes 589832 | tf_op jit(solution)/shard_map/ppermute | solution.py:16
  109.3 8.4 %collective-permute-start.9 = (bf16[16,6144]{1,0:T(8,128)(2,1)S(1)}, bf16[16,6144]{1,0:T(8,128)(2,1)S(1)}, u32[]{:S(2)}, u32[]{:S(2)}) collective-permute-start(bf16[16,6144]{1,0:T(8,128)(2,1)S(1)} %collective-permute-done.8.refs_2_), channel_id=1, source_target_pairs={{0,8},{4,12},{8,0},{12,4},{16,24},{20,28},{24,16},{28,20},{1,9},{5... | collective-permute-start | bytes 589832 | tf_op jit(solution)/shard_map/ppermute | solution.py:16
  109.4 12.6 %collective-permute-start.24 = (bf16[16,6144]{1,0:T(8,128)(2,1)S(1)}, bf16[16,6144]{1,0:T(8,128)(2,1)S(1)}, u32[]{:S(2)}, u32[]{:S(2)}) collective-permute-start(bf16[16,6144]{1,0:T(8,128)(2,1)S(1)} %fusion.12.refs_0_), channel_id=1, source_target_pairs={{0,8},{4,12},{8,0},{12,4},{16,24},{20,28},{24,16},{28,20},{1,9},{5... | collective-permute-start | bytes 589832 | tf_op jit(solution)/shard_map/ppermute | solution.py:16
  111.4 10.6 %collective-permute-start.12 = (bf16[16,6144]{1,0:T(8,128)(2,1)S(1)}, bf16[16,6144]{1,0:T(8,128)(2,1)S(1)}, u32[]{:S(2)}, u32[]{:S(2)}) collective-permute-start(bf16[16,6144]{1,0:T(8,128)(2,1)S(1)} %collective-permute-done.8.refs_2_), channel_id=1, source_target_pairs={{0,4},{4,0},{8,12},{12,8},{16,20},{20,16},{24,28},{28,24},{1,5},{5... | collective-permute-start | bytes 589832 | tf_op jit(solution)/shard_map/ppermute | solution.py:16
  111.4 11.1 %collective-permute-start.11 = (bf16[16,6144]{1,0:T(8,128)(2,1)S(1)}, bf16[16,6144]{1,0:T(8,128)(2,1)S(1)}, u32[]{:S(2)}, u32[]{:S(2)}) collective-permute-start(bf16[16,6144]{1,0:T(8,128)(2,1)S(1)} %collective-permute-done.7.refs_1_), channel_id=1, source_target_pairs={{0,4},{4,0},{8,12},{12,8},{16,20},{20,16},{24,28},{28,24},{1,5},{5... | collective-permute-start | bytes 589832 | tf_op jit(solution)/shard_map/ppermute | solution.py:16
  113.6 12.5 %collective-permute-start.26 = (bf16[16,6144]{1,0:T(8,128)(2,1)S(1)}, bf16[16,6144]{1,0:T(8,128)(2,1)S(1)}, u32[]{:S(2)}, u32[]{:S(2)}) collective-permute-start(bf16[16,6144]{1,0:T(8,128)(2,1)S(1)} %collective-permute-done.25.refs_2_), channel_id=1, source_target_pairs={{0,8},{4,12},{8,0},{12,4},{16,24},{20,28},{24,16},{28,20},{1,9},{5... | collective-permute-start | bytes 589832 | tf_op jit(solution)/shard_map/ppermute | solution.py:16
  117.8 8.4 %collective-permute-start.13 = (bf16[16,6144]{1,0:T(8,128)(2,1)S(1)}, bf16[16,6144]{1,0:T(8,128)(2,1)S(1)}, u32[]{:S(2)}, u32[]{:S(2)}) collective-permute-start(bf16[16,6144]{1,0:T(8,128)(2,1)S(1)} %collective-permute-done.9.refs_3_), channel_id=1, source_target_pairs={{0,4},{4,0},{8,12},{12,8},{16,20},{20,16},{24,28},{28,24},{1,5},{5... | collective-permute-start | bytes 589832 | tf_op jit(solution)/shard_map/ppermute | solution.py:16
  122.0 14.6 %collective-permute-start.27 = (bf16[16,6144]{1,0:T(8,128)(2,1)S(1)}, bf16[16,6144]{1,0:T(8,128)(2,1)S(1)}, u32[]{:S(2)}, u32[]{:S(2)}) collective-permute-start(bf16[16,6144]{1,0:T(8,128)(2,1)S(1)} %fusion.12.refs_0_), channel_id=1, source_target_pairs={{0,4},{4,0},{8,12},{12,8},{16,20},{20,16},{24,28},{28,24},{1,5},{5... | collective-permute-start | bytes 589832 | tf_op jit(solution)/shard_map/ppermute | solution.py:16
  122.0 16.0 %collective-permute-start.29 = (bf16[16,6144]{1,0:T(8,128)(2,1)S(1)}, bf16[16,6144]{1,0:T(8,128)(2,1)S(1)}, u32[]{:S(2)}, u32[]{:S(2)}) collective-permute-start(bf16[16,6144]{1,0:T(8,128)(2,1)S(1)} %collective-permute-done.25.refs_2_), channel_id=1, source_target_pairs={{0,4},{4,0},{8,12},{12,8},{16,20},{20,16},{24,28},{28,24},{1,5},{5... | collective-permute-start | bytes 589832 | tf_op jit(solution)/shard_map/ppermute | solution.py:16
  122.5 15.6 %collective-permute-start.28 = (bf16[16,6144]{1,0:T(8,128)(2,1)S(1)}, bf16[16,6144]{1,0:T(8,128)(2,1)S(1)}, u32[]{:S(2)}, u32[]{:S(2)}) collective-permute-start(bf16[16,6144]{1,0:T(8,128)(2,1)S(1)} %collective-permute-done.24.refs_1_), channel_id=1, source_target_pairs={{0,4},{4,0},{8,12},{12,8},{16,20},{20,16},{24,28},{28,24},{1,5},{5... | collective-permute-start | bytes 589832 | tf_op jit(solution)/shard_map/ppermute | solution.py:16
  126.1 12.0 %collective-permute-start.30 = (bf16[16,6144]{1,0:T(8,128)(2,1)S(1)}, bf16[16,6144]{1,0:T(8,128)(2,1)S(1)}, u32[]{:S(2)}, u32[]{:S(2)}) collective-permute-start(bf16[16,6144]{1,0:T(8,128)(2,1)S(1)} %collective-permute-done.26.refs_3_), channel_id=1, source_target_pairs={{0,4},{4,0},{8,12},{12,8},{16,20},{20,16},{24,28},{28,24},{1,5},{5... | collective-permute-start | bytes 589832 | tf_op jit(solution)/shard_map/ppermute | solution.py:16
  133.3 18.3 %collective-permute-start.14 = (f16[1536,128]{1,0:T(8,128)(2,1)S(1)}, f16[1536,128]{1,0:T(8,128)(2,1)S(1)}, u32[]{:S(2)}, u32[]{:S(2)}) collective-permute-start(f16[1536,128]{1,0:T(8,128)(2,1)S(1)} %get-tuple-element.34), channel_id=1, source_target_pairs={{0,1},{1,0},{2,3},{3,2},{4,5},{5,4},{6,7},{7,6},{8,9},{9,8},{10,11... | collective-permute-start | bytes 1179656 | tf_op jit(solution)/shard_map/ppermute | solution.py:16
  136.6 20.4 %collective-permute-start.15 = (f16[1536,128]{1,0:T(8,128)(2,1)S(1)}, f16[1536,128]{1,0:T(8,128)(2,1)S(1)}, u32[]{:S(2)}, u32[]{:S(2)}) collective-permute-start(f16[1536,128]{1,0:T(8,128)(2,1)S(1)} %get-tuple-element.36), channel_id=1, source_target_pairs={{0,2},{1,3},{2,0},{3,1},{4,6},{5,7},{6,4},{7,5},{8,10},{9,11},{10,... | collective-permute-start | bytes 1179656 | tf_op jit(solution)/shard_map/ppermute | solution.py:16
  138.0 18.9 %collective-permute-start.16 = (f16[1536,128]{1,0:T(8,128)(2,1)S(1)}, f16[1536,128]{1,0:T(8,128)(2,1)S(1)}, u32[]{:S(2)}, u32[]{:S(2)}) collective-permute-start(f16[1536,128]{1,0:T(8,128)(2,1)S(1)} %get-tuple-element.35), channel_id=1, source_target_pairs={{0,3},{1,2},{2,1},{3,0},{4,7},{5,6},{6,5},{7,4},{8,11},{9,10},{10,... | collective-permute-start | bytes 1179656 | tf_op jit(solution)/shard_map/ppermute | solution.py:16
  145.4 17.5 %collective-permute-start.31 = (f16[1536,128]{1,0:T(8,128)(2,1)S(1)}, f16[1536,128]{1,0:T(8,128)(2,1)S(1)}, u32[]{:S(2)}, u32[]{:S(2)}) collective-permute-start(f16[1536,128]{1,0:T(8,128)(2,1)S(1)} %get-tuple-element.37), channel_id=1, source_target_pairs={{0,1},{1,0},{2,3},{3,2},{4,5},{5,4},{6,7},{7,6},{8,9},{9,8},{10,11... | collective-permute-start | bytes 1179656 | tf_op jit(solution)/shard_map/ppermute | solution.py:16
  150.1 23.1 %collective-permute-start.32 = (f16[1536,128]{1,0:T(8,128)(2,1)S(1)}, f16[1536,128]{1,0:T(8,128)(2,1)S(1)}, u32[]{:S(2)}, u32[]{:S(2)}) collective-permute-start(f16[1536,128]{1,0:T(8,128)(2,1)S(1)} %get-tuple-element.39), channel_id=1, source_target_pairs={{0,2},{1,3},{2,0},{3,1},{4,6},{5,7},{6,4},{7,5},{8,10},{9,11},{10,... | collective-permute-start | bytes 1179656 | tf_op jit(solution)/shard_map/ppermute | solution.py:16
  151.6 21.6 %collective-permute-start.33 = (f16[1536,128]{1,0:T(8,128)(2,1)S(1)}, f16[1536,128]{1,0:T(8,128)(2,1)S(1)}, u32[]{:S(2)}, u32[]{:S(2)}) collective-permute-start(f16[1536,128]{1,0:T(8,128)(2,1)S(1)} %get-tuple-element.38), channel_id=1, source_target_pairs={{0,3},{1,2},{2,1},{3,0},{4,7},{5,6},{6,5},{7,4},{8,11},{9,10},{10,... | collective-permute-start | bytes 1179656 | tf_op jit(solution)/shard_map/ppermute | solution.py:16
  177.2 1.4 collective-permute-start.34
  178.6 6.4 %collective-permute-start.35 = (f32[128,256]{0,1:T(8,128)S(1)}, f32[128,256]{0,1:T(8,128)S(1)}, u32[]{:S(2)}, u32[]{:S(2)}) collective-permute-start(f32[128,256]{0,1:T(8,128)S(1)} %dynamic-slice_add_fusion), channel_id=1, source_target_pairs={{0,1},{1,0},{2,3},{3,2},{4,5},{5,4},{6,7},{7,6},{8,9},{9,8},{10,11... | collective-permute-start | bytes 393224 | tf_op jit(solution)/shard_map/ppermute | solution.py:16
  179.0 8.1 %collective-permute-start.36 = (f32[128,256]{0,1:T(8,128)S(1)}, f32[128,256]{0,1:T(8,128)S(1)}, u32[]{:S(2)}, u32[]{:S(2)}) collective-permute-start(f32[128,256]{0,1:T(8,128)S(1)} %dynamic-slice_add_fusion), channel_id=1, source_target_pairs={{0,2},{1,3},{2,0},{3,1},{4,6},{5,7},{6,4},{7,5},{8,10},{9,11},{10,... | collective-permute-start | bytes 393224 | tf_op jit(solution)/shard_map/ppermute | solution.py:16
  180.6 6.5 %collective-permute-start.37 = (f32[128,256]{0,1:T(8,128)S(1)}, f32[128,256]{0,1:T(8,128)S(1)}, u32[]{:S(2)}, u32[]{:S(2)}) collective-permute-start(f32[128,256]{0,1:T(8,128)S(1)} %dynamic-slice_add_fusion), channel_id=1, source_target_pairs={{0,3},{1,2},{2,1},{3,0},{4,7},{5,6},{6,5},{7,4},{8,11},{9,10},{10,... | collective-permute-start | bytes 393224 | tf_op jit(solution)/shard_map/ppermute | solution.py:16
  187.2 5.0 %collective-permute-start.38 = (f32[128,256]{0,1:T(8,128)S(1)}, f32[128,256]{0,1:T(8,128)S(1)}, u32[]{:S(2)}, u32[]{:S(2)}) collective-permute-start(f32[128,256]{0,1:T(8,128)S(1)} %add_bitcast_fusion), channel_id=1, source_target_pairs={{0,8},{4,12},{8,0},{12,4},{16,24},{20,28},{24,16},{28,20},{1,9},{5... | collective-permute-start | bytes 393224 | tf_op jit(solution)/shard_map/ppermute | solution.py:16
  192.3 6.8 %collective-permute-start.39 = (f32[128,256]{0,1:T(8,128)S(1)}, f32[128,256]{0,1:T(8,128)S(1)}, u32[]{:S(2)}, u32[]{:S(2)}) collective-permute-start(f32[128,256]{0,1:T(8,128)S(1)} %fusion.38), channel_id=1, source_target_pairs={{0,16},{4,20},{8,24},{12,28},{16,0},{20,4},{24,8},{28,12},{1,17},{... | collective-permute-start | bytes 393224 | tf_op jit(solution)/shard_map/ppermute | solution.py:16
  199.1 1.4 collective-permute-start.40

commit v2 on v1

v2 whole, which is shorter than its diff:
```python
import functools
import jax
import jax.numpy as jnp
from jax import lax
from jax.experimental import pallas as pl
from jax.experimental.pallas import tpu as pltpu
from jax.sharding import PartitionSpec as P

BR = 12
BC = 12
GROUP = 16
SUBLANES = 8
VMEM_LIMIT = 52 * 1024 * 1024
NO_COST = pl.CostEstimate(flops=0, bytes_accessed=0, transcendentals=0)


def swap(value, axis, offset):
    size = lax.axis_size(axis)
    return lax.ppermute(value, axis, [(i, i ^ offset) for i in range(size)])


def fetch_tiles(count, tiles_ref, tile_buf, sems):
    slots = tiles_ref.shape[0]
    for slot in range(slots):
        @pl.when(slot < count)
        def _():
            pltpu.make_async_copy(tiles_ref.at[slot], tile_buf.at[slot], sems.at[slot]).start()


def wait_tile(slot, tiles_ref, tile_buf, sems):
    pltpu.make_async_copy(tiles_ref.at[slot], tile_buf.at[slot], sems.at[slot]).wait()


def transposed_kernel(count_ref, rows_ref, cols_ref, tiles_ref, *refs):
    pieces, (mine_ref, other_ref, sketch_buf, tile_buf, sems) = refs[:-5], refs[-5:]
    count = count_ref[0, 0]
    fetch_tiles(count, tiles_ref, tile_buf, sems)
    row_index, col_index = lax.axis_index("row"), lax.axis_index("col")
    tile_size = tiles_ref.shape[1]
    width = pieces[0].shape[1]
    groups = pieces[0].shape[0] // GROUP
    half = groups // 2
    core, place = row_index % 2, row_index // 2
    for offset, piece in enumerate(pieces):
        lanes = pl.ds(pl.multiple_of((col_index ^ offset) * width, 128), width)
        for group in range(groups):
            source = (core ^ (group // half)) * half + (place ^ (group % half))
            sketch_buf[pl.ds(group * GROUP, GROUP), lanes] = piece[
                pl.ds(pl.multiple_of(source * GROUP, GROUP), GROUP), :
            ]
    mine_ref[...] = jnp.zeros_like(mine_ref)
    other_ref[...] = jnp.zeros_like(other_ref)
    split = mine_ref.shape[0]

    def step(slot, carry):
        wait_tile(slot, tiles_ref, tile_buf, sems)
        block = sketch_buf[:, pl.ds(pl.multiple_of(rows_ref[0, 0, slot] * tile_size, 128), tile_size)]
        product = jnp.dot(block, tile_buf[slot], preferred_element_type=jnp.float32)
        lanes = pl.ds(pl.multiple_of(cols_ref[0, 0, slot] * tile_size, 128), tile_size)
        mine_ref[:, lanes] += product[:split]
        other_ref[:, lanes] += product[split:]
        return carry

    lax.fori_loop(0, count, step, 0)


def forward_kernel(count_ref, rows_ref, cols_ref, tiles_ref, *refs):
    outs = lax.axis_size("col")
    column_buf, total, tile_buf, sems = refs[-4:]
    pieces, out_refs = refs[: -4 - outs], refs[-4 - outs : -4]
    count = count_ref[0, 0]
    fetch_tiles(count, tiles_ref, tile_buf, sems)
    row_index, col_index = lax.axis_index("row"), lax.axis_index("col")
    tile_size = tiles_ref.shape[1]
    half = len(pieces) // 2
    core, place = row_index % 2, row_index // 2
    for offset, piece in enumerate(pieces):
        target = (core ^ (offset // half)) * half + (place ^ (offset % half))
        column_buf[pl.ds(pl.multiple_of(target * GROUP, GROUP), GROUP), :] = piece[...]
    total[...] = jnp.zeros_like(total)

    def step(slot, carry):
        wait_tile(slot, tiles_ref, tile_buf, sems)
        block = column_buf[:, pl.ds(pl.multiple_of(cols_ref[0, 0, slot] * tile_size, 128), tile_size)]
        product = lax.dot_general(
            tile_buf[slot], block, (((1,), (1,)), ((), ())), preferred_element_type=jnp.float32
        )
        total[pl.ds(pl.multiple_of(rows_ref[0, 0, slot] * tile_size, 128), tile_size), :] += product
        return carry

    lax.fori_loop(0, count, step, 0)
    for offset, out_ref in enumerate(out_refs):
        width = out_ref.shape[0]
        start = pl.multiple_of((col_index ^ offset) * width, 128)
        out_ref[...] = total[pl.ds(start, width), :].astype(out_ref.dtype)


def tile_call(kernel, out_shape, scratch, counts, rows, cols, tiles, pieces):
    slots, tile_size, _ = tiles.shape
    smem = pl.BlockSpec(memory_space=pltpu.SMEM)
    vmem = pl.BlockSpec(memory_space=pltpu.VMEM)
    return pl.pallas_call(
        kernel,
        out_shape=out_shape,
        in_specs=[smem, smem, smem, pl.BlockSpec(memory_space=pl.ANY)] + [vmem] * len(pieces),
        out_specs=jax.tree.map(lambda _: vmem, out_shape),
        scratch_shapes=scratch
        + [
            pltpu.VMEM((slots, tile_size, tile_size), jnp.bfloat16),
            pltpu.SemaphoreType.DMA((slots,)),
        ],
        compiler_params=pltpu.CompilerParams(vmem_limit_bytes=VMEM_LIMIT),
        cost_estimate=NO_COST,
    )(counts, rows, cols, tiles, *pieces)


def after(value, token):
    return value if token is None else lax.optimization_barrier((value, token))[0]


def half(value):
    return value.astype(jnp.float16)


def full(value):
    return value.astype(jnp.float32)


class Chunk:
    def __init__(self, call_transposed, call_forward, shard):
        self.call_transposed, self.call_forward = call_transposed, call_forward
        self.places = lax.axis_size("row") // 2
        self.offsets = range(1, lax.axis_size("col"))
        self.low = lambda d: d & -d
        self.pieces = [shard] + [swap(shard, "col", d) for d in self.offsets]

    def multiply_transposed(self, token=None):
        self.mine, self.other = self.call_transposed(after(self.pieces, token))

    def send_other(self, token=None):
        self.sent = after(self.other, token)
        self.arrived = swap(self.sent, "row", 1)

    def reduce_begin(self, token=None):
        arrived = after(self.arrived, token)
        rows = lambda value, d: value[d * GROUP : (d + 1) * GROUP]
        self.parts = {d: rows(self.mine, d) + rows(arrived, d) for d in range(self.places)}
        self.arriving = {d: [] for d in range(self.places)}
        for d in range(3, self.places, 2):
            self.pass_on(d)

    def pass_on(self, d, token=None):
        for value in after(self.arriving[d], token):
            self.parts[d] = self.parts[d] + full(value)
        self.sent = half(self.parts[d])
        bit = self.low(d)
        self.arriving[d ^ bit].append(swap(self.sent, "row", 2 * bit))

    def reduce_rest(self, token=None):
        for d in sorted(range(2, self.places, 2), key=lambda d: (self.low(d), d)):
            self.pass_on(d, token)
            token = None
        self.parts[1] = after(self.parts[1], self.sent)
        self.pass_on(1)

    def own(self, token=None):
        for value in after(self.arriving[0], token):
            self.parts[0] = self.parts[0] + full(value)
        self.whole = {0: self.parts[0].astype(jnp.bfloat16)}
        self.ways = sorted(range(1, self.places), key=lambda d: (bin(d).count("1"), -d))
        for d in self.ways:
            if bin(d).count("1") == 1 and d > 1:
                self.spread(d)

    def spread(self, d, token=None):
        self.whole[d] = swap(after(self.whole[d ^ self.low(d)], token), "row", 2 * self.low(d))

    def spread_rest(self, token=None):
        first = self.ways[0]
        if token is not None:
            self.whole[first] = after(self.whole[first], token)
        for d in self.ways:
            if d not in self.whole:
                self.spread(d)

    def share(self, token=None):
        near = [self.whole[d] for d in range(self.places)]
        late = [d for d in range(1, self.places) if d != self.ways[0]]
        for d, value in zip(late, after([near[d] for d in late], token)):
            near[d] = value
        self.columns = near + [swap(v, "row", 1) for v in near]

    def multiply_forward(self, token=None):
        self.forward = self.call_forward(after(self.columns, token))

    def send_rows(self, token=None):
        self.total, *self.sent = after(self.forward, token)
        self.arrived = [swap(value, "col", d) for d, value in zip(self.offsets, self.sent)]

    def finish(self, token=None, *others):
        parts = [self.total] + after(self.arrived, token)
        shape = self.total.shape
        return pl.pallas_call(
            finish_kernel,
            out_shape=(
                jax.ShapeDtypeStruct(shape, jnp.float32),
                jax.ShapeDtypeStruct((shape[1] * (len(others) + 1), shape[1]), jnp.float32),
            ),
            compiler_params=pltpu.CompilerParams(vmem_limit_bytes=VMEM_LIMIT),
            cost_estimate=NO_COST,
        )(*others, *parts)


def run_alone(chunk):
    for step in (
        chunk.multiply_transposed, chunk.send_other, chunk.reduce_begin, chunk.reduce_rest, chunk.own,
        chunk.spread_rest, chunk.share, chunk.multiply_forward, chunk.send_rows,
    ):
        step()
    return chunk.finish()


def run_pair(a, b):
    a.multiply_transposed()
    a.send_other(b.pieces[1:3])
    a.reduce_begin()
    a.reduce_rest()
    b.multiply_transposed(a.sent)
    b.send_other(a.arriving[0])
    a.own(b.sent)
    a.spread(1)
    b.reduce_begin(a.whole[0])
    a.spread_rest(b.sent)
    b.reduce_rest([a.whole[1], a.whole[2]])
    b.own()
    b.spread(1)
    a.share(b.whole[0])
    a.multiply_forward()
    a.send_rows(b.whole[1])
    b.spread_rest(a.sent)
    b.share()
    b.multiply_forward(a.sent)
    b.send_rows()


class Sum:
    def __init__(self, value):
        half = value.shape[0] // 2
        self.core = lax.axis_index("row") % 2
        mine = lax.dynamic_slice_in_dim(value, self.core * half, half, 0)
        other = lax.dynamic_slice_in_dim(value, (1 - self.core) * half, half, 0)
        self.mine = mine + swap(other, "row", 1)

    def over_row(self, token=None):
        bit = 2
        while bit < lax.axis_size("row"):
            arrived = swap(self.mine, "row", bit)
            if token is not None and bit == 2:
                arrived = after(arrived, token)
            self.mine = self.mine + arrived
            bit *= 2

    def over_col(self, token=None):
        mine = after(self.mine, token)
        arrived = [swap(mine, "col", d) for d in range(1, lax.axis_size("col"))]
        stack = jnp.stack([mine] + arrived)
        self.mine = sum(
            lax.dynamic_index_in_dim(stack, lax.axis_index("col") ^ d, 0, keepdims=False)
            for d in range(lax.axis_size("col"))
        )

    def finish(self):
        other = swap(self.mine, "row", 1)
        return jnp.where(
            self.core == 0, jnp.concatenate([self.mine, other]), jnp.concatenate([other, self.mine])
        )


def product(left, right, left_dim, right_dim):
    return lax.dot_general(
        left, right, (((left_dim,), (right_dim,)), ((), ())),
        precision=lax.Precision.HIGHEST, preferred_element_type=jnp.float32,
    )


def finish_kernel(*refs):
    parts = lax.axis_size("col")
    rows_ref, gram_ref = refs[-2:]
    others, parts = refs[: -2 - parts], refs[-2 - parts : -2]
    total = parts[0][...]
    for part in parts[1:]:
        total = total + part[...].astype(jnp.float32)
    rows_ref[...] = total
    size = total.shape[1]
    for i, other in enumerate(others):
        gram_ref[size * i : size * (i + 1), :] = product(other[...], total, 0, 0)
    gram_ref[size * len(others) :, :] = product(total, total, 0, 0)


def factor_with_inverse(matrix):
    size = matrix.shape[1]
    groups = size // SUBLANES
    shape = (SUBLANES, size)
    row = lax.broadcasted_iota(jnp.int32, shape, 0)
    col = lax.broadcasted_iota(jnp.int32, shape, 1)
    left = [matrix[SUBLANES * g : SUBLANES * (g + 1), :] for g in range(groups)]
    right = [(col == row + SUBLANES * g).astype(jnp.float32) for g in range(groups)]
    spread = lambda value, j: jnp.broadcast_to(value[j : j + 1, :], shape)
    for p in range(groups):
        columns = [
            {
                g: jnp.broadcast_to(left[g][:, SUBLANES * p + k : SUBLANES * p + k + 1], shape)
                for g in range(p, groups)
            }
            for k in range(SUBLANES)
        ]
        pivots = None
        for j in range(SUBLANES):
            pivot = spread(columns[j][p], j)
            inverse = 1.0 / pivot
            pivots = pivot if pivots is None else jnp.where(row == j, pivot, pivots)
            left_row, right_row = spread(left[p], j), spread(right[p], j)
            heads = {k: spread(columns[k][p], j) for k in range(j + 1, SUBLANES)}
            for g in range(p, groups):
                scale = columns[j][g] * inverse
                if g == p:
                    scale = jnp.where(row > j, scale, 0.0)
                left[g] = left[g] - scale * left_row
                right[g] = right[g] - scale * right_row
                for k, head in heads.items():
                    columns[k][g] = columns[k][g] - scale * head
        scale = lax.rsqrt(pivots)
        left[p] = jnp.where(col >= row + SUBLANES * p, left[p] * scale, 0.0)
        right[p] = right[p] * scale
    return jnp.concatenate(left), jnp.concatenate(right)


def first_factor_kernel(total_rows, gram_ref, rows_ref, upper_ref, inverse_ref, basis_ref):
    upper, inverse = factor_with_inverse(gram_ref[...] / total_rows)
    upper_ref[...] = upper
    inverse_ref[...] = inverse
    basis_ref[...] = product(rows_ref[...], inverse, 1, 1)


def second_factor_kernel(
    total_rows, gram_ref, upper_ref, inverse_ref, first_ref, rows_ref, basis_ref, factor_ref
):
    split = upper_ref.shape[0]
    mixed, last = gram_ref[:split] / total_rows, gram_ref[split:] / total_rows
    corner = product(inverse_ref[...], mixed, 1, 0)
    upper, inverse = factor_with_inverse(last - product(corner, corner, 0, 0))
    factor_ref[:split, :split] = upper_ref[...]
    factor_ref[:split, split:] = corner
    factor_ref[split:, :split] = jnp.zeros_like(upper)
    factor_ref[split:, split:] = upper
    first = first_ref[...]
    basis_ref[:, :split] = first
    basis_ref[:, split:] = product(rows_ref[...], inverse, 1, 1) - product(
        first, product(corner, inverse, 1, 1), 1, 0
    )


def body(tiles, tile_rows, tile_cols, tile_counts, sketch):
    tiles = tiles[0, 0]
    slots, tile_size, _ = tiles.shape
    width, sketch_width = sketch.shape
    chunk = min(sketch_width, GROUP * lax.axis_size("row"))
    group_rows, group_cols = BR * tile_size, BC * tile_size
    shard = sketch.T
    partial = jax.ShapeDtypeStruct((chunk // 2, group_cols), jnp.float32)
    call_transposed = lambda pieces: tile_call(
        transposed_kernel,
        (partial, partial),
        [pltpu.VMEM((chunk, group_rows), jnp.bfloat16)],
        tile_counts, tile_rows, tile_cols, tiles, pieces,
    )
    call_forward = lambda pieces: tile_call(
        forward_kernel,
        tuple(
            jax.ShapeDtypeStruct((width, chunk), jnp.bfloat16 if offset else jnp.float32)
            for offset in range(lax.axis_size("col"))
        ),
        [pltpu.VMEM((chunk, group_cols), jnp.bfloat16), pltpu.VMEM((group_rows, chunk), jnp.float32)],
        tile_counts, tile_rows, tile_cols, tiles, pieces,
    )
    chunks = [
        Chunk(call_transposed, call_forward, shard[start : start + chunk])
        for start in range(0, sketch_width, chunk)
    ]
    split = sketch_width // 2
    if len(chunks) == 2:
        run_pair(*chunks)
        first, first_gram = chunks[0].finish(chunks[1].sent)
        first_gram = after(first_gram, chunks[1].arrived[:1])
    else:
        whole, gram = run_alone(chunks[0])
        first, second = whole[:, :split], whole[:, split:]
        first_gram, mixed_gram = gram[:split, :split], gram[:, split:]
    total_rows = group_rows * lax.axis_size("row")
    params = pltpu.CompilerParams(vmem_limit_bytes=VMEM_LIMIT)
    square = jax.ShapeDtypeStruct((split, split), jnp.float32)
    first_gram = Sum(first_gram)
    first_gram.over_row()
    if len(chunks) == 2:
        second, mixed_gram = chunks[1].finish(first_gram.mine, first)
    first_gram.over_col()
    mixed_gram = Sum(mixed_gram)
    upper, inverse, first_basis = pl.pallas_call(
        functools.partial(first_factor_kernel, total_rows),
        out_shape=(square, square, jax.ShapeDtypeStruct(first.shape, jnp.float32)),
        compiler_params=params,
    )(first_gram.finish(), first)
    mixed_gram.over_row(upper)
    mixed_gram.over_col()
    return pl.pallas_call(
        functools.partial(second_factor_kernel, total_rows),
        out_shape=(
            jax.ShapeDtypeStruct((width, sketch_width), jnp.float32),
            jax.ShapeDtypeStruct((sketch_width, sketch_width), jnp.float32),
        ),
        compiler_params=params,
    )(mixed_gram.finish(), upper, inverse, first_basis, second)


def solution(mesh):
    return jax.shard_map(
        body,
        mesh=mesh,
        in_specs=(
            P("row", "col", None, None, None),
            P("row", "col", None),
            P("row", "col", None),
            P("row", "col"),
            P(("row", "col"), None),
        ),
        out_specs=(P(("row", "col"), None), P()),
        check_vma=False,
    )
```

time: 266 us -> 182 us (0.68)
  other arithmetic: 64.8 us -> 2.8 us
  waiting for transfers between devices: 120 us -> 89.8 us
  Pallas kernels: 18.4 us -> 35.7 us
  local copies, waits for them, and re-layouts: 8.72 us -> 2.38 us
  matrix products: 6.21 us -> 0 us
  starting transfers between devices: 45.1 us -> 49.3 us
    another operation x14 -> x2, other arithmetic: 58.7 us -> 0.03 us  [over_col(): stack = jnp.stack([mine] + arrived)]
    ppermute x41 -> x48, waiting for transfers between devices: 120 us -> 89.8 us  [swap(): return lax.ppermute(value, axis, [(i, i ^ offset) for i in range(size)])]
    pallas_call x0 -> x4, Pallas kernels: none -> 17.3 us  [the longest x1 7.39 us: body(): pl.pallas_call(functools.partial(second_factor_kernel, total_rows), out_s...]
    ppermute x41 -> x48, starting transfers between devices: 45.1 us -> 49.3 us  [swap(): return lax.ppermute(value, axis, [(i, i ^ offset) for i in range(size)])]
    another operation x9 -> x0, local copies, waits for them, and re-layouts: 4.03 us -> none
    another operation x5 -> x0, matrix products: 3.58 us -> none  [the longest x3 3.11 us: body(): lax.linalg.triangular_solve(cholesky_lower, owned_rows, left_side=False,...]
  transfers between devices with their start and end apart: 41 -> 48, of which waited for: 21 -> 27; matrix products, arithmetic and copies ran while one was open for 3% -> 1% of each run, Pallas kernels for 5% -> 16%
where the time goes in v2:
time: 182 us
  waiting for transfers between devices  89.8 us (49%)
  starting transfers between devices  49.3 us (27%)
  Pallas kernels  35.7 us (20%)
  other arithmetic  2.8 us (2%)
  local copies, waits for them, and re-layouts  2.38 us (1%)
    ppermute x48, waiting for transfers between devices, swap(): return lax.ppermute(value, axis, [(i, i ^ offset) for i in range(size)])  89.8 us
    ppermute x48, starting transfers between devices, swap(): return lax.ppermute(value, axis, [(i, i ^ offset) for i in range(size)])  49.3 us
    pallas_call x4, Pallas kernels, tile_call(): pl.pallas_call(kernel, out_shape=out_shape, in_specs=[smem, smem, smem, p...  18.4 us
    pallas_call x1, Pallas kernels, body(): pl.pallas_call(functools.partial(second_factor_kernel, total_rows), out_s...  7.39 us
    pallas_call x2, Pallas kernels, finish(): pl.pallas_call(finish_kernel, out_shape=(jax.ShapeDtypeStruct(shape, jnp....  5.03 us
    pallas_call x1, Pallas kernels, body(): pl.pallas_call(functools.partial(first_factor_kernel, total_rows), out_sh...  4.88 us
  transfers between devices with their start and end apart: 48, of which 27 were waited for; matrix products, arithmetic and copies ran while one was open for 1% of the time, Pallas kernels for 16%

profile of v2, /device:TPU:0, one launch (start us, length us, event | category | flops | bytes accessed | tf_op | source)
XLA Modules:
  0.0 181.6 jit_solution(4964183414233089158)
XLA Ops:
  0.7 1.4 copy.7
  2.1 3.0 %collective-permute-start = (bf16[128,1536]{1,0:T(8,128)(2,1)S(1)}, bf16[128,1536]{1,0:T(8,128)(2,1)S(1)}, u32[]{:S(2)}, u32[]{:S(2)}) collective-permute-start(bf16[128,1536]{1,0:T(8,128)(2,1)S(1)} %get-tuple-element.117.refs_0_), channel_id=1, source_target_pairs={{0,1},{1,0},{2,3},{3,2},{4,5},{5,4},{6,7},{7,6},{8,9},{9,8},{10,11... | collective-permute-start | bytes 1179656 | tf_op jit(solution)/shard_map/ppermute | solution.py:19
  5.1 1.5 collective-permute-start.1
  6.7 1.9 %collective-permute-start.3 = (bf16[128,1536]{1,0:T(8,128)(2,1)S(1)}, bf16[128,1536]{1,0:T(8,128)(2,1)S(1)}, u32[]{:S(2)}, u32[]{:S(2)}) collective-permute-start(bf16[128,1536]{1,0:T(8,128)(2,1)S(1)} %get-tuple-element.61.refs_0_), channel_id=1, source_target_pairs={{0,1},{1,0},{2,3},{3,2},{4,5},{5,4},{6,7},{7,6},{8,9},{9,8},{10,11... | collective-permute-start | bytes 1179656 | tf_op jit(solution)/shard_map/ppermute | solution.py:19
  8.6 1.5 collective-permute-start.4
  10.8 4.3 %collective-permute-done.refs_1_ = bf16[128,1536]{1,0:T(8,128)(2,1)S(1)} collective-permute-done((bf16[128,1536]{1,0:T(8,128)(2,1)S(1)}, bf16[128,1536]{1,0:T(8,128)(2,1)S(1)}, u32[]{:S(2)}, u32[]{:S(2)}) %collective-permute-start) | collective-permute-done | bytes 393248 | tf_op jit(solution)/shard_map/ppermute | solution.py:19
  15.1 10.5 %collective-permute-done.1.refs_2_ = bf16[128,1536]{1,0:T(8,128)(2,1)S(1)} collective-permute-done((bf16[128,1536]{1,0:T(8,128)(2,1)S(1)}, bf16[128,1536]{1,0:T(8,128)(2,1)S(1)}, u32[]{:S(2)}, u32[]{:S(2)}) %collective-permute-start.1) | collective-permute-done | bytes 393248 | tf_op jit(solution)/shard_map/ppermute | solution.py:19
  25.6 4.6 %shard_map.68 = (f32[64,6144]{1,0:T(8,128)}, f32[64,6144]{1,0:T(8,128)}) custom-call(s32[1,1]{1,0:T(1,128)S(6)} %copy.8.count_ref, s32[1,1,16]{2,1,0:T(1,128)S(1)} %copy-done.3, s32[1,1,16]{2,1,0:T(1,128)S(1)} %copy-done.4, bf16[16,512,512]{2,1,0:T(8,128)(2,1)} %bitcast.14, bf16[128,1536]{1,0:T(8,128)(2,1)S(1)} %get-tuple-element.117.refs_0_, ...), custom_call_target="tpu_custom_call" | custom-call | tf_op jit(solution)/shard_map/pallas_call | solution.py:102
  31.2 1.4 collective-permute-done.4.refs_2_
  32.6 3.6 %collective-permute-done.5 = f32[64,6144]{1,0:T(8,128)S(1)} collective-permute-done((f32[64,6144]{1,0:T(8,128)}, f32[64,6144]{1,0:T(8,128)S(1)}, u32[]{:S(2)}, u32[]{:S(2)}) %collective-permute-start.5) | collective-permute-done | bytes 1572896 | tf_op jit(solution)/shard_map/ppermute | solution.py:19
  37.4 2.0 %collective-permute-start.6 = (f16[16,6144]{1,0:T(8,128)(2,1)S(1)}, f16[16,6144]{1,0:T(8,128)(2,1)S(1)}, u32[]{:S(2)}, u32[]{:S(2)}) collective-permute-start(f16[16,6144]{1,0:T(8,128)(2,1)S(1)} %get-tuple-element.115), channel_id=1, source_target_pairs={{0,8},{4,12},{8,0},{12,4},{16,24},{20,28},{24,16},{28,20},{1,9},{5... | collective-permute-start | bytes 589832 | tf_op jit(solution)/shard_map/ppermute | solution.py:19
  40.5 4.1 %collective-permute-done.6 = f16[16,6144]{1,0:T(8,128)(2,1)S(1)} collective-permute-done((f16[16,6144]{1,0:T(8,128)(2,1)S(1)}, f16[16,6144]{1,0:T(8,128)(2,1)S(1)}, u32[]{:S(2)}, u32[]{:S(2)}) %collective-permute-start.6) | collective-permute-done | bytes 196640 | tf_op jit(solution)/shard_map/ppermute | solution.py:19
  44.7 2.4 %collective-permute-start.7 = (f16[16,6144]{1,0:T(8,128)(2,1)S(1)}, f16[16,6144]{1,0:T(8,128)(2,1)S(1)}, u32[]{:S(2)}, u32[]{:S(2)}) collective-permute-start(f16[16,6144]{1,0:T(8,128)(2,1)S(1)} %fusion.2), channel_id=1, source_target_pairs={{0,16},{4,20},{8,24},{12,28},{16,0},{20,4},{24,8},{28,12},{1,17},{... | collective-permute-start | bytes 589832 | tf_op jit(solution)/shard_map/ppermute | solution.py:19
  47.2 1.6 collective-permute-start.8
  48.8 2.4 %collective-permute-done.9.refs_3_ = bf16[128,1536]{1,0:T(8,128)(2,1)S(1)} collective-permute-done((bf16[128,1536]{1,0:T(8,128)(2,1)S(1)}, bf16[128,1536]{1,0:T(8,128)(2,1)S(1)}, u32[]{:S(2)}, u32[]{:S(2)}) %collective-permute-start.9) | collective-permute-done | bytes 393248 | tf_op jit(solution)/shard_map/ppermute | solution.py:19
  51.2 4.6 %shard_map.69 = (f32[64,6144]{1,0:T(8,128)}, f32[64,6144]{1,0:T(8,128)}) custom-call(s32[1,1]{1,0:T(1,128)S(6)} %copy.8.count_ref, s32[1,1,16]{2,1,0:T(1,128)S(1)} %copy-done.3, s32[1,1,16]{2,1,0:T(1,128)S(1)} %copy-done.4, bf16[16,512,512]{2,1,0:T(8,128)(2,1)} %bitcast.15, bf16[128,1536]{1,0:T(8,128)(2,1)S(1)} %get-tuple-element.61.refs_0_, ...), custom_call_target="tpu_custom_call" | custom-call | tf_op jit(solution)/shard_map/pallas_call | solution.py:102
  56.9 2.2 %collective-permute-start.10 = (bf16[16,6144]{1,0:T(8,128)(2,1)S(1)}, bf16[16,6144]{1,0:T(8,128)(2,1)S(1)}, u32[]{:S(2)}, u32[]{:S(2)}) collective-permute-start(bf16[16,6144]{1,0:T(8,128)(2,1)S(1)} %fusion.5.refs_0_), channel_id=1, source_target_pairs={{0,8},{4,12},{8,0},{12,4},{16,24},{20,28},{24,16},{28,20},{1,9},{5... | collective-permute-start | bytes 589832 | tf_op jit(solution)/shard_map/ppermute | solution.py:19
  59.0 1.4 collective-permute-start.11
  61.4 2.2 %collective-permute-start.14 = (f16[16,6144]{1,0:T(8,128)(2,1)S(1)}, f16[16,6144]{1,0:T(8,128)(2,1)S(1)}, u32[]{:S(2)}, u32[]{:S(2)}) collective-permute-start(f16[16,6144]{1,0:T(8,128)(2,1)S(1)} %add_convert_fusion.2), channel_id=1, source_target_pairs={{0,8},{4,12},{8,0},{12,4},{16,24},{20,28},{24,16},{28,20},{1,9},{5... | collective-permute-start | bytes 589832 | tf_op jit(solution)/shard_map/ppermute | solution.py:19
  63.6 7.5 %collective-permute-done.11.refs_2_ = bf16[16,6144]{1,0:T(8,128)(2,1)S(1)} collective-permute-done((bf16[16,6144]{1,0:T(8,128)(2,1)S(1)}, bf16[16,6144]{1,0:T(8,128)(2,1)S(1)}, u32[]{:S(2)}, u32[]{:S(2)}) %collective-permute-start.11) | collective-permute-done | bytes 196640 | tf_op jit(solution)/shard_map/ppermute | solution.py:19
  71.1 1.9 %collective-permute-done.14 = f16[16,6144]{1,0:T(8,128)(2,1)S(1)} collective-permute-done((f16[16,6144]{1,0:T(8,128)(2,1)S(1)}, f16[16,6144]{1,0:T(8,128)(2,1)S(1)}, u32[]{:S(2)}, u32[]{:S(2)}) %collective-permute-start.14) | collective-permute-done | bytes 196640 | tf_op jit(solution)/shard_map/ppermute | solution.py:19
  73.2 1.9 %collective-permute-start.16 = (f16[16,6144]{1,0:T(8,128)(2,1)S(1)}, f16[16,6144]{1,0:T(8,128)(2,1)S(1)}, u32[]{:S(2)}, u32[]{:S(2)}) collective-permute-start(f16[16,6144]{1,0:T(8,128)(2,1)S(1)} %convert_element_type.53), channel_id=1, source_target_pairs={{0,8},{4,12},{8,0},{12,4},{16,24},{20,28},{24,16},{28,20},{1,9},{5... | collective-permute-start | bytes 589832 | tf_op jit(solution)/shard_map/ppermute | solution.py:19
  75.1 1.3 collective-permute-start.15
  77.7 6.9 %collective-permute-done.16 = f16[16,6144]{1,0:T(8,128)(2,1)S(1)} collective-permute-done((f16[16,6144]{1,0:T(8,128)(2,1)S(1)}, f16[16,6144]{1,0:T(8,128)(2,1)S(1)}, u32[]{:S(2)}, u32[]{:S(2)}) %collective-permute-start.16) | collective-permute-done | bytes 196640 | tf_op jit(solution)/shard_map/ppermute | solution.py:19
  84.5 1.4 collective-permute-done.15
  86.1 2.3 %collective-permute-done.13.refs_3_ = bf16[16,6144]{1,0:T(8,128)(2,1)S(1)} collective-permute-done((bf16[16,6144]{1,0:T(8,128)(2,1)S(1)}, bf16[16,6144]{1,0:T(8,128)(2,1)S(1)}, u32[]{:S(2)}, u32[]{:S(2)}) %collective-permute-start.13) | collective-permute-done | bytes 196640 | tf_op jit(solution)/shard_map/ppermute | solution.py:19
  88.9 1.6 collective-permute-start.21
  91.8 4.5 %shard_map.70 = (f32[1536,128]{1,0:T(8,128)}, bf16[1536,128]{1,0:T(8,128)(2,1)S(1)}, bf16[1536,128]{1,0:T(8,128)(2,1)}, bf16[1536,128]{1,0:T(8,128)(2,1)}) custom-call(s32[1,1]{1,0:T(1,128)S(6)} %copy.8.count_ref, s32[1,1,16]{2,1,0:T(1,128)S(1)} %copy-done.3, s32[1,1,16]{2,1,0:T(1,128)S(1)} %copy-done.4, bf16[16,512,512]{2,1,0:T(8,128)(2,1)} %bitcast.16, ...), custom_call_target="tpu_custom_call" | custom-call | tf_op jit(solution)/shard_map/pallas_call | solution.py:102
  96.3 2.2 %collective-permute-done.21.refs_1_ = bf16[16,6144]{1,0:T(8,128)(2,1)S(1)} collective-permute-done((bf16[16,6144]{1,0:T(8,128)(2,1)S(1)}, bf16[16,6144]{1,0:T(8,128)(2,1)S(1)}, u32[]{:S(2)}, u32[]{:S(2)}) %collective-permute-start.21) | collective-permute-done | bytes 196640 | tf_op jit(solution)/shard_map/ppermute | solution.py:19
  98.6 3.7 %collective-permute-done.25.refs_2_ = bf16[16,6144]{1,0:T(8,128)(2,1)S(1)} collective-permute-done((bf16[16,6144]{1,0:T(8,128)(2,1)S(1)}, bf16[16,6144]{1,0:T(8,128)(2,1)S(1)}, u32[]{:S(2)}, u32[]{:S(2)}) %collective-permute-start.25) | collective-permute-done | bytes 196640 | tf_op jit(solution)/shard_map/ppermute | solution.py:19
  102.8 5.2 %collective-permute-done.26.refs_3_ = bf16[16,6144]{1,0:T(8,128)(2,1)S(1)} collective-permute-done((bf16[16,6144]{1,0:T(8,128)(2,1)S(1)}, bf16[16,6144]{1,0:T(8,128)(2,1)S(1)}, u32[]{:S(2)}, u32[]{:S(2)}) %collective-permute-start.26) | collective-permute-done | bytes 196640 | tf_op jit(solution)/shard_map/ppermute | solution.py:19
  107.9 1.3 collective-permute-start.23
  109.3 2.2 %collective-permute-start.24 = (bf16[1536,128]{1,0:T(8,128)(2,1)}, bf16[1536,128]{1,0:T(8,128)(2,1)S(1)}, u32[]{:S(2)}, u32[]{:S(2)}) collective-permute-start(bf16[1536,128]{1,0:T(8,128)(2,1)} %get-tuple-element.83), channel_id=1, source_target_pairs={{0,3},{1,2},{2,1},{3,0},{4,7},{5,6},{6,5},{7,4},{8,11},{9,10},{10,... | collective-permute-start | bytes 1179656 | tf_op jit(solution)/shard_map/ppermute | solution.py:19
  111.4 4.7 %shard_map.71 = (f32[1536,128]{1,0:T(8,128)}, bf16[1536,128]{1,0:T(8,128)(2,1)S(1)}, bf16[1536,128]{1,0:T(8,128)(2,1)}, bf16[1536,128]{1,0:T(8,128)(2,1)}) custom-call(s32[1,1]{1,0:T(1,128)S(6)} %copy.8.count_ref, s32[1,1,16]{2,1,0:T(1,128)S(1)} %copy-done.3, s32[1,1,16]{2,1,0:T(1,128)S(1)} %copy-done.4, bf16[16,512,512]{2,1,0:T(8,128)(2,1)} %bitcast.17, ...), custom_call_target="tpu_custom_call" | custom-call | tf_op jit(solution)/shard_map/pallas_call | solution.py:102
  116.1 3.1 %collective-permute-start.31 = (bf16[1536,128]{1,0:T(8,128)(2,1)S(1)}, bf16[1536,128]{1,0:T(8,128)(2,1)S(1)}, u32[]{:S(2)}, u32[]{:S(2)}) collective-permute-start(bf16[1536,128]{1,0:T(8,128)(2,1)S(1)} %get-tuple-element.93), channel_id=1, source_target_pairs={{0,1},{1,0},{2,3},{3,2},{4,5},{5,4},{6,7},{7,6},{8,9},{9,8},{10,11... | collective-permute-start | bytes 1179656 | tf_op jit(solution)/shard_map/ppermute | solution.py:19
  120.8 7.5 %collective-permute-done.23.refs_2_ = bf16[1536,128]{1,0:T(8,128)(2,1)S(1)} collective-permute-done((bf16[1536,128]{1,0:T(8,128)(2,1)}, bf16[1536,128]{1,0:T(8,128)(2,1)S(1)}, u32[]{:S(2)}, u32[]{:S(2)}) %collective-permute-start.23) | collective-permute-done | bytes 393248 | tf_op jit(solution)/shard_map/ppermute | solution.py:19
  128.3 2.0 %shard_map.72 = (f32[1536,128]{1,0:T(8,128)S(1)}, f32[128,128]{1,0:T(8,128)S(1)}) custom-call(f32[1536,128]{1,0:T(8,128)} %get-tuple-element.80.refs_0_, bf16[1536,128]{1,0:T(8,128)(2,1)S(1)} %collective-permute-done.22.refs_1_, bf16[1536,128]{1,0:T(8,128)(2,1)S(1)} %collective-permute-done.23.refs_2_, bf16[1536,128]{1,0:T(8,128)(2,1)S(1)} %collective-permute-done.24.refs_3_), custom_call_target="tpu_custom_call" | custom-call | tf_op jit(solution)/shard_map/pallas_call | solution.py:203
  131.2 5.5 %collective-permute-done.31.refs_2_ = bf16[1536,128]{1,0:T(8,128)(2,1)S(1)} collective-permute-done((bf16[1536,128]{1,0:T(8,128)(2,1)S(1)}, bf16[1536,128]{1,0:T(8,128)(2,1)S(1)}, u32[]{:S(2)}, u32[]{:S(2)}) %collective-permute-start.31) | collective-permute-done | bytes 393248 | tf_op jit(solution)/shard_map/ppermute | solution.py:19
  138.2 3.6 %collective-permute-done.35 = f32[64,128]{1,0:T(8,128)S(1)} collective-permute-done((f32[64,128]{1,0:T(8,128)S(1)}, f32[64,128]{1,0:T(8,128)S(1)}, u32[]{:S(2)}, u32[]{:S(2)}) %collective-permute-start.35) | collective-permute-done | bytes 32800 | tf_op jit(solution)/shard_map/ppermute | solution.py:19
  142.4 4.3 %collective-permute-done.36 = f32[64,128]{1,0:T(8,128)S(1)} collective-permute-done((f32[64,128]{1,0:T(8,128)S(1)}, f32[64,128]{1,0:T(8,128)S(1)}, u32[]{:S(2)}, u32[]{:S(2)}) %collective-permute-start.36) | collective-permute-done | bytes 32800 | tf_op jit(solution)/shard_map/ppermute | solution.py:19
  148.3 1.9 %collective-permute-start.39 = (f32[64,128]{1,0:T(8,128)S(1)}, f32[64,128]{1,0:T(8,128)S(1)}, u32[]{:S(2)}, u32[]{:S(2)}) collective-permute-start(f32[64,128]{1,0:T(8,128)S(1)} %add.142), channel_id=1, source_target_pairs={{0,1},{1,0},{2,3},{3,2},{4,5},{5,4},{6,7},{7,6},{8,9},{9,8},{10,11... | collective-permute-start | bytes 98312 | tf_op jit(solution)/shard_map/ppermute | solution.py:19
  150.3 3.0 %shard_map.73 = (f32[1536,128]{1,0:T(8,128)}, f32[256,128]{1,0:T(8,128)S(1)}) custom-call(f32[1536,128]{1,0:T(8,128)} %copy-done, f32[1536,128]{1,0:T(8,128)} %get-tuple-element.100.refs_1_, bf16[1536,128]{1,0:T(8,128)(2,1)S(1)} %collective-permute-done.31.refs_2_, bf16[1536,128]{1,0:T(8,128)(2,1)S(1)} %collective-permute-done.32.refs_3_, ...), custom_call_target="tpu_custom_call" | custom-call | tf_op jit(solution)/shard_map/pallas_call | solution.py:203
  154.9 4.9 %shard_map.74 = (f32[128,128]{1,0:T(8,128)S(1)}, f32[128,128]{1,0:T(8,128)S(1)}, f32[1536,128]{1,0:T(8,128)S(1)}) custom-call(f32[128,128]{1,0:T(8,128)S(1)} %maximum_select_fusion.1.gram_ref, f32[1536,128]{1,0:T(8,128)S(1)} %copy-done.1), custom_call_target="tpu_custom_call" | custom-call | tf_op jit(solution)/shard_map/pallas_call | solution.py:408
  159.8 2.5 %collective-permute-start.43 = (f32[128,128]{1,0:T(8,128)S(1)}, f32[128,128]{1,0:T(8,128)S(1)}, u32[]{:S(2)}, u32[]{:S(2)}) collective-permute-start(f32[128,128]{1,0:T(8,128)S(1)} %add.154), channel_id=1, source_target_pairs={{0,16},{4,20},{8,24},{12,28},{16,0},{20,4},{24,8},{28,12},{1,17},{... | collective-permute-start | bytes 196616 | tf_op jit(solution)/shard_map/ppermute | solution.py:19
  162.3 4.2 %collective-permute-done.43 = f32[128,128]{1,0:T(8,128)S(1)} collective-permute-done((f32[128,128]{1,0:T(8,128)S(1)}, f32[128,128]{1,0:T(8,128)S(1)}, u32[]{:S(2)}, u32[]{:S(2)}) %collective-permute-start.43) | collective-permute-done | bytes 65568 | tf_op jit(solution)/shard_map/ppermute | solution.py:19
  168.5 1.6 collective-permute-start.44
  170.1 2.2 %collective-permute-done.46 = f32[128,128]{1,0:T(8,128)S(1)} collective-permute-done((f32[128,128]{1,0:T(8,128)S(1)}, f32[128,128]{1,0:T(8,128)S(1)}, u32[]{:S(2)}, u32[]{:S(2)}) %collective-permute-start.46) | collective-permute-done | bytes 65568 | tf_op jit(solution)/shard_map/ppermute | solution.py:19
  174.2 7.4 %shard_map.75 = (f32[1536,256]{1,0:T(8,128)}, f32[256,256]{1,0:T(8,128)}) custom-call(f32[256,128]{1,0:T(8,128)S(1)} %maximum_select_fusion.gram_ref, f32[128,128]{1,0:T(8,128)S(1)} %get-tuple-element.107.upper_ref, f32[128,128]{1,0:T(8,128)S(1)} %get-tuple-element.109.inverse_ref, f32[1536,128]{1,0:T(8,128)S(1)} %get-tuple-element.110.first_ref, ...), custom_call_target="tpu_custom_call" | custom-call | tf_op jit(solution)/shard_map/pallas_call | solution.py:415
  (94 shorter events, 20.9 us)
Async XLA Ops:
  2.1 12.9 %collective-permute-start = (bf16[128,1536]{1,0:T(8,128)(2,1)S(1)}, bf16[128,1536]{1,0:T(8,128)(2,1)S(1)}, u32[]{:S(2)}, u32[]{:S(2)}) collective-permute-start(bf16[128,1536]{1,0:T(8,128)(2,1)S(1)} %get-tuple-element.117.refs_0_), channel_id=1, source_target_pairs={{0,1},{1,0},{2,3},{3,2},{4,5},{5,4},{6,7},{7,6},{8,9},{9,8},{10,11... | collective-permute-start | bytes 1179656 | tf_op jit(solution)/shard_map/ppermute | solution.py:19
  5.1 20.5 %collective-permute-start.1 = (bf16[128,1536]{1,0:T(8,128)(2,1)S(1)}, bf16[128,1536]{1,0:T(8,128)(2,1)S(1)}, u32[]{:S(2)}, u32[]{:S(2)}) collective-permute-start(bf16[128,1536]{1,0:T(8,128)(2,1)S(1)} %get-tuple-element.117.refs_0_), channel_id=1, source_target_pairs={{0,2},{1,3},{2,0},{3,1},{4,6},{5,7},{6,4},{7,5},{8,10},{9,11},{10,... | collective-permute-start | bytes 1179656 | tf_op jit(solution)/shard_map/ppermute | solution.py:19
  6.7 18.9 %collective-permute-start.2 = (bf16[128,1536]{1,0:T(8,128)(2,1)S(1)}, bf16[128,1536]{1,0:T(8,128)(2,1)S(1)}, u32[]{:S(2)}, u32[]{:S(2)}) collective-permute-start(bf16[128,1536]{1,0:T(8,128)(2,1)S(1)} %get-tuple-element.117.refs_0_), channel_id=1, source_target_pairs={{0,3},{1,2},{2,1},{3,0},{4,7},{5,6},{6,5},{7,4},{8,11},{9,10},{10,... | collective-permute-start | bytes 1179656 | tf_op jit(solution)/shard_map/ppermute | solution.py:19
  6.7 24.5 %collective-permute-start.3 = (bf16[128,1536]{1,0:T(8,128)(2,1)S(1)}, bf16[128,1536]{1,0:T(8,128)(2,1)S(1)}, u32[]{:S(2)}, u32[]{:S(2)}) collective-permute-start(bf16[128,1536]{1,0:T(8,128)(2,1)S(1)} %get-tuple-element.61.refs_0_), channel_id=1, source_target_pairs={{0,1},{1,0},{2,3},{3,2},{4,5},{5,4},{6,7},{7,6},{8,9},{9,8},{10,11... | collective-permute-start | bytes 1179656 | tf_op jit(solution)/shard_map/ppermute | solution.py:19
  8.6 23.9 %collective-permute-start.4 = (bf16[128,1536]{1,0:T(8,128)(2,1)S(1)}, bf16[128,1536]{1,0:T(8,128)(2,1)S(1)}, u32[]{:S(2)}, u32[]{:S(2)}) collective-permute-start(bf16[128,1536]{1,0:T(8,128)(2,1)S(1)} %get-tuple-element.61.refs_0_), channel_id=1, source_target_pairs={{0,2},{1,3},{2,0},{3,1},{4,6},{5,7},{6,4},{7,5},{8,10},{9,11},{10,... | collective-permute-start | bytes 1179656 | tf_op jit(solution)/shard_map/ppermute | solution.py:19
  32.6 3.6 %collective-permute-start.5 = (f32[64,6144]{1,0:T(8,128)}, f32[64,6144]{1,0:T(8,128)S(1)}, u32[]{:S(2)}, u32[]{:S(2)}) collective-permute-start(f32[64,6144]{1,0:T(8,128)} %get-tuple-element.59), channel_id=1, source_target_pairs={{0,4},{4,0},{8,12},{12,8},{16,20},{20,16},{24,28},{28,24},{1,5},{5... | collective-permute-start | bytes 4718600 | tf_op jit(solution)/shard_map/ppermute | solution.py:19
  37.4 7.2 %collective-permute-start.6 = (f16[16,6144]{1,0:T(8,128)(2,1)S(1)}, f16[16,6144]{1,0:T(8,128)(2,1)S(1)}, u32[]{:S(2)}, u32[]{:S(2)}) collective-permute-start(f16[16,6144]{1,0:T(8,128)(2,1)S(1)} %get-tuple-element.115), channel_id=1, source_target_pairs={{0,8},{4,12},{8,0},{12,4},{16,24},{20,28},{24,16},{28,20},{1,9},{5... | collective-permute-start | bytes 589832 | tf_op jit(solution)/shard_map/ppermute | solution.py:19
  39.4 11.8 %collective-permute-start.9 = (bf16[128,1536]{1,0:T(8,128)(2,1)S(1)}, bf16[128,1536]{1,0:T(8,128)(2,1)S(1)}, u32[]{:S(2)}, u32[]{:S(2)}) collective-permute-start(bf16[128,1536]{1,0:T(8,128)(2,1)S(1)} %get-tuple-element.61.refs_0_), channel_id=1, source_target_pairs={{0,3},{1,2},{2,1},{3,0},{4,7},{5,6},{6,5},{7,4},{8,11},{9,10},{10,... | collective-permute-start | bytes 1179656 | tf_op jit(solution)/shard_map/ppermute | solution.py:19
  44.7 11.5 %collective-permute-start.7 = (f16[16,6144]{1,0:T(8,128)(2,1)S(1)}, f16[16,6144]{1,0:T(8,128)(2,1)S(1)}, u32[]{:S(2)}, u32[]{:S(2)}) collective-permute-start(f16[16,6144]{1,0:T(8,128)(2,1)S(1)} %fusion.2), channel_id=1, source_target_pairs={{0,16},{4,20},{8,24},{12,28},{16,0},{20,4},{24,8},{28,12},{1,17},{... | collective-permute-start | bytes 589832 | tf_op jit(solution)/shard_map/ppermute | solution.py:19
  47.2 9.1 %collective-permute-start.8 = (f16[16,6144]{1,0:T(8,128)(2,1)S(1)}, f16[16,6144]{1,0:T(8,128)(2,1)S(1)}, u32[]{:S(2)}, u32[]{:S(2)}) collective-permute-start(f16[16,6144]{1,0:T(8,128)(2,1)S(1)} %convert_element_type.45), channel_id=1, source_target_pairs={{0,8},{4,12},{8,0},{12,4},{16,24},{20,28},{24,16},{28,20},{1,9},{5... | collective-permute-start | bytes 589832 | tf_op jit(solution)/shard_map/ppermute | solution.py:19
  56.3 4.2 %collective-permute-start.12 = (f32[64,6144]{1,0:T(8,128)}, f32[64,6144]{1,0:T(8,128)S(1)}, u32[]{:S(2)}, u32[]{:S(2)}) collective-permute-start(f32[64,6144]{1,0:T(8,128)} %get-tuple-element.66), channel_id=1, source_target_pairs={{0,4},{4,0},{8,12},{12,8},{16,20},{20,16},{24,28},{28,24},{1,5},{5... | collective-permute-start | bytes 4718600 | tf_op jit(solution)/shard_map/ppermute | solution.py:19
  56.9 14.2 %collective-permute-start.10 = (bf16[16,6144]{1,0:T(8,128)(2,1)S(1)}, bf16[16,6144]{1,0:T(8,128)(2,1)S(1)}, u32[]{:S(2)}, u32[]{:S(2)}) collective-permute-start(bf16[16,6144]{1,0:T(8,128)(2,1)S(1)} %fusion.5.refs_0_), channel_id=1, source_target_pairs={{0,8},{4,12},{8,0},{12,4},{16,24},{20,28},{24,16},{28,20},{1,9},{5... | collective-permute-start | bytes 589832 | tf_op jit(solution)/shard_map/ppermute | solution.py:19
  59.0 12.1 %collective-permute-start.11 = (bf16[16,6144]{1,0:T(8,128)(2,1)S(1)}, bf16[16,6144]{1,0:T(8,128)(2,1)S(1)}, u32[]{:S(2)}, u32[]{:S(2)}) collective-permute-start(bf16[16,6144]{1,0:T(8,128)(2,1)S(1)} %fusion.5.refs_0_), channel_id=1, source_target_pairs={{0,16},{4,20},{8,24},{12,28},{16,0},{20,4},{24,8},{28,12},{1,17},{... | collective-permute-start | bytes 589832 | tf_op jit(solution)/shard_map/ppermute | solution.py:19
  61.4 11.6 %collective-permute-start.14 = (f16[16,6144]{1,0:T(8,128)(2,1)S(1)}, f16[16,6144]{1,0:T(8,128)(2,1)S(1)}, u32[]{:S(2)}, u32[]{:S(2)}) collective-permute-start(f16[16,6144]{1,0:T(8,128)(2,1)S(1)} %add_convert_fusion.2), channel_id=1, source_target_pairs={{0,8},{4,12},{8,0},{12,4},{16,24},{20,28},{24,16},{28,20},{1,9},{5... | collective-permute-start | bytes 589832 | tf_op jit(solution)/shard_map/ppermute | solution.py:19
  73.2 11.3 %collective-permute-start.16 = (f16[16,6144]{1,0:T(8,128)(2,1)S(1)}, f16[16,6144]{1,0:T(8,128)(2,1)S(1)}, u32[]{:S(2)}, u32[]{:S(2)}) collective-permute-start(f16[16,6144]{1,0:T(8,128)(2,1)S(1)} %convert_element_type.53), channel_id=1, source_target_pairs={{0,8},{4,12},{8,0},{12,4},{16,24},{20,28},{24,16},{28,20},{1,9},{5... | collective-permute-start | bytes 589832 | tf_op jit(solution)/shard_map/ppermute | solution.py:19
  75.1 10.9 %collective-permute-start.15 = (f16[16,6144]{1,0:T(8,128)(2,1)S(1)}, f16[16,6144]{1,0:T(8,128)(2,1)S(1)}, u32[]{:S(2)}, u32[]{:S(2)}) collective-permute-start(f16[16,6144]{1,0:T(8,128)(2,1)S(1)} %get-tuple-element.112), channel_id=1, source_target_pairs={{0,16},{4,20},{8,24},{12,28},{16,0},{20,4},{24,8},{28,12},{1,17},{... | collective-permute-start | bytes 589832 | tf_op jit(solution)/shard_map/ppermute | solution.py:19
  76.4 14.2 %collective-permute-start.17 = (bf16[16,6144]{1,0:T(8,128)(2,1)S(1)}, bf16[16,6144]{1,0:T(8,128)(2,1)S(1)}, u32[]{:S(2)}, u32[]{:S(2)}) collective-permute-start(bf16[16,6144]{1,0:T(8,128)(2,1)S(1)} %fusion.5.refs_0_), channel_id=1, source_target_pairs={{0,4},{4,0},{8,12},{12,8},{16,20},{20,16},{24,28},{28,24},{1,5},{5... | collective-permute-start | bytes 589832 | tf_op jit(solution)/shard_map/ppermute | solution.py:19
  76.4 12.0 %collective-permute-start.13 = (bf16[16,6144]{1,0:T(8,128)(2,1)S(1)}, bf16[16,6144]{1,0:T(8,128)(2,1)S(1)}, u32[]{:S(2)}, u32[]{:S(2)}) collective-permute-start(bf16[16,6144]{1,0:T(8,128)(2,1)S(1)} %collective-permute-done.11.refs_2_), channel_id=1, source_target_pairs={{0,8},{4,12},{8,0},{12,4},{16,24},{20,28},{24,16},{28,20},{1,9},{5... | collective-permute-start | bytes 589832 | tf_op jit(solution)/shard_map/ppermute | solution.py:19
  77.4 14.4 %collective-permute-start.19 = (bf16[16,6144]{1,0:T(8,128)(2,1)S(1)}, bf16[16,6144]{1,0:T(8,128)(2,1)S(1)}, u32[]{:S(2)}, u32[]{:S(2)}) collective-permute-start(bf16[16,6144]{1,0:T(8,128)(2,1)S(1)} %collective-permute-done.11.refs_2_), channel_id=1, source_target_pairs={{0,4},{4,0},{8,12},{12,8},{16,20},{20,16},{24,28},{28,24},{1,5},{5... | collective-permute-start | bytes 589832 | tf_op jit(solution)/shard_map/ppermute | solution.py:19
  88.4 3.4 %collective-permute-start.18 = (bf16[16,6144]{1,0:T(8,128)(2,1)S(1)}, bf16[16,6144]{1,0:T(8,128)(2,1)S(1)}, u32[]{:S(2)}, u32[]{:S(2)}) collective-permute-start(bf16[16,6144]{1,0:T(8,128)(2,1)S(1)} %collective-permute-done.10.refs_1_), channel_id=1, source_target_pairs={{0,4},{4,0},{8,12},{12,8},{16,20},{20,16},{24,28},{28,24},{1,5},{5... | collective-permute-start | bytes 589832 | tf_op jit(solution)/shard_map/ppermute | solution.py:19
  88.4 3.4 %collective-permute-start.20 = (bf16[16,6144]{1,0:T(8,128)(2,1)S(1)}, bf16[16,6144]{1,0:T(8,128)(2,1)S(1)}, u32[]{:S(2)}, u32[]{:S(2)}) collective-permute-start(bf16[16,6144]{1,0:T(8,128)(2,1)S(1)} %collective-permute-done.13.refs_3_), channel_id=1, source_target_pairs={{0,4},{4,0},{8,12},{12,8},{16,20},{20,16},{24,28},{28,24},{1,5},{5... | collective-permute-start | bytes 589832 | tf_op jit(solution)/shard_map/ppermute | solution.py:19
  88.9 9.7 %collective-permute-start.21 = (bf16[16,6144]{1,0:T(8,128)(2,1)S(1)}, bf16[16,6144]{1,0:T(8,128)(2,1)S(1)}, u32[]{:S(2)}, u32[]{:S(2)}) collective-permute-start(bf16[16,6144]{1,0:T(8,128)(2,1)S(1)} %add_convert_fusion.refs_0_), channel_id=1, source_target_pairs={{0,8},{4,12},{8,0},{12,4},{16,24},{20,28},{24,16},{28,20},{1,9},{5... | collective-permute-start | bytes 589832 | tf_op jit(solution)/shard_map/ppermute | solution.py:19
  90.6 11.7 %collective-permute-start.25 = (bf16[16,6144]{1,0:T(8,128)(2,1)S(1)}, bf16[16,6144]{1,0:T(8,128)(2,1)S(1)}, u32[]{:S(2)}, u32[]{:S(2)}) collective-permute-start(bf16[16,6144]{1,0:T(8,128)(2,1)S(1)} %add_convert_fusion.refs_0_), channel_id=1, source_target_pairs={{0,16},{4,20},{8,24},{12,28},{16,0},{20,4},{24,8},{28,12},{1,17},{... | collective-permute-start | bytes 589832 | tf_op jit(solution)/shard_map/ppermute | solution.py:19
  102.2 5.7 %collective-permute-start.26 = (bf16[16,6144]{1,0:T(8,128)(2,1)S(1)}, bf16[16,6144]{1,0:T(8,128)(2,1)S(1)}, u32[]{:S(2)}, u32[]{:S(2)}) collective-permute-start(bf16[16,6144]{1,0:T(8,128)(2,1)S(1)} %collective-permute-done.25.refs_2_), channel_id=1, source_target_pairs={{0,8},{4,12},{8,0},{12,4},{16,24},{20,28},{24,16},{28,20},{1,9},{5... | collective-permute-start | bytes 589832 | tf_op jit(solution)/shard_map/ppermute | solution.py:19
  102.2 5.7 %collective-permute-start.27 = (bf16[16,6144]{1,0:T(8,128)(2,1)S(1)}, bf16[16,6144]{1,0:T(8,128)(2,1)S(1)}, u32[]{:S(2)}, u32[]{:S(2)}) collective-permute-start(bf16[16,6144]{1,0:T(8,128)(2,1)S(1)} %add_convert_fusion.refs_0_), channel_id=1, source_target_pairs={{0,4},{4,0},{8,12},{12,8},{16,20},{20,16},{24,28},{28,24},{1,5},{5... | collective-permute-start | bytes 589832 | tf_op jit(solution)/shard_map/ppermute | solution.py:19
  102.2 7.0 %collective-permute-start.28 = (bf16[16,6144]{1,0:T(8,128)(2,1)S(1)}, bf16[16,6144]{1,0:T(8,128)(2,1)S(1)}, u32[]{:S(2)}, u32[]{:S(2)}) collective-permute-start(bf16[16,6144]{1,0:T(8,128)(2,1)S(1)} %collective-permute-done.21.refs_1_), channel_id=1, source_target_pairs={{0,4},{4,0},{8,12},{12,8},{16,20},{20,16},{24,28},{28,24},{1,5},{5... | collective-permute-start | bytes 589832 | tf_op jit(solution)/shard_map/ppermute | solution.py:19
  102.8 8.7 %collective-permute-start.29 = (bf16[16,6144]{1,0:T(8,128)(2,1)S(1)}, bf16[16,6144]{1,0:T(8,128)(2,1)S(1)}, u32[]{:S(2)}, u32[]{:S(2)}) collective-permute-start(bf16[16,6144]{1,0:T(8,128)(2,1)S(1)} %collective-permute-done.25.refs_2_), channel_id=1, source_target_pairs={{0,4},{4,0},{8,12},{12,8},{16,20},{20,16},{24,28},{28,24},{1,5},{5... | collective-permute-start | bytes 589832 | tf_op jit(solution)/shard_map/ppermute | solution.py:19
  107.9 3.5 %collective-permute-start.30 = (bf16[16,6144]{1,0:T(8,128)(2,1)S(1)}, bf16[16,6144]{1,0:T(8,128)(2,1)S(1)}, u32[]{:S(2)}, u32[]{:S(2)}) collective-permute-start(bf16[16,6144]{1,0:T(8,128)(2,1)S(1)} %collective-permute-done.26.refs_3_), channel_id=1, source_target_pairs={{0,4},{4,0},{8,12},{12,8},{16,20},{20,16},{24,28},{28,24},{1,5},{5... | collective-permute-start | bytes 589832 | tf_op jit(solution)/shard_map/ppermute | solution.py:19
  107.9 12.3 %collective-permute-start.22 = (bf16[1536,128]{1,0:T(8,128)(2,1)S(1)}, bf16[1536,128]{1,0:T(8,128)(2,1)S(1)}, u32[]{:S(2)}, u32[]{:S(2)}) collective-permute-start(bf16[1536,128]{1,0:T(8,128)(2,1)S(1)} %get-tuple-element.81), channel_id=1, source_target_pairs={{0,1},{1,0},{2,3},{3,2},{4,5},{5,4},{6,7},{7,6},{8,9},{9,8},{10,11... | collective-permute-start | bytes 1179656 | tf_op jit(solution)/shard_map/ppermute | solution.py:19
  107.9 20.3 %collective-permute-start.23 = (bf16[1536,128]{1,0:T(8,128)(2,1)}, bf16[1536,128]{1,0:T(8,128)(2,1)S(1)}, u32[]{:S(2)}, u32[]{:S(2)}) collective-permute-start(bf16[1536,128]{1,0:T(8,128)(2,1)} %get-tuple-element.82), channel_id=1, source_target_pairs={{0,2},{1,3},{2,0},{3,1},{4,6},{5,7},{6,4},{7,5},{8,10},{9,11},{10,... | collective-permute-start | bytes 1179656 | tf_op jit(solution)/shard_map/ppermute | solution.py:19
  109.3 19.0 %collective-permute-start.24 = (bf16[1536,128]{1,0:T(8,128)(2,1)}, bf16[1536,128]{1,0:T(8,128)(2,1)S(1)}, u32[]{:S(2)}, u32[]{:S(2)}) collective-permute-start(bf16[1536,128]{1,0:T(8,128)(2,1)} %get-tuple-element.83), channel_id=1, source_target_pairs={{0,3},{1,2},{2,1},{3,0},{4,7},{5,6},{6,5},{7,4},{8,11},{9,10},{10,... | collective-permute-start | bytes 1179656 | tf_op jit(solution)/shard_map/ppermute | solution.py:19
  116.1 20.6 %collective-permute-start.31 = (bf16[1536,128]{1,0:T(8,128)(2,1)S(1)}, bf16[1536,128]{1,0:T(8,128)(2,1)S(1)}, u32[]{:S(2)}, u32[]{:S(2)}) collective-permute-start(bf16[1536,128]{1,0:T(8,128)(2,1)S(1)} %get-tuple-element.93), channel_id=1, source_target_pairs={{0,1},{1,0},{2,3},{3,2},{4,5},{5,4},{6,7},{7,6},{8,9},{9,8},{10,11... | collective-permute-start | bytes 1179656 | tf_op jit(solution)/shard_map/ppermute | solution.py:19
  119.2 31.0 %collective-permute-start.32 = (bf16[1536,128]{1,0:T(8,128)(2,1)}, bf16[1536,128]{1,0:T(8,128)(2,1)S(1)}, u32[]{:S(2)}, u32[]{:S(2)}) collective-permute-start(bf16[1536,128]{1,0:T(8,128)(2,1)} %get-tuple-element.94), channel_id=1, source_target_pairs={{0,2},{1,3},{2,0},{3,1},{4,6},{5,7},{6,4},{7,5},{8,10},{9,11},{10,... | collective-permute-start | bytes 1179656 | tf_op jit(solution)/shard_map/ppermute | solution.py:19
  120.2 30.1 %collective-permute-start.33 = (bf16[1536,128]{1,0:T(8,128)(2,1)}, bf16[1536,128]{1,0:T(8,128)(2,1)S(1)}, u32[]{:S(2)}, u32[]{:S(2)}) collective-permute-start(bf16[1536,128]{1,0:T(8,128)(2,1)} %get-tuple-element.95), channel_id=1, source_target_pairs={{0,3},{1,2},{2,1},{3,0},{4,7},{5,6},{6,5},{7,4},{8,11},{9,10},{10,... | collective-permute-start | bytes 1179656 | tf_op jit(solution)/shard_map/ppermute | solution.py:19
  136.7 1.2 collective-permute-start.34
  138.0 3.9 %collective-permute-start.35 = (f32[64,128]{1,0:T(8,128)S(1)}, f32[64,128]{1,0:T(8,128)S(1)}, u32[]{:S(2)}, u32[]{:S(2)}) collective-permute-start(f32[64,128]{1,0:T(8,128)S(1)} %dynamic-slice_add_fusion.1), channel_id=1, source_target_pairs={{0,8},{4,12},{8,0},{12,4},{16,24},{20,28},{24,16},{28,20},{1,9},{5... | collective-permute-start | bytes 98312 | tf_op jit(solution)/shard_map/ppermute | solution.py:19
  141.9 4.9 %collective-permute-start.36 = (f32[64,128]{1,0:T(8,128)S(1)}, f32[64,128]{1,0:T(8,128)S(1)}, u32[]{:S(2)}, u32[]{:S(2)}) collective-permute-start(f32[64,128]{1,0:T(8,128)S(1)} %add.141), channel_id=1, source_target_pairs={{0,16},{4,20},{8,24},{12,28},{16,0},{20,4},{24,8},{28,12},{1,17},{... | collective-permute-start | bytes 98312 | tf_op jit(solution)/shard_map/ppermute | solution.py:19
  146.8 6.6 %collective-permute-start.41 = (f32[64,128]{1,0:T(8,128)S(1)}, f32[64,128]{1,0:T(8,128)S(1)}, u32[]{:S(2)}, u32[]{:S(2)}) collective-permute-start(f32[64,128]{1,0:T(8,128)S(1)} %add.142), channel_id=1, source_target_pairs={{0,3},{1,2},{2,1},{3,0},{4,7},{5,6},{6,5},{7,4},{8,11},{9,10},{10,... | collective-permute-start | bytes 98312 | tf_op jit(solution)/shard_map/ppermute | solution.py:19
  147.5 5.9 %collective-permute-start.40 = (f32[64,128]{1,0:T(8,128)S(1)}, f32[64,128]{1,0:T(8,128)S(1)}, u32[]{:S(2)}, u32[]{:S(2)}) collective-permute-start(f32[64,128]{1,0:T(8,128)S(1)} %add.142), channel_id=1, source_target_pairs={{0,2},{1,3},{2,0},{3,1},{4,6},{5,7},{6,4},{7,5},{8,10},{9,11},{10,... | collective-permute-start | bytes 98312 | tf_op jit(solution)/shard_map/ppermute | solution.py:19
  148.3 5.1 %collective-permute-start.39 = (f32[64,128]{1,0:T(8,128)S(1)}, f32[64,128]{1,0:T(8,128)S(1)}, u32[]{:S(2)}, u32[]{:S(2)}) collective-permute-start(f32[64,128]{1,0:T(8,128)S(1)} %add.142), channel_id=1, source_target_pairs={{0,1},{1,0},{2,3},{3,2},{4,5},{5,4},{6,7},{7,6},{8,9},{9,8},{10,11... | collective-permute-start | bytes 98312 | tf_op jit(solution)/shard_map/ppermute | solution.py:19
  153.3 1.3 collective-permute-start.37
  153.4 1.5 collective-permute-start.42
  154.6 5.2 %collective-permute-start.38 = (f32[128,128]{1,0:T(8,128)S(1)}, f32[128,128]{1,0:T(8,128)S(1)}, u32[]{:S(2)}, u32[]{:S(2)}) collective-permute-start(f32[128,128]{1,0:T(8,128)S(1)} %dynamic-slice_add_fusion), channel_id=1, source_target_pairs={{0,8},{4,12},{8,0},{12,4},{16,24},{20,28},{24,16},{28,20},{1,9},{5... | collective-permute-start | bytes 196616 | tf_op jit(solution)/shard_map/ppermute | solution.py:19
  159.8 6.6 %collective-permute-start.43 = (f32[128,128]{1,0:T(8,128)S(1)}, f32[128,128]{1,0:T(8,128)S(1)}, u32[]{:S(2)}, u32[]{:S(2)}) collective-permute-start(f32[128,128]{1,0:T(8,128)S(1)} %add.154), channel_id=1, source_target_pairs={{0,16},{4,20},{8,24},{12,28},{16,0},{20,4},{24,8},{28,12},{1,17},{... | collective-permute-start | bytes 196616 | tf_op jit(solution)/shard_map/ppermute | solution.py:19
  166.5 5.8 %collective-permute-start.46 = (f32[128,128]{1,0:T(8,128)S(1)}, f32[128,128]{1,0:T(8,128)S(1)}, u32[]{:S(2)}, u32[]{:S(2)}) collective-permute-start(f32[128,128]{1,0:T(8,128)S(1)} %add.155), channel_id=1, source_target_pairs={{0,3},{1,2},{2,1},{3,0},{4,7},{5,6},{6,5},{7,4},{8,11},{9,10},{10,... | collective-permute-start | bytes 196616 | tf_op jit(solution)/shard_map/ppermute | solution.py:19
  167.6 4.9 %collective-permute-start.45 = (f32[128,128]{1,0:T(8,128)S(1)}, f32[128,128]{1,0:T(8,128)S(1)}, u32[]{:S(2)}, u32[]{:S(2)}) collective-permute-start(f32[128,128]{1,0:T(8,128)S(1)} %add.155), channel_id=1, source_target_pairs={{0,2},{1,3},{2,0},{3,1},{4,6},{5,7},{6,4},{7,5},{8,10},{9,11},{10,... | collective-permute-start | bytes 196616 | tf_op jit(solution)/shard_map/ppermute | solution.py:19
  168.5 4.3 %collective-permute-start.44 = (f32[128,128]{1,0:T(8,128)S(1)}, f32[128,128]{1,0:T(8,128)S(1)}, u32[]{:S(2)}, u32[]{:S(2)}) collective-permute-start(f32[128,128]{1,0:T(8,128)S(1)} %add.155), channel_id=1, source_target_pairs={{0,1},{1,0},{2,3},{3,2},{4,5},{5,4},{6,7},{7,6},{8,9},{9,8},{10,11... | collective-permute-start | bytes 196616 | tf_op jit(solution)/shard_map/ppermute | solution.py:19
  172.9 1.3 collective-permute-start.47
  (7 other events, 108.0 us)

commit v3 on v2

--- a/solution.py
+++ b/solution.py
@@ -31,41 +31,55 @@
     pltpu.make_async_copy(tiles_ref.at[slot], tile_buf.at[slot], sems.at[slot]).wait()
 
 
-def transposed_kernel(count_ref, rows_ref, cols_ref, tiles_ref, *refs):
-    pieces, (mine_ref, other_ref, sketch_buf, tile_buf, sems) = refs[:-5], refs[-5:]
+def prepare_kernel(sketch_ref, *refs):
+    urgent_ref, *half_refs, flipped = refs
+    row_index = lax.axis_index("row")
+    core, place = row_index % 2, row_index // 2
+    places = lax.axis_size("row") // 2
+    flipped[...] = sketch_ref[...].T
+
+    def copy(target, index, half, which_core, offset):
+        group = (half * 2 + (core ^ which_core)) * places + (place ^ offset)
+        target[GROUP * index : GROUP * (index + 1), :] = flipped[
+            pl.ds(pl.multiple_of(group * GROUP, GROUP), GROUP), :
+        ]
+
+    for which_core in range(2):
+        for half, half_ref in enumerate(half_refs):
+            copy(urgent_ref, which_core * len(half_refs) + half, half, which_core, places - 1)
+            for offset in range(places - 1):
+                copy(half_ref, which_core * (places - 1) + offset, half, which_core, offset)
+
+
+def transposed_kernel(places, count_ref, rows_ref, cols_ref, tiles_ref, *refs):
+    *out_refs, sketch_buf, tile_buf, sems = refs[len(places) :]
     count = count_ref[0, 0]
     fetch_tiles(count, tiles_ref, tile_buf, sems)
-    row_index, col_index = lax.axis_index("row"), lax.axis_index("col")
+    col_index = lax.axis_index("col")
     tile_size = tiles_ref.shape[1]
-    width = pieces[0].shape[1]
-    groups = pieces[0].shape[0] // GROUP
-    half = groups // 2
-    core, place = row_index % 2, row_index // 2
-    for offset, piece in enumerate(pieces):
+    for (offset, start), piece in zip(places, refs):
+        depth, width = piece.shape
         lanes = pl.ds(pl.multiple_of((col_index ^ offset) * width, 128), width)
-        for group in range(groups):
-            source = (core ^ (group // half)) * half + (place ^ (group % half))
-            sketch_buf[pl.ds(group * GROUP, GROUP), lanes] = piece[
-                pl.ds(pl.multiple_of(source * GROUP, GROUP), GROUP), :
-            ]
-    mine_ref[...] = jnp.zeros_like(mine_ref)
-    other_ref[...] = jnp.zeros_like(other_ref)
-    split = mine_ref.shape[0]
+        if width == sketch_buf.shape[1]:
+            lanes = slice(None)
+        sketch_buf[start : start + depth, lanes] = piece[...]
+    for out_ref in out_refs:
+        out_ref[...] = jnp.zeros_like(out_ref)
 
     def step(slot, carry):
         wait_tile(slot, tiles_ref, tile_buf, sems)
         block = sketch_buf[:, pl.ds(pl.multiple_of(rows_ref[0, 0, slot] * tile_size, 128), tile_size)]
         product = jnp.dot(block, tile_buf[slot], preferred_element_type=jnp.float32)
         lanes = pl.ds(pl.multiple_of(cols_ref[0, 0, slot] * tile_size, 128), tile_size)
-        mine_ref[:, lanes] += product[:split]
-        other_ref[:, lanes] += product[split:]
+        depth = out_refs[0].shape[0]
+        for i, out_ref in enumerate(out_refs):
+            out_ref[:, lanes] += product[depth * i : depth * (i + 1)]
         return carry
 
     lax.fori_loop(0, count, step, 0)
 
 
-def forward_kernel(count_ref, rows_ref, cols_ref, tiles_ref, *refs):
-    outs = lax.axis_size("col")
+def forward_kernel(outs, count_ref, rows_ref, cols_ref, tiles_ref, *refs):
     column_buf, total, tile_buf, sems = refs[-4:]
     pieces, out_refs = refs[: -4 - outs], refs[-4 - outs : -4]
     count = count_ref[0, 0]
@@ -75,8 +89,11 @@
     half = len(pieces) // 2
     core, place = row_index % 2, row_index // 2
     for offset, piece in enumerate(pieces):
-        target = (core ^ (offset // half)) * half + (place ^ (offset % half))
-        column_buf[pl.ds(pl.multiple_of(target * GROUP, GROUP), GROUP), :] = piece[...]
+        if half:
+            target = (core ^ (offset // half)) * half + (place ^ (offset % half))
+            column_buf[pl.ds(pl.multiple_of(target * GROUP, GROUP), GROUP), :] = piece[...]
+        else:
+            column_buf[...] = piece[...]
     total[...] = jnp.zeros_like(total)
 
     def step(slot, carry):
@@ -91,8 +108,11 @@
     lax.fori_loop(0, count, step, 0)
     for offset, out_ref in enumerate(out_refs):
         width = out_ref.shape[0]
-        start = pl.multiple_of((col_index ^ offset) * width, 128)
-        out_ref[...] = total[pl.ds(start, width), :].astype(out_ref.dtype)
+        if outs == 1:
+            out_ref[...] = total[...]
+        else:
+            start = pl.multiple_of((col_index ^ offset) * width, 128)
+            out_ref[...] = total[pl.ds(start, width), :].astype(out_ref.dtype)
 
 
 def tile_call(kernel, out_shape, scratch, counts, rows, cols, tiles, pieces):
@@ -126,68 +146,56 @@
     return value.astype(jnp.float32)
 
 
-class Chunk:
+def gather(shard):
+    return [(0, 0, shard)] + [(d, 0, swap(shard, "col", d)) for d in range(1, lax.axis_size("col"))]
+
+
+class Half:
     def __init__(self, call_transposed, call_forward, shard):
         self.call_transposed, self.call_forward = call_transposed, call_forward
-        self.places = lax.axis_size("row") // 2
-        self.offsets = range(1, lax.axis_size("col"))
-        self.low = lambda d: d & -d
-        self.pieces = [shard] + [swap(shard, "col", d) for d in self.offsets]
+        self.shard = shard
+
+    def gather_near(self):
+        self.middle = self.shard.shape[0] // 2
+        parts = [self.shard[: self.middle], self.shard[self.middle :]]
+        self.near = [[swap(part, "col", d) for part in parts] for d in (1, 2)]
+
+    def gather_far(self):
+        first, second = self.near
+        self.pieces = [(0, 0, self.shard)]
+        self.pieces += [(d, self.middle * i, part) for d in (1, 2) for i, part in enumerate(self.near[d - 1])]
+        self.pieces.append((3, 0, swap(second[0], "col", 1)))
+        self.pieces.append((3, self.middle, swap(first[1], "col", 2)))
 
     def multiply_transposed(self, token=None):
-        self.mine, self.other = self.call_transposed(after(self.pieces, token))
+        self.mine, self.other = self.call_transposed(self.pieces, token)
 
     def send_other(self, token=None):
-        self.sent = after(self.other, token)
-        self.arrived = swap(self.sent, "row", 1)
-
-    def reduce_begin(self, token=None):
-        arrived = after(self.arrived, token)
+        self.arrived = swap(after(self.other, token), "row", 1)
+
+    def reduce(self, far):
         rows = lambda value, d: value[d * GROUP : (d + 1) * GROUP]
-        self.parts = {d: rows(self.mine, d) + rows(arrived, d) for d in range(self.places)}
-        self.arriving = {d: [] for d in range(self.places)}
-        for d in range(3, self.places, 2):
-            self.pass_on(d)
-
-    def pass_on(self, d, token=None):
-        for value in after(self.arriving[d], token):
-            self.parts[d] = self.parts[d] + full(value)
-        self.sent = half(self.parts[d])
-        bit = self.low(d)
-        self.arriving[d ^ bit].append(swap(self.sent, "row", 2 * bit))
-
-    def reduce_rest(self, token=None):
-        for d in sorted(range(2, self.places, 2), key=lambda d: (self.low(d), d)):
-            self.pass_on(d, token)
-            token = None
-        self.parts[1] = after(self.parts[1], self.sent)
-        self.pass_on(1)
+        self.parts = [rows(self.mine, d) + rows(self.arrived, d) for d in range(3)]
+        self.sent = half(self.parts[2] + full(far))
+        middle = swap(self.sent, "row", 4)
+        self.arriving = [middle]
+
+    def reduce_last(self, token):
+        self.arriving.append(swap(half(after(self.parts[1], token)), "row", 2))
 
     def own(self, token=None):
-        for value in after(self.arriving[0], token):
-            self.parts[0] = self.parts[0] + full(value)
-        self.whole = {0: self.parts[0].astype(jnp.bfloat16)}
-        self.ways = sorted(range(1, self.places), key=lambda d: (bin(d).count("1"), -d))
-        for d in self.ways:
-            if bin(d).count("1") == 1 and d > 1:
-                self.spread(d)
-
-    def spread(self, d, token=None):
-        self.whole[d] = swap(after(self.whole[d ^ self.low(d)], token), "row", 2 * self.low(d))
-
-    def spread_rest(self, token=None):
-        first = self.ways[0]
-        if token is not None:
-            self.whole[first] = after(self.whole[first], token)
-        for d in self.ways:
-            if d not in self.whole:
-                self.spread(d)
+        middle, low = after(self.arriving, token)
+        self.whole = {0: (self.parts[0] + full(middle) + full(low)).astype(jnp.bfloat16)}
+        self.whole[2] = swap(self.whole[0], "row", 4)
+        self.whole[1] = swap(self.whole[0], "row", 2)
+
+    def spread(self, token=None):
+        self.whole[2] = after(self.whole[2], token)
+        self.whole[3] = swap(self.whole[2], "row", 2)
 
     def share(self, token=None):
-        near = [self.whole[d] for d in range(self.places)]
-        late = [d for d in range(1, self.places) if d != self.ways[0]]
-        for d, value in zip(late, after([near[d] for d in late], token)):
-            near[d] = value
+        self.whole[1], self.whole[3] = after([self.whole[1], self.whole[3]], token)
+        near = [self.whole[d] for d in range(4)]
         self.columns = near + [swap(v, "row", 1) for v in near]
 
     def multiply_forward(self, token=None):
@@ -195,52 +203,54 @@
 
     def send_rows(self, token=None):
         self.total, *self.sent = after(self.forward, token)
-        self.arrived = [swap(value, "col", d) for d, value in zip(self.offsets, self.sent)]
+        self.arrived = [swap(value, "col", d + 1) for d, value in enumerate(self.sent)]
 
     def finish(self, token=None, *others):
-        parts = [self.total] + after(self.arrived, token)
-        shape = self.total.shape
-        return pl.pallas_call(
-            finish_kernel,
-            out_shape=(
-                jax.ShapeDtypeStruct(shape, jnp.float32),
-                jax.ShapeDtypeStruct((shape[1] * (len(others) + 1), shape[1]), jnp.float32),
-            ),
-            compiler_params=pltpu.CompilerParams(vmem_limit_bytes=VMEM_LIMIT),
-            cost_estimate=NO_COST,
-        )(*others, *parts)
-
-
-def run_alone(chunk):
-    for step in (
-        chunk.multiply_transposed, chunk.send_other, chunk.reduce_begin, chunk.reduce_rest, chunk.own,
-        chunk.spread_rest, chunk.share, chunk.multiply_forward, chunk.send_rows,
-    ):
-        step()
-    return chunk.finish()
-
-
-def run_pair(a, b):
-    a.multiply_transposed()
-    a.send_other(b.pieces[1:3])
-    a.reduce_begin()
-    a.reduce_rest()
+        return finish_call([self.total] + after(self.arrived, token), *others)
+
+
+def finish_call(parts, *others):
+    shape = parts[0].shape
+    return pl.pallas_call(
+        functools.partial(finish_kernel, len(parts)),
+        out_shape=(
+            jax.ShapeDtypeStruct(shape, jnp.float32),
+            jax.ShapeDtypeStruct((shape[1] * (len(others) + 1), shape[1]), jnp.float32),
+        ),
+        compiler_params=pltpu.CompilerParams(vmem_limit_bytes=VMEM_LIMIT),
+        cost_estimate=NO_COST,
+    )(*others, *parts)
+
+
+def run_pair(call_transposed, a, b, urgent):
+    pieces = gather(urgent)
+    a.gather_near()
+    mine, other = call_transposed(pieces, None)
+    arrived = swap(after(other, a.near), "row", 1)
+    a.gather_far()
+    b.shard = after(b.shard, [piece[2] for piece in a.pieces[5:]])
+    b.gather_near()
+    sent = half(mine + arrived)
+    far = swap(sent, "row", 2)
+    a.multiply_transposed(sent)
+    a.send_other([b.near, far])
+    b.gather_far()
+    a.reduce(far[:GROUP])
+    a.reduce_last(a.sent)
     b.multiply_transposed(a.sent)
     b.send_other(a.arriving[0])
-    a.own(b.sent)
-    a.spread(1)
-    b.reduce_begin(a.whole[0])
-    a.spread_rest(b.sent)
-    b.reduce_rest([a.whole[1], a.whole[2]])
-    b.own()
-    b.spread(1)
-    a.share(b.whole[0])
+    a.own(b.other)
+    b.reduce(after(far[GROUP:], a.whole[0]))
+    a.spread(b.sent)
+    b.reduce_last(a.whole[3])
+    a.share()
     a.multiply_forward()
-    a.send_rows(b.whole[1])
-    b.spread_rest(a.sent)
+    b.own(a.forward)
+    a.send_rows()
+    b.spread(a.arrived[:2])
     b.share()
-    b.multiply_forward(a.sent)
-    b.send_rows()
+    b.multiply_forward()
+    b.send_rows(a.arrived[2:])
 
 
 class Sum:
@@ -251,13 +261,10 @@
         other = lax.dynamic_slice_in_dim(value, (1 - self.core) * half, half, 0)
         self.mine = mine + swap(other, "row", 1)
 
-    def over_row(self, token=None):
+    def over_row(self, tokens):
         bit = 2
         while bit < lax.axis_size("row"):
-            arrived = swap(self.mine, "row", bit)
-            if token is not None and bit == 2:
-                arrived = after(arrived, token)
-            self.mine = self.mine + arrived
+            self.mine = self.mine + after(swap(self.mine, "row", bit), tokens.get(bit))
             bit *= 2
 
     def over_col(self, token=None):
@@ -283,8 +290,7 @@
     )
 
 
-def finish_kernel(*refs):
-    parts = lax.axis_size("col")
+def finish_kernel(parts, *refs):
     rows_ref, gram_ref = refs[-2:]
     others, parts = refs[: -2 - parts], refs[-2 - parts : -2]
     total = parts[0][...]
@@ -364,45 +370,61 @@
     tiles = tiles[0, 0]
     slots, tile_size, _ = tiles.shape
     width, sketch_width = sketch.shape
-    chunk = min(sketch_width, GROUP * lax.axis_size("row"))
     group_rows, group_cols = BR * tile_size, BC * tile_size
-    shard = sketch.T
-    partial = jax.ShapeDtypeStruct((chunk // 2, group_cols), jnp.float32)
-    call_transposed = lambda pieces: tile_call(
-        transposed_kernel,
-        (partial, partial),
-        [pltpu.VMEM((chunk, group_rows), jnp.bfloat16)],
-        tile_counts, tile_rows, tile_cols, tiles, pieces,
-    )
-    call_forward = lambda pieces: tile_call(
-        forward_kernel,
-        tuple(
-            jax.ShapeDtypeStruct((width, chunk), jnp.bfloat16 if offset else jnp.float32)
-            for offset in range(lax.axis_size("col"))
-        ),
-        [pltpu.VMEM((chunk, group_cols), jnp.bfloat16), pltpu.VMEM((group_rows, chunk), jnp.float32)],
-        tile_counts, tile_rows, tile_cols, tiles, pieces,
-    )
-    chunks = [
-        Chunk(call_transposed, call_forward, shard[start : start + chunk])
-        for start in range(0, sketch_width, chunk)
-    ]
     split = sketch_width // 2
-    if len(chunks) == 2:
-        run_pair(*chunks)
-        first, first_gram = chunks[0].finish(chunks[1].sent)
-        first_gram = after(first_gram, chunks[1].arrived[:1])
+    rows_axis, cols_axis = lax.axis_size("row"), lax.axis_size("col")
+
+    def call_transposed(pieces, token):
+        depth = pieces[0][2].shape[0]
+        outs = 2 if rows_axis == 8 else 1
+        return tile_call(
+            functools.partial(transposed_kernel, [piece[:2] for piece in pieces]),
+            [jax.ShapeDtypeStruct((depth // outs, group_cols), jnp.float32)] * outs,
+            [pltpu.VMEM((depth, group_rows), jnp.bfloat16)],
+            tile_counts, tile_rows, tile_cols, tiles, after([piece[2] for piece in pieces], token),
+        )
+
+    def call_forward(columns, outs=cols_axis):
+        depth = sum(piece.shape[0] for piece in columns)
+        return tile_call(
+            functools.partial(forward_kernel, outs),
+            [
+                jax.ShapeDtypeStruct((group_rows // outs, depth), jnp.bfloat16 if offset else jnp.float32)
+                for offset in range(outs)
+            ],
+            [pltpu.VMEM((depth, group_cols), jnp.bfloat16), pltpu.VMEM((group_rows, depth), jnp.float32)],
+            tile_counts, tile_rows, tile_cols, tiles, columns,
+        )
+
+    paired = rows_axis == 8 and cols_axis == 4 and sketch_width == 2 * GROUP * rows_axis
+    if paired:
+        part = lambda groups: jax.ShapeDtypeStruct((groups * GROUP, width), jnp.bfloat16)
+        urgent, *halves = pl.pallas_call(
+            prepare_kernel,
+            out_shape=[part(4), part(6), part(6)],
+            scratch_shapes=[pltpu.VMEM((sketch_width, width), jnp.bfloat16)],
+            compiler_params=pltpu.CompilerParams(vmem_limit_bytes=VMEM_LIMIT),
+            cost_estimate=NO_COST,
+        )(sketch)
+        a, b = [Half(call_transposed, call_forward, shard) for shard in halves]
+        run_pair(call_transposed, a, b, urgent)
+        first, first_gram = a.finish(b.sent)
     else:
-        whole, gram = run_alone(chunks[0])
+        everything = lax.all_gather(sketch.T, "col", axis=1, tiled=True)
+        (partial,) = call_transposed([(0, 0, everything)], None)
+        columns = lax.psum_scatter(partial, "row", scatter_dimension=0, tiled=True).astype(jnp.bfloat16)
+        columns = lax.all_gather(columns, "row", axis=0, tiled=True)
+        (partial,) = call_forward([columns], 1)
+        whole, gram = finish_call([lax.psum_scatter(partial, "col", scatter_dimension=0, tiled=True)])
         first, second = whole[:, :split], whole[:, split:]
         first_gram, mixed_gram = gram[:split, :split], gram[:, split:]
     total_rows = group_rows * lax.axis_size("row")
     params = pltpu.CompilerParams(vmem_limit_bytes=VMEM_LIMIT)
     square = jax.ShapeDtypeStruct((split, split), jnp.float32)
     first_gram = Sum(first_gram)
-    first_gram.over_row()
-    if len(chunks) == 2:
-        second, mixed_gram = chunks[1].finish(first_gram.mine, first)
+    first_gram.over_row({2: b.arrived[:1]} if paired else {})
+    if paired:
+        second, mixed_gram = b.finish(first_gram.mine, first)
     first_gram.over_col()
     mixed_gram = Sum(mixed_gram)
     upper, inverse, first_basis = pl.pallas_call(
@@ -410,7 +432,7 @@
         out_shape=(square, square, jax.ShapeDtypeStruct(first.shape, jnp.float32)),
         compiler_params=params,
     )(first_gram.finish(), first)
-    mixed_gram.over_row(upper)
+    mixed_gram.over_row({4: upper})
     mixed_gram.over_col()
     return pl.pallas_call(
         functools.partial(second_factor_kernel, total_rows),

time: 182 us -> 172 us (0.945)
  waiting for transfers between devices: 89.8 us -> 70.1 us
  Pallas kernels: 35.7 us -> 52.8 us
  starting transfers between devices: 49.3 us -> 41.1 us
    ppermute x48 -> x57, waiting for transfers between devices: 89.8 us -> 70.1 us  [swap(): return lax.ppermute(value, axis, [(i, i ^ offset) for i in range(size)])]
    pallas_call x4 -> x5, Pallas kernels: 18.4 us -> 35.2 us  [tile_call(): pl.pallas_call(kernel, out_shape=out_shape, in_specs=[smem, smem, smem, p...]
    ppermute x48 -> x57, starting transfers between devices: 49.3 us -> 41.1 us  [swap(): return lax.ppermute(value, axis, [(i, i ^ offset) for i in range(size)])]
    pallas_call x2 -> x3, Pallas kernels: 5.03 us -> 5.28 us  [the longest x2 4.98 us: finish_call(): pl.pallas_call(functools.partial(finish_kernel, len(parts)), out_shape=(j...]
  transfers between devices with their start and end apart: 48 -> 57, of which waited for: 27 -> 24; matrix products, arithmetic and copies ran while one was open for 1% -> 1% of each run, Pallas kernels for 16% -> 26%
where the time goes in v3:
time: 172 us; the launch traced here: 171 us
  waiting for transfers between devices  70.1 us (41%)
  Pallas kernels  52.8 us (31%)
  starting transfers between devices  41.1 us (24%)
  other arithmetic  2.92 us (2%)
  local copies, waits for them, and re-layouts  2.08 us (1%)
  between operations  1.9 us (1%)
    ppermute x57, waiting for transfers between devices, swap(): return lax.ppermute(value, axis, [(i, i ^ offset) for i in range(size)])  70.1 us
    ppermute x57, starting transfers between devices, swap(): return lax.ppermute(value, axis, [(i, i ^ offset) for i in range(size)])  41.1 us
    pallas_call x5, Pallas kernels, tile_call(): pl.pallas_call(kernel, out_shape=out_shape, in_specs=[smem, smem, smem, p...  35.2 us
    pallas_call x1, Pallas kernels, body(): pl.pallas_call(functools.partial(second_factor_kernel, total_rows), out_s...  7.39 us
    pallas_call x2, Pallas kernels, finish_call(): pl.pallas_call(functools.partial(finish_kernel, len(parts)), out_shape=(j...  4.98 us
    pallas_call x1, Pallas kernels, body(): pl.pallas_call(functools.partial(first_factor_kernel, total_rows), out_sh...  4.88 us
  transfers between devices with their start and end apart: 57, of which 24 were waited for; matrix products, arithmetic and copies ran while one was open for 1% of the time, Pallas kernels for 26%

profile of v3, /device:TPU:0, one launch (start us, length us, event | category | flops | bytes accessed | tf_op | source)
XLA Modules:
  0.0 170.8 jit_solution(499154454624676971)
XLA Ops:
  0.6 1.1 copy-done.3
  2.1 4.0 %collective-permute-start.8 = (bf16[64,1536]{1,0:T(8,128)(2,1)S(1)}, bf16[64,1536]{1,0:T(8,128)(2,1)S(1)}, u32[]{:S(2)}, u32[]{:S(2)}) collective-permute-start(bf16[64,1536]{1,0:T(8,128)(2,1)S(1)} %get-tuple-element.66.refs_0_), channel_id=1, source_target_pairs={{0,3},{1,2},{2,1},{3,0},{4,7},{5,6},{6,5},{7,4},{8,11},{9,10},{10,... | collective-permute-start | bytes 589832 | tf_op jit(solution)/shard_map/ppermute | solution.py:19
  6.7 2.0 %collective-permute-start.3 = (bf16[48,1536]{1,0:T(8,128)(2,1)S(1)}, bf16[48,1536]{1,0:T(8,128)(2,1)S(1)}, u32[]{:S(2)}, u32[]{:S(2)}) collective-permute-start(bf16[48,1536]{1,0:T(8,128)(2,1)S(1)} %get-tuple-element.134), channel_id=1, source_target_pairs={{0,2},{1,3},{2,0},{3,1},{4,6},{5,7},{6,4},{7,5},{8,10},{9,11},{10,... | collective-permute-start | bytes 442376 | tf_op jit(solution)/shard_map/ppermute | solution.py:19
  8.7 1.5 collective-permute-start.1
  10.2 1.6 collective-permute-done.8.refs_3_
  11.8 2.0 %collective-permute-start.2 = (bf16[48,1536]{1,0:T(8,128)(2,1)S(1)}, bf16[48,1536]{1,0:T(8,128)(2,1)S(1)}, u32[]{:S(2)}, u32[]{:S(2)}) collective-permute-start(bf16[48,1536]{1,0:T(8,128)(2,1)S(1)} %get-tuple-element.135), channel_id=1, source_target_pairs={{0,2},{1,3},{2,0},{3,1},{4,6},{5,7},{6,4},{7,5},{8,10},{9,11},{10,... | collective-permute-start | bytes 442376 | tf_op jit(solution)/shard_map/ppermute | solution.py:19
  13.8 1.4 collective-permute-done.7.refs_2_
  15.3 1.7 collective-permute-start
  17.6 6.0 %shard_map.69 = (f32[32,6144]{1,0:T(8,128)S(1)}, f32[32,6144]{1,0:T(8,128)}) custom-call(s32[1,1]{1,0:T(1,128)S(6)} %copy.7.count_ref, s32[1,1,16]{2,1,0:T(1,128)S(1)} %copy-done.4, s32[1,1,16]{2,1,0:T(1,128)S(1)} %copy-done.5, bf16[16,512,512]{2,1,0:T(8,128)(2,1)} %bitcast.13, bf16[64,1536]{1,0:T(8,128)(2,1)S(1)} %get-tuple-element.66.refs_0_, ...), custom_call_target="tpu_custom_call" | custom-call | tf_op jit(solution)/shard_map/pallas_call | solution.py:122
  24.6 5.4 %collective-permute-done.5.refs_6_ = bf16[48,1536]{1,0:T(8,128)(2,1)S(1)} collective-permute-done((bf16[48,1536]{1,0:T(8,128)(2,1)S(1)}, bf16[48,1536]{1,0:T(8,128)(2,1)S(1)}, u32[]{:S(2)}, u32[]{:S(2)}) %collective-permute-start.5) | collective-permute-done | bytes 147488 | tf_op jit(solution)/shard_map/ppermute | solution.py:19
  30.1 1.7 collective-permute-start.14
  31.8 1.1 collective-permute-start.13
  34.1 1.7 %collective-permute-start.10 = (bf16[48,1536]{1,0:T(8,128)(2,1)S(1)}, bf16[48,1536]{1,0:T(8,128)(2,1)S(1)}, u32[]{:S(2)}, u32[]{:S(2)}) collective-permute-start(bf16[48,1536]{1,0:T(8,128)(2,1)S(1)} %get-tuple-element.133), channel_id=1, source_target_pairs={{0,1},{1,0},{2,3},{3,2},{4,5},{5,4},{6,7},{7,6},{8,9},{9,8},{10,11... | collective-permute-start | bytes 442376 | tf_op jit(solution)/shard_map/ppermute | solution.py:19
  35.9 6.8 %shard_map.70 = (f32[48,6144]{1,0:T(8,128)}, f32[48,6144]{1,0:T(8,128)}) custom-call(s32[1,1]{1,0:T(1,128)S(6)} %copy.7.count_ref, s32[1,1,16]{2,1,0:T(1,128)S(1)} %copy-done.4, s32[1,1,16]{2,1,0:T(1,128)S(1)} %copy-done.5, bf16[16,512,512]{2,1,0:T(8,128)(2,1)} %bitcast.14, bf16[96,1536]{1,0:T(8,128)(2,1)S(1)} %get-tuple-element.70.refs_0_, ...), custom_call_target="tpu_custom_call" | custom-call | tf_op jit(solution)/shard_map/pallas_call | solution.py:122
  42.8 3.0 %collective-permute-done.15 = f32[48,6144]{1,0:T(8,128)S(1)} collective-permute-done((f32[48,6144]{1,0:T(8,128)}, f32[48,6144]{1,0:T(8,128)S(1)}, u32[]{:S(2)}, u32[]{:S(2)}) %collective-permute-start.15) | collective-permute-done | bytes 1179680 | tf_op jit(solution)/shard_map/ppermute | solution.py:19
  45.9 1.3 slice_add_fusion.3
  49.1 1.4 collective-permute-start.18
  50.5 3.3 %collective-permute-done.19.refs_6_ = bf16[48,1536]{1,0:T(8,128)(2,1)S(1)} collective-permute-done((bf16[48,1536]{1,0:T(8,128)(2,1)S(1)}, bf16[48,1536]{1,0:T(8,128)(2,1)S(1)}, u32[]{:S(2)}, u32[]{:S(2)}) %collective-permute-start.19) | collective-permute-done | bytes 147488 | tf_op jit(solution)/shard_map/ppermute | solution.py:19
  54.2 6.8 %shard_map.71 = (f32[48,6144]{1,0:T(8,128)}, f32[48,6144]{1,0:T(8,128)}) custom-call(s32[1,1]{1,0:T(1,128)S(6)} %copy.7.count_ref, s32[1,1,16]{2,1,0:T(1,128)S(1)} %copy-done.4, s32[1,1,16]{2,1,0:T(1,128)S(1)} %copy-done.5, bf16[16,512,512]{2,1,0:T(8,128)(2,1)} %bitcast.15, bf16[96,1536]{1,0:T(8,128)(2,1)S(1)} %get-tuple-element.83.refs_0_, ...), custom_call_target="tpu_custom_call" | custom-call | tf_op jit(solution)/shard_map/pallas_call | solution.py:122
  61.1 1.2 fusion.9.refs_0_
  64.3 10.4 %collective-permute-done.21.refs_2_ = bf16[16,6144]{1,0:T(8,128)(2,1)S(1)} collective-permute-done((bf16[16,6144]{1,0:T(8,128)(2,1)S(1)}, bf16[16,6144]{1,0:T(8,128)(2,1)S(1)}, u32[]{:S(2)}, u32[]{:S(2)}) %collective-permute-start.21) | collective-permute-done | bytes 196640 | tf_op jit(solution)/shard_map/ppermute | solution.py:19
  75.3 1.6 collective-permute-start.31
  76.8 5.9 %collective-permute-done.23.refs_3_ = bf16[16,6144]{1,0:T(8,128)(2,1)S(1)} collective-permute-done((bf16[16,6144]{1,0:T(8,128)(2,1)S(1)}, bf16[16,6144]{1,0:T(8,128)(2,1)S(1)}, u32[]{:S(2)}, u32[]{:S(2)}) %collective-permute-start.23) | collective-permute-done | bytes 196640 | tf_op jit(solution)/shard_map/ppermute | solution.py:19
  82.9 1.3 collective-permute-done.27.refs_7_
  84.2 7.8 %shard_map.72 = (f32[1536,128]{1,0:T(8,128)}, bf16[1536,128]{1,0:T(8,128)(2,1)S(1)}, bf16[1536,128]{1,0:T(8,128)(2,1)}, bf16[1536,128]{1,0:T(8,128)(2,1)}) custom-call(s32[1,1]{1,0:T(1,128)S(6)} %copy.7.count_ref, s32[1,1,16]{2,1,0:T(1,128)S(1)} %copy-done.4, s32[1,1,16]{2,1,0:T(1,128)S(1)} %copy-done.5, bf16[16,512,512]{2,1,0:T(8,128)(2,1)} %bitcast.16, ...), custom_call_target="tpu_custom_call" | custom-call | tf_op jit(solution)/shard_map/pallas_call | solution.py:122
  92.9 1.5 collective-permute-start.33
  94.3 9.8 %collective-permute-done.34.refs_2_ = bf16[16,6144]{1,0:T(8,128)(2,1)S(1)} collective-permute-done((bf16[16,6144]{1,0:T(8,128)(2,1)S(1)}, bf16[16,6144]{1,0:T(8,128)(2,1)S(1)}, u32[]{:S(2)}, u32[]{:S(2)}) %collective-permute-start.34) | collective-permute-done | bytes 196640 | tf_op jit(solution)/shard_map/ppermute | solution.py:19
  104.1 1.4 collective-permute-start.30
  106.1 4.8 %collective-permute-done.35.refs_3_ = bf16[16,6144]{1,0:T(8,128)(2,1)S(1)} collective-permute-done((bf16[16,6144]{1,0:T(8,128)(2,1)S(1)}, bf16[16,6144]{1,0:T(8,128)(2,1)S(1)}, u32[]{:S(2)}, u32[]{:S(2)}) %collective-permute-start.35) | collective-permute-done | bytes 196640 | tf_op jit(solution)/shard_map/ppermute | solution.py:19
  110.9 1.4 collective-permute-done.39.refs_7_
  112.3 8.0 %shard_map.73 = (f32[1536,128]{1,0:T(8,128)}, bf16[1536,128]{1,0:T(8,128)(2,1)S(1)}, bf16[1536,128]{1,0:T(8,128)(2,1)}, bf16[1536,128]{1,0:T(8,128)(2,1)}) custom-call(s32[1,1]{1,0:T(1,128)S(6)} %copy.7.count_ref, s32[1,1,16]{2,1,0:T(1,128)S(1)} %copy-done.4, s32[1,1,16]{2,1,0:T(1,128)S(1)} %copy-done.5, bf16[16,512,512]{2,1,0:T(8,128)(2,1)} %bitcast.17, ...), custom_call_target="tpu_custom_call" | custom-call | tf_op jit(solution)/shard_map/pallas_call | solution.py:122
  120.7 3.2 %collective-permute-start.42 = (bf16[1536,128]{1,0:T(8,128)(2,1)}, bf16[1536,128]{1,0:T(8,128)(2,1)S(1)}, u32[]{:S(2)}, u32[]{:S(2)}) collective-permute-start(bf16[1536,128]{1,0:T(8,128)(2,1)} %get-tuple-element.111), channel_id=1, source_target_pairs={{0,3},{1,2},{2,1},{3,0},{4,7},{5,6},{6,5},{7,4},{8,11},{9,10},{10,... | collective-permute-start | bytes 1179656 | tf_op jit(solution)/shard_map/ppermute | solution.py:19
  123.9 2.0 %shard_map.74 = (f32[1536,128]{1,0:T(8,128)S(1)}, f32[128,128]{1,0:T(8,128)S(1)}) custom-call(f32[1536,128]{1,0:T(8,128)} %get-tuple-element.97.refs_0_, bf16[1536,128]{1,0:T(8,128)(2,1)S(1)} %collective-permute-done.28.refs_1_, bf16[1536,128]{1,0:T(8,128)(2,1)S(1)} %collective-permute-done.29.refs_2_, bf16[1536,128]{1,0:T(8,128)(2,1)S(1)} %collective-permute-done.30.refs_3_), custom_call_target="tpu_custom_call" | custom-call | tf_op jit(solution)/shard_map/pallas_call | solution.py:214
  126.8 1.2 collective-permute-done.43
  128.0 3.9 %collective-permute-done.44 = f32[64,128]{1,0:T(8,128)S(1)} collective-permute-done((f32[64,128]{1,0:T(8,128)S(1)}, f32[64,128]{1,0:T(8,128)S(1)}, u32[]{:S(2)}, u32[]{:S(2)}) %collective-permute-start.44) | collective-permute-done | bytes 32800 | tf_op jit(solution)/shard_map/ppermute | solution.py:19
  132.5 4.8 %collective-permute-done.45 = f32[64,128]{1,0:T(8,128)S(1)} collective-permute-done((f32[64,128]{1,0:T(8,128)S(1)}, f32[64,128]{1,0:T(8,128)S(1)}, u32[]{:S(2)}, u32[]{:S(2)}) %collective-permute-start.45) | collective-permute-done | bytes 32800 | tf_op jit(solution)/shard_map/ppermute | solution.py:19
  137.3 1.8 %collective-permute-start.50 = (f32[64,128]{1,0:T(8,128)S(1)}, f32[64,128]{1,0:T(8,128)S(1)}, u32[]{:S(2)}, u32[]{:S(2)}) collective-permute-start(f32[64,128]{1,0:T(8,128)S(1)} %add.138), channel_id=1, source_target_pairs={{0,2},{1,3},{2,0},{3,1},{4,6},{5,7},{6,4},{7,5},{8,10},{9,11},{10,... | collective-permute-start | bytes 98312 | tf_op jit(solution)/shard_map/ppermute | solution.py:19
  139.0 1.7 collective-permute-start.49
  140.7 2.9 %shard_map.75 = (f32[1536,128]{1,0:T(8,128)}, f32[256,128]{1,0:T(8,128)S(1)}) custom-call(f32[1536,128]{1,0:T(8,128)} %copy-done, f32[1536,128]{1,0:T(8,128)} %get-tuple-element.116.refs_1_, bf16[1536,128]{1,0:T(8,128)(2,1)S(1)} %collective-permute-done.40.refs_2_, bf16[1536,128]{1,0:T(8,128)(2,1)S(1)} %collective-permute-done.41.refs_3_, ...), custom_call_target="tpu_custom_call" | custom-call | tf_op jit(solution)/shard_map/pallas_call | solution.py:214
  143.8 1.2 collective-permute-done.46
  145.4 4.0 %collective-permute-done.47 = f32[128,128]{1,0:T(8,128)S(1)} collective-permute-done((f32[128,128]{1,0:T(8,128)S(1)}, f32[128,128]{1,0:T(8,128)S(1)}, u32[]{:S(2)}, u32[]{:S(2)}) %collective-permute-start.47) | collective-permute-done | bytes 65568 | tf_op jit(solution)/shard_map/ppermute | solution.py:19
  149.5 4.9 %shard_map.76 = (f32[128,128]{1,0:T(8,128)S(1)}, f32[128,128]{1,0:T(8,128)S(1)}, f32[1536,128]{1,0:T(8,128)S(1)}) custom-call(f32[128,128]{1,0:T(8,128)S(1)} %maximum_select_fusion.1.gram_ref, f32[1536,128]{1,0:T(8,128)S(1)} %copy-done.1), custom_call_target="tpu_custom_call" | custom-call | tf_op jit(solution)/shard_map/pallas_call | solution.py:430
  154.9 1.1 collective-permute-start.55
  156.0 1.8 %collective-permute-start.54 = (f32[128,128]{1,0:T(8,128)S(1)}, f32[128,128]{1,0:T(8,128)S(1)}, u32[]{:S(2)}, u32[]{:S(2)}) collective-permute-start(f32[128,128]{1,0:T(8,128)S(1)} %add.151), channel_id=1, source_target_pairs={{0,2},{1,3},{2,0},{3,1},{4,6},{5,7},{6,4},{7,5},{8,10},{9,11},{10,... | collective-permute-start | bytes 196616 | tf_op jit(solution)/shard_map/ppermute | solution.py:19
  158.5 1.7 %collective-permute-done.55 = f32[128,128]{1,0:T(8,128)S(1)} collective-permute-done((f32[128,128]{1,0:T(8,128)S(1)}, f32[128,128]{1,0:T(8,128)S(1)}, u32[]{:S(2)}, u32[]{:S(2)}) %collective-permute-start.55) | collective-permute-done | bytes 65568 | tf_op jit(solution)/shard_map/ppermute | solution.py:19
  160.9 1.2 collective-permute-done.53
  162.2 1.2 collective-permute-done.56
  163.4 7.4 %shard_map.77 = (f32[1536,256]{1,0:T(8,128)}, f32[256,256]{1,0:T(8,128)}) custom-call(f32[256,128]{1,0:T(8,128)S(1)} %maximum_select_fusion.gram_ref, f32[128,128]{1,0:T(8,128)S(1)} %get-tuple-element.123.upper_ref, f32[128,128]{1,0:T(8,128)S(1)} %get-tuple-element.125.inverse_ref, f32[1536,128]{1,0:T(8,128)S(1)} %get-tuple-element.126.first_ref, ...), custom_call_target="tpu_custom_call" | custom-call | tf_op jit(solution)/shard_map/pallas_call | solution.py:437
  (119 shorter events, 14.1 us)
Async XLA Ops:
  2.1 9.7 %collective-permute-start.8 = (bf16[64,1536]{1,0:T(8,128)(2,1)S(1)}, bf16[64,1536]{1,0:T(8,128)(2,1)S(1)}, u32[]{:S(2)}, u32[]{:S(2)}) collective-permute-start(bf16[64,1536]{1,0:T(8,128)(2,1)S(1)} %get-tuple-element.66.refs_0_), channel_id=1, source_target_pairs={{0,3},{1,2},{2,1},{3,0},{4,7},{5,6},{6,5},{7,4},{8,11},{9,10},{10,... | collective-permute-start | bytes 589832 | tf_op jit(solution)/shard_map/ppermute | solution.py:19
  6.0 9.2 %collective-permute-start.7 = (bf16[64,1536]{1,0:T(8,128)(2,1)S(1)}, bf16[64,1536]{1,0:T(8,128)(2,1)S(1)}, u32[]{:S(2)}, u32[]{:S(2)}) collective-permute-start(bf16[64,1536]{1,0:T(8,128)(2,1)S(1)} %get-tuple-element.66.refs_0_), channel_id=1, source_target_pairs={{0,2},{1,3},{2,0},{3,1},{4,6},{5,7},{6,4},{7,5},{8,10},{9,11},{10,... | collective-permute-start | bytes 589832 | tf_op jit(solution)/shard_map/ppermute | solution.py:19
  6.5 11.0 %collective-permute-start.6 = (bf16[64,1536]{1,0:T(8,128)(2,1)S(1)}, bf16[64,1536]{1,0:T(8,128)(2,1)S(1)}, u32[]{:S(2)}, u32[]{:S(2)}) collective-permute-start(bf16[64,1536]{1,0:T(8,128)(2,1)S(1)} %get-tuple-element.66.refs_0_), channel_id=1, source_target_pairs={{0,1},{1,0},{2,3},{3,2},{4,5},{5,4},{6,7},{7,6},{8,9},{9,8},{10,11... | collective-permute-start | bytes 589832 | tf_op jit(solution)/shard_map/ppermute | solution.py:19
  6.7 16.9 %collective-permute-start.3 = (bf16[48,1536]{1,0:T(8,128)(2,1)S(1)}, bf16[48,1536]{1,0:T(8,128)(2,1)S(1)}, u32[]{:S(2)}, u32[]{:S(2)}) collective-permute-start(bf16[48,1536]{1,0:T(8,128)(2,1)S(1)} %get-tuple-element.134), channel_id=1, source_target_pairs={{0,2},{1,3},{2,0},{3,1},{4,6},{5,7},{6,4},{7,5},{8,10},{9,11},{10,... | collective-permute-start | bytes 442376 | tf_op jit(solution)/shard_map/ppermute | solution.py:19
  8.7 14.9 %collective-permute-start.1 = (bf16[48,1536]{1,0:T(8,128)(2,1)S(1)}, bf16[48,1536]{1,0:T(8,128)(2,1)S(1)}, u32[]{:S(2)}, u32[]{:S(2)}) collective-permute-start(bf16[48,1536]{1,0:T(8,128)(2,1)S(1)} %get-tuple-element.134), channel_id=1, source_target_pairs={{0,1},{1,0},{2,3},{3,2},{4,5},{5,4},{6,7},{7,6},{8,9},{9,8},{10,11... | collective-permute-start | bytes 442376 | tf_op jit(solution)/shard_map/ppermute | solution.py:19
  11.8 11.8 %collective-permute-start.2 = (bf16[48,1536]{1,0:T(8,128)(2,1)S(1)}, bf16[48,1536]{1,0:T(8,128)(2,1)S(1)}, u32[]{:S(2)}, u32[]{:S(2)}) collective-permute-start(bf16[48,1536]{1,0:T(8,128)(2,1)S(1)} %get-tuple-element.135), channel_id=1, source_target_pairs={{0,2},{1,3},{2,0},{3,1},{4,6},{5,7},{6,4},{7,5},{8,10},{9,11},{10,... | collective-permute-start | bytes 442376 | tf_op jit(solution)/shard_map/ppermute | solution.py:19
  15.3 8.4 %collective-permute-start = (bf16[48,1536]{1,0:T(8,128)(2,1)S(1)}, bf16[48,1536]{1,0:T(8,128)(2,1)S(1)}, u32[]{:S(2)}, u32[]{:S(2)}) collective-permute-start(bf16[48,1536]{1,0:T(8,128)(2,1)S(1)} %get-tuple-element.135), channel_id=1, source_target_pairs={{0,1},{1,0},{2,3},{3,2},{4,5},{5,4},{6,7},{7,6},{8,9},{9,8},{10,11... | collective-permute-start | bytes 442376 | tf_op jit(solution)/shard_map/ppermute | solution.py:19
  23.6 6.3 %collective-permute-start.9 = (f32[32,6144]{1,0:T(8,128)}, f32[32,6144]{1,0:T(8,128)S(1)}, u32[]{:S(2)}, u32[]{:S(2)}) collective-permute-start(f32[32,6144]{1,0:T(8,128)} %get-tuple-element.69), channel_id=1, source_target_pairs={{0,4},{4,0},{8,12},{12,8},{16,20},{20,16},{24,28},{28,24},{1,5},{5... | collective-permute-start | bytes 2359304 | tf_op jit(solution)/shard_map/ppermute | solution.py:19
  23.7 6.3 %collective-permute-start.5 = (bf16[48,1536]{1,0:T(8,128)(2,1)S(1)}, bf16[48,1536]{1,0:T(8,128)(2,1)S(1)}, u32[]{:S(2)}, u32[]{:S(2)}) collective-permute-start(bf16[48,1536]{1,0:T(8,128)(2,1)S(1)} %collective-permute-done.1.refs_2_), channel_id=1, source_target_pairs={{0,2},{1,3},{2,0},{3,1},{4,6},{5,7},{6,4},{7,5},{8,10},{9,11},{10,... | collective-permute-start | bytes 442376 | tf_op jit(solution)/shard_map/ppermute | solution.py:19
  23.8 6.2 %collective-permute-start.4 = (bf16[48,1536]{1,0:T(8,128)(2,1)S(1)}, bf16[48,1536]{1,0:T(8,128)(2,1)S(1)}, u32[]{:S(2)}, u32[]{:S(2)}) collective-permute-start(bf16[48,1536]{1,0:T(8,128)(2,1)S(1)} %collective-permute-done.2.refs_3_), channel_id=1, source_target_pairs={{0,1},{1,0},{2,3},{3,2},{4,5},{5,4},{6,7},{7,6},{8,9},{9,8},{10,11... | collective-permute-start | bytes 442376 | tf_op jit(solution)/shard_map/ppermute | solution.py:19
  30.1 12.7 %collective-permute-start.14 = (f16[32,6144]{1,0:T(8,128)(2,1)S(1)}, f16[32,6144]{1,0:T(8,128)(2,1)S(1)}, u32[]{:S(2)}, u32[]{:S(2)}) collective-permute-start(f16[32,6144]{1,0:T(8,128)(2,1)S(1)} %add_convert_fusion), channel_id=1, source_target_pairs={{0,8},{4,12},{8,0},{12,4},{16,24},{20,28},{24,16},{28,20},{1,9},{5... | collective-permute-start | bytes 1179656 | tf_op jit(solution)/shard_map/ppermute | solution.py:19
  31.8 10.9 %collective-permute-start.13 = (bf16[48,1536]{1,0:T(8,128)(2,1)S(1)}, bf16[48,1536]{1,0:T(8,128)(2,1)S(1)}, u32[]{:S(2)}, u32[]{:S(2)}) collective-permute-start(bf16[48,1536]{1,0:T(8,128)(2,1)S(1)} %get-tuple-element.132), channel_id=1, source_target_pairs={{0,2},{1,3},{2,0},{3,1},{4,6},{5,7},{6,4},{7,5},{8,10},{9,11},{10,... | collective-permute-start | bytes 442376 | tf_op jit(solution)/shard_map/ppermute | solution.py:19
  32.9 9.8 %collective-permute-start.11 = (bf16[48,1536]{1,0:T(8,128)(2,1)S(1)}, bf16[48,1536]{1,0:T(8,128)(2,1)S(1)}, u32[]{:S(2)}, u32[]{:S(2)}) collective-permute-start(bf16[48,1536]{1,0:T(8,128)(2,1)S(1)} %get-tuple-element.132), channel_id=1, source_target_pairs={{0,1},{1,0},{2,3},{3,2},{4,5},{5,4},{6,7},{7,6},{8,9},{9,8},{10,11... | collective-permute-start | bytes 442376 | tf_op jit(solution)/shard_map/ppermute | solution.py:19
  33.2 9.5 %collective-permute-start.12 = (bf16[48,1536]{1,0:T(8,128)(2,1)S(1)}, bf16[48,1536]{1,0:T(8,128)(2,1)S(1)}, u32[]{:S(2)}, u32[]{:S(2)}) collective-permute-start(bf16[48,1536]{1,0:T(8,128)(2,1)S(1)} %get-tuple-element.133), channel_id=1, source_target_pairs={{0,2},{1,3},{2,0},{3,1},{4,6},{5,7},{6,4},{7,5},{8,10},{9,11},{10,... | collective-permute-start | bytes 442376 | tf_op jit(solution)/shard_map/ppermute | solution.py:19
  34.1 8.6 %collective-permute-start.10 = (bf16[48,1536]{1,0:T(8,128)(2,1)S(1)}, bf16[48,1536]{1,0:T(8,128)(2,1)S(1)}, u32[]{:S(2)}, u32[]{:S(2)}) collective-permute-start(bf16[48,1536]{1,0:T(8,128)(2,1)S(1)} %get-tuple-element.133), channel_id=1, source_target_pairs={{0,1},{1,0},{2,3},{3,2},{4,5},{5,4},{6,7},{7,6},{8,9},{9,8},{10,11... | collective-permute-start | bytes 442376 | tf_op jit(solution)/shard_map/ppermute | solution.py:19
  47.1 13.9 %collective-permute-start.16 = (f16[16,6144]{1,0:T(8,128)(2,1)S(1)}, f16[16,6144]{1,0:T(8,128)(2,1)S(1)}, u32[]{:S(2)}, u32[]{:S(2)}) collective-permute-start(f16[16,6144]{1,0:T(8,128)(2,1)S(1)} %get-tuple-element.131), channel_id=1, source_target_pairs={{0,16},{4,20},{8,24},{12,28},{16,0},{20,4},{24,8},{28,12},{1,17},{... | collective-permute-start | bytes 589832 | tf_op jit(solution)/shard_map/ppermute | solution.py:19
  47.6 13.4 %collective-permute-start.17 = (f16[16,6144]{1,0:T(8,128)(2,1)S(1)}, f16[16,6144]{1,0:T(8,128)(2,1)S(1)}, u32[]{:S(2)}, u32[]{:S(2)}) collective-permute-start(f16[16,6144]{1,0:T(8,128)(2,1)S(1)} %convert_element_type.42), channel_id=1, source_target_pairs={{0,8},{4,12},{8,0},{12,4},{16,24},{20,28},{24,16},{28,20},{1,9},{5... | collective-permute-start | bytes 589832 | tf_op jit(solution)/shard_map/ppermute | solution.py:19
  48.5 5.3 %collective-permute-start.19 = (bf16[48,1536]{1,0:T(8,128)(2,1)S(1)}, bf16[48,1536]{1,0:T(8,128)(2,1)S(1)}, u32[]{:S(2)}, u32[]{:S(2)}) collective-permute-start(bf16[48,1536]{1,0:T(8,128)(2,1)S(1)} %collective-permute-done.11.refs_2_), channel_id=1, source_target_pairs={{0,2},{1,3},{2,0},{3,1},{4,6},{5,7},{6,4},{7,5},{8,10},{9,11},{10,... | collective-permute-start | bytes 442376 | tf_op jit(solution)/shard_map/ppermute | solution.py:19
  49.1 5.1 %collective-permute-start.18 = (bf16[48,1536]{1,0:T(8,128)(2,1)S(1)}, bf16[48,1536]{1,0:T(8,128)(2,1)S(1)}, u32[]{:S(2)}, u32[]{:S(2)}) collective-permute-start(bf16[48,1536]{1,0:T(8,128)(2,1)S(1)} %collective-permute-done.12.refs_3_), channel_id=1, source_target_pairs={{0,1},{1,0},{2,3},{3,2},{4,5},{5,4},{6,7},{7,6},{8,9},{9,8},{10,11... | collective-permute-start | bytes 442376 | tf_op jit(solution)/shard_map/ppermute | solution.py:19
  62.3 12.4 %collective-permute-start.21 = (bf16[16,6144]{1,0:T(8,128)(2,1)S(1)}, bf16[16,6144]{1,0:T(8,128)(2,1)S(1)}, u32[]{:S(2)}, u32[]{:S(2)}) collective-permute-start(bf16[16,6144]{1,0:T(8,128)(2,1)S(1)} %fusion.9.refs_0_), channel_id=1, source_target_pairs={{0,16},{4,20},{8,24},{12,28},{16,0},{20,4},{24,8},{28,12},{1,17},{... | collective-permute-start | bytes 589832 | tf_op jit(solution)/shard_map/ppermute | solution.py:19
  62.9 11.8 %collective-permute-start.20 = (bf16[16,6144]{1,0:T(8,128)(2,1)S(1)}, bf16[16,6144]{1,0:T(8,128)(2,1)S(1)}, u32[]{:S(2)}, u32[]{:S(2)}) collective-permute-start(bf16[16,6144]{1,0:T(8,128)(2,1)S(1)} %fusion.9.refs_0_), channel_id=1, source_target_pairs={{0,8},{4,12},{8,0},{12,4},{16,24},{20,28},{24,16},{28,20},{1,9},{5... | collective-permute-start | bytes 589832 | tf_op jit(solution)/shard_map/ppermute | solution.py:19
  74.7 8.1 %collective-permute-start.23 = (bf16[16,6144]{1,0:T(8,128)(2,1)S(1)}, bf16[16,6144]{1,0:T(8,128)(2,1)S(1)}, u32[]{:S(2)}, u32[]{:S(2)}) collective-permute-start(bf16[16,6144]{1,0:T(8,128)(2,1)S(1)} %collective-permute-done.21.refs_2_), channel_id=1, source_target_pairs={{0,8},{4,12},{8,0},{12,4},{16,24},{20,28},{24,16},{28,20},{1,9},{5... | collective-permute-start | bytes 589832 | tf_op jit(solution)/shard_map/ppermute | solution.py:19
  74.7 8.1 %collective-permute-start.24 = (bf16[16,6144]{1,0:T(8,128)(2,1)S(1)}, bf16[16,6144]{1,0:T(8,128)(2,1)S(1)}, u32[]{:S(2)}, u32[]{:S(2)}) collective-permute-start(bf16[16,6144]{1,0:T(8,128)(2,1)S(1)} %fusion.9.refs_0_), channel_id=1, source_target_pairs={{0,4},{4,0},{8,12},{12,8},{16,20},{20,16},{24,28},{28,24},{1,5},{5... | collective-permute-start | bytes 589832 | tf_op jit(solution)/shard_map/ppermute | solution.py:19
  74.7 8.2 %collective-permute-start.25 = (bf16[16,6144]{1,0:T(8,128)(2,1)S(1)}, bf16[16,6144]{1,0:T(8,128)(2,1)S(1)}, u32[]{:S(2)}, u32[]{:S(2)}) collective-permute-start(bf16[16,6144]{1,0:T(8,128)(2,1)S(1)} %collective-permute-done.20.refs_1_), channel_id=1, source_target_pairs={{0,4},{4,0},{8,12},{12,8},{16,20},{20,16},{24,28},{28,24},{1,5},{5... | collective-permute-start | bytes 589832 | tf_op jit(solution)/shard_map/ppermute | solution.py:19
  75.2 7.7 %collective-permute-start.26 = (bf16[16,6144]{1,0:T(8,128)(2,1)S(1)}, bf16[16,6144]{1,0:T(8,128)(2,1)S(1)}, u32[]{:S(2)}, u32[]{:S(2)}) collective-permute-start(bf16[16,6144]{1,0:T(8,128)(2,1)S(1)} %collective-permute-done.21.refs_2_), channel_id=1, source_target_pairs={{0,4},{4,0},{8,12},{12,8},{16,20},{20,16},{24,28},{28,24},{1,5},{5... | collective-permute-start | bytes 589832 | tf_op jit(solution)/shard_map/ppermute | solution.py:19
  75.3 16.9 %collective-permute-start.31 = (f16[16,6144]{1,0:T(8,128)(2,1)S(1)}, f16[16,6144]{1,0:T(8,128)(2,1)S(1)}, u32[]{:S(2)}, u32[]{:S(2)}) collective-permute-start(f16[16,6144]{1,0:T(8,128)(2,1)S(1)} %get-tuple-element.129), channel_id=1, source_target_pairs={{0,16},{4,20},{8,24},{12,28},{16,0},{20,4},{24,8},{28,12},{1,17},{... | collective-permute-start | bytes 589832 | tf_op jit(solution)/shard_map/ppermute | solution.py:19
  82.8 9.3 %collective-permute-start.32 = (f16[16,6144]{1,0:T(8,128)(2,1)S(1)}, f16[16,6144]{1,0:T(8,128)(2,1)S(1)}, u32[]{:S(2)}, u32[]{:S(2)}) collective-permute-start(f16[16,6144]{1,0:T(8,128)(2,1)S(1)} %convert_element_type.48), channel_id=1, source_target_pairs={{0,8},{4,12},{8,0},{12,4},{16,24},{20,28},{24,16},{28,20},{1,9},{5... | collective-permute-start | bytes 589832 | tf_op jit(solution)/shard_map/ppermute | solution.py:19
  92.0 12.1 %collective-permute-start.28 = (bf16[1536,128]{1,0:T(8,128)(2,1)S(1)}, bf16[1536,128]{1,0:T(8,128)(2,1)S(1)}, u32[]{:S(2)}, u32[]{:S(2)}) collective-permute-start(bf16[1536,128]{1,0:T(8,128)(2,1)S(1)} %get-tuple-element.98), channel_id=1, source_target_pairs={{0,1},{1,0},{2,3},{3,2},{4,5},{5,4},{6,7},{7,6},{8,9},{9,8},{10,11... | collective-permute-start | bytes 1179656 | tf_op jit(solution)/shard_map/ppermute | solution.py:19
  92.1 12.0 %collective-permute-start.29 = (bf16[1536,128]{1,0:T(8,128)(2,1)}, bf16[1536,128]{1,0:T(8,128)(2,1)S(1)}, u32[]{:S(2)}, u32[]{:S(2)}) collective-permute-start(bf16[1536,128]{1,0:T(8,128)(2,1)} %get-tuple-element.99), channel_id=1, source_target_pairs={{0,2},{1,3},{2,0},{3,1},{4,6},{5,7},{6,4},{7,5},{8,10},{9,11},{10,... | collective-permute-start | bytes 1179656 | tf_op jit(solution)/shard_map/ppermute | solution.py:19
  92.3 11.8 %collective-permute-start.34 = (bf16[16,6144]{1,0:T(8,128)(2,1)S(1)}, bf16[16,6144]{1,0:T(8,128)(2,1)S(1)}, u32[]{:S(2)}, u32[]{:S(2)}) collective-permute-start(bf16[16,6144]{1,0:T(8,128)(2,1)S(1)} %fusion.2.refs_0_), channel_id=1, source_target_pairs={{0,16},{4,20},{8,24},{12,28},{16,0},{20,4},{24,8},{28,12},{1,17},{... | collective-permute-start | bytes 589832 | tf_op jit(solution)/shard_map/ppermute | solution.py:19
  92.9 12.7 %collective-permute-start.33 = (bf16[16,6144]{1,0:T(8,128)(2,1)S(1)}, bf16[16,6144]{1,0:T(8,128)(2,1)S(1)}, u32[]{:S(2)}, u32[]{:S(2)}) collective-permute-start(bf16[16,6144]{1,0:T(8,128)(2,1)S(1)} %fusion.2.refs_0_), channel_id=1, source_target_pairs={{0,8},{4,12},{8,0},{12,4},{16,24},{20,28},{24,16},{28,20},{1,9},{5... | collective-permute-start | bytes 589832 | tf_op jit(solution)/shard_map/ppermute | solution.py:19
  104.1 6.8 %collective-permute-start.35 = (bf16[16,6144]{1,0:T(8,128)(2,1)S(1)}, bf16[16,6144]{1,0:T(8,128)(2,1)S(1)}, u32[]{:S(2)}, u32[]{:S(2)}) collective-permute-start(bf16[16,6144]{1,0:T(8,128)(2,1)S(1)} %collective-permute-done.34.refs_2_), channel_id=1, source_target_pairs={{0,8},{4,12},{8,0},{12,4},{16,24},{20,28},{24,16},{28,20},{1,9},{5... | collective-permute-start | bytes 589832 | tf_op jit(solution)/shard_map/ppermute | solution.py:19
  104.1 16.2 %collective-permute-start.30 = (bf16[1536,128]{1,0:T(8,128)(2,1)S(1)}, bf16[1536,128]{1,0:T(8,128)(2,1)S(1)}, u32[]{:S(2)}, u32[]{:S(2)}) collective-permute-start(bf16[1536,128]{1,0:T(8,128)(2,1)S(1)} %copy-done.8), channel_id=1, source_target_pairs={{0,3},{1,2},{2,1},{3,0},{4,7},{5,6},{6,5},{7,4},{8,11},{9,10},{10,... | collective-permute-start | bytes 1179656 | tf_op jit(solution)/shard_map/ppermute | solution.py:19
  105.5 5.3 %collective-permute-start.36 = (bf16[16,6144]{1,0:T(8,128)(2,1)S(1)}, bf16[16,6144]{1,0:T(8,128)(2,1)S(1)}, u32[]{:S(2)}, u32[]{:S(2)}) collective-permute-start(bf16[16,6144]{1,0:T(8,128)(2,1)S(1)} %fusion.2.refs_0_), channel_id=1, source_target_pairs={{0,4},{4,0},{8,12},{12,8},{16,20},{20,16},{24,28},{28,24},{1,5},{5... | collective-permute-start | bytes 589832 | tf_op jit(solution)/shard_map/ppermute | solution.py:19
  105.6 5.3 %collective-permute-start.37 = (bf16[16,6144]{1,0:T(8,128)(2,1)S(1)}, bf16[16,6144]{1,0:T(8,128)(2,1)S(1)}, u32[]{:S(2)}, u32[]{:S(2)}) collective-permute-start(bf16[16,6144]{1,0:T(8,128)(2,1)S(1)} %collective-permute-done.33.refs_1_), channel_id=1, source_target_pairs={{0,4},{4,0},{8,12},{12,8},{16,20},{20,16},{24,28},{28,24},{1,5},{5... | collective-permute-start | bytes 589832 | tf_op jit(solution)/shard_map/ppermute | solution.py:19
  106.1 4.8 %collective-permute-start.38 = (bf16[16,6144]{1,0:T(8,128)(2,1)S(1)}, bf16[16,6144]{1,0:T(8,128)(2,1)S(1)}, u32[]{:S(2)}, u32[]{:S(2)}) collective-permute-start(bf16[16,6144]{1,0:T(8,128)(2,1)S(1)} %collective-permute-done.34.refs_2_), channel_id=1, source_target_pairs={{0,4},{4,0},{8,12},{12,8},{16,20},{20,16},{24,28},{28,24},{1,5},{5... | collective-permute-start | bytes 589832 | tf_op jit(solution)/shard_map/ppermute | solution.py:19
  120.3 12.1 %collective-permute-start.40 = (bf16[1536,128]{1,0:T(8,128)(2,1)S(1)}, bf16[1536,128]{1,0:T(8,128)(2,1)S(1)}, u32[]{:S(2)}, u32[]{:S(2)}) collective-permute-start(bf16[1536,128]{1,0:T(8,128)(2,1)S(1)} %get-tuple-element.109), channel_id=1, source_target_pairs={{0,1},{1,0},{2,3},{3,2},{4,5},{5,4},{6,7},{7,6},{8,9},{9,8},{10,11... | collective-permute-start | bytes 1179656 | tf_op jit(solution)/shard_map/ppermute | solution.py:19
  120.7 20.0 %collective-permute-start.41 = (bf16[1536,128]{1,0:T(8,128)(2,1)}, bf16[1536,128]{1,0:T(8,128)(2,1)S(1)}, u32[]{:S(2)}, u32[]{:S(2)}) collective-permute-start(bf16[1536,128]{1,0:T(8,128)(2,1)} %get-tuple-element.110), channel_id=1, source_target_pairs={{0,2},{1,3},{2,0},{3,1},{4,6},{5,7},{6,4},{7,5},{8,10},{9,11},{10,... | collective-permute-start | bytes 1179656 | tf_op jit(solution)/shard_map/ppermute | solution.py:19
  120.7 20.0 %collective-permute-start.42 = (bf16[1536,128]{1,0:T(8,128)(2,1)}, bf16[1536,128]{1,0:T(8,128)(2,1)S(1)}, u32[]{:S(2)}, u32[]{:S(2)}) collective-permute-start(bf16[1536,128]{1,0:T(8,128)(2,1)} %get-tuple-element.111), channel_id=1, source_target_pairs={{0,3},{1,2},{2,1},{3,0},{4,7},{5,6},{6,5},{7,4},{8,11},{9,10},{10,... | collective-permute-start | bytes 1179656 | tf_op jit(solution)/shard_map/ppermute | solution.py:19
  132.4 4.8 %collective-permute-start.45 = (f32[64,128]{1,0:T(8,128)S(1)}, f32[64,128]{1,0:T(8,128)S(1)}, u32[]{:S(2)}, u32[]{:S(2)}) collective-permute-start(f32[64,128]{1,0:T(8,128)S(1)} %add.137), channel_id=1, source_target_pairs={{0,16},{4,20},{8,24},{12,28},{16,0},{20,4},{24,8},{28,12},{1,17},{... | collective-permute-start | bytes 98312 | tf_op jit(solution)/shard_map/ppermute | solution.py:19
  137.2 6.5 %collective-permute-start.51 = (f32[64,128]{1,0:T(8,128)S(1)}, f32[64,128]{1,0:T(8,128)S(1)}, u32[]{:S(2)}, u32[]{:S(2)}) collective-permute-start(f32[64,128]{1,0:T(8,128)S(1)} %add.138), channel_id=1, source_target_pairs={{0,3},{1,2},{2,1},{3,0},{4,7},{5,6},{6,5},{7,4},{8,11},{9,10},{10,... | collective-permute-start | bytes 98312 | tf_op jit(solution)/shard_map/ppermute | solution.py:19
  137.3 6.5 %collective-permute-start.50 = (f32[64,128]{1,0:T(8,128)S(1)}, f32[64,128]{1,0:T(8,128)S(1)}, u32[]{:S(2)}, u32[]{:S(2)}) collective-permute-start(f32[64,128]{1,0:T(8,128)S(1)} %add.138), channel_id=1, source_target_pairs={{0,2},{1,3},{2,0},{3,1},{4,6},{5,7},{6,4},{7,5},{8,10},{9,11},{10,... | collective-permute-start | bytes 98312 | tf_op jit(solution)/shard_map/ppermute | solution.py:19
  139.0 4.8 %collective-permute-start.49 = (f32[64,128]{1,0:T(8,128)S(1)}, f32[64,128]{1,0:T(8,128)S(1)}, u32[]{:S(2)}, u32[]{:S(2)}) collective-permute-start(f32[64,128]{1,0:T(8,128)S(1)} %add.138), channel_id=1, source_target_pairs={{0,1},{1,0},{2,3},{3,2},{4,5},{5,4},{6,7},{7,6},{8,9},{9,8},{10,11... | collective-permute-start | bytes 98312 | tf_op jit(solution)/shard_map/ppermute | solution.py:19
  145.0 4.3 %collective-permute-start.47 = (f32[128,128]{1,0:T(8,128)S(1)}, f32[128,128]{1,0:T(8,128)S(1)}, u32[]{:S(2)}, u32[]{:S(2)}) collective-permute-start(f32[128,128]{1,0:T(8,128)S(1)} %dynamic-slice_add_fusion), channel_id=1, source_target_pairs={{0,8},{4,12},{8,0},{12,4},{16,24},{20,28},{24,16},{28,20},{1,9},{5... | collective-permute-start | bytes 196616 | tf_op jit(solution)/shard_map/ppermute | solution.py:19
  145.1 4.3 %collective-permute-start.52 = (f32[64,128]{1,0:T(8,128)S(1)}, f32[64,128]{1,0:T(8,128)S(1)}, u32[]{:S(2)}, u32[]{:S(2)}) collective-permute-start(f32[64,128]{1,0:T(8,128)S(1)} %add_bitcast_fusion.1), channel_id=1, source_target_pairs={{0,4},{4,0},{8,12},{12,8},{16,20},{20,16},{24,28},{28,24},{1,5},{5... | collective-permute-start | bytes 98312 | tf_op jit(solution)/shard_map/ppermute | solution.py:19
  149.4 5.5 %collective-permute-start.48 = (f32[128,128]{1,0:T(8,128)S(1)}, f32[128,128]{1,0:T(8,128)S(1)}, u32[]{:S(2)}, u32[]{:S(2)}) collective-permute-start(f32[128,128]{1,0:T(8,128)S(1)} %add.142), channel_id=1, source_target_pairs={{0,16},{4,20},{8,24},{12,28},{16,0},{20,4},{24,8},{28,12},{1,17},{... | collective-permute-start | bytes 196616 | tf_op jit(solution)/shard_map/ppermute | solution.py:19
  154.9 5.3 %collective-permute-start.55 = (f32[128,128]{1,0:T(8,128)S(1)}, f32[128,128]{1,0:T(8,128)S(1)}, u32[]{:S(2)}, u32[]{:S(2)}) collective-permute-start(f32[128,128]{1,0:T(8,128)S(1)} %add.151), channel_id=1, source_target_pairs={{0,3},{1,2},{2,1},{3,0},{4,7},{5,6},{6,5},{7,4},{8,11},{9,10},{10,... | collective-permute-start | bytes 196616 | tf_op jit(solution)/shard_map/ppermute | solution.py:19
  156.0 4.9 %collective-permute-start.54 = (f32[128,128]{1,0:T(8,128)S(1)}, f32[128,128]{1,0:T(8,128)S(1)}, u32[]{:S(2)}, u32[]{:S(2)}) collective-permute-start(f32[128,128]{1,0:T(8,128)S(1)} %add.151), channel_id=1, source_target_pairs={{0,2},{1,3},{2,0},{3,1},{4,6},{5,7},{6,4},{7,5},{8,10},{9,11},{10,... | collective-permute-start | bytes 196616 | tf_op jit(solution)/shard_map/ppermute | solution.py:19
  (19 other events, 100.9 us)

commit v4 on v3

--- a/solution.py
+++ b/solution.py
@@ -27,8 +27,32 @@
             pltpu.make_async_copy(tiles_ref.at[slot], tile_buf.at[slot], sems.at[slot]).start()
 
 
-def wait_tile(slot, tiles_ref, tile_buf, sems):
-    pltpu.make_async_copy(tiles_ref.at[slot], tile_buf.at[slot], sems.at[slot]).wait()
+def for_each_tile(layout_ref, tiles_ref, tile_buf, sems, multiply, add, forward=False):
+    slots = tiles_ref.shape[0]
+    count = layout_ref[0]
+
+    def wait(slot):
+        pltpu.make_async_copy(tiles_ref.at[slot], tile_buf.at[slot], sems.at[slot]).wait()
+
+    def step(pair, carry):
+        slot = 2 * pair
+        other = jnp.minimum(slot + 1, slots - 1)
+        paired = slot + 1 < count
+        wait(slot)
+
+        @pl.when(paired)
+        def _():
+            wait(other)
+
+        ends = [(layout_ref[1 + s], layout_ref[1 + slots + s]) for s in (slot, other)]
+        (source, target), (other_source, other_target) = [end[::-1] if forward else end for end in ends]
+        value = multiply(slot, source)
+        other_value = multiply(other, other_source)
+        add(target, value)
+        add(other_target, jnp.where(paired, other_value, 0.0))
+        return carry
+
+    lax.fori_loop(0, (count + 1) // 2, step, 0)
 
 
 def prepare_kernel(sketch_ref, *refs):
@@ -51,9 +75,9 @@
                 copy(half_ref, which_core * (places - 1) + offset, half, which_core, offset)
 
 
-def transposed_kernel(places, count_ref, rows_ref, cols_ref, tiles_ref, *refs):
+def transposed_kernel(places, layout_ref, tiles_ref, *refs):
     *out_refs, sketch_buf, tile_buf, sems = refs[len(places) :]
-    count = count_ref[0, 0]
+    count = layout_ref[0]
     fetch_tiles(count, tiles_ref, tile_buf, sems)
     col_index = lax.axis_index("col")
     tile_size = tiles_ref.shape[1]
@@ -66,23 +90,23 @@
     for out_ref in out_refs:
         out_ref[...] = jnp.zeros_like(out_ref)
 
-    def step(slot, carry):
-        wait_tile(slot, tiles_ref, tile_buf, sems)
-        block = sketch_buf[:, pl.ds(pl.multiple_of(rows_ref[0, 0, slot] * tile_size, 128), tile_size)]
-        product = jnp.dot(block, tile_buf[slot], preferred_element_type=jnp.float32)
-        lanes = pl.ds(pl.multiple_of(cols_ref[0, 0, slot] * tile_size, 128), tile_size)
+    def multiply(slot, row):
+        block = sketch_buf[:, pl.ds(pl.multiple_of(row * tile_size, 128), tile_size)]
+        return jnp.dot(block, tile_buf[slot], preferred_element_type=jnp.float32)
+
+    def add(col, value):
+        lanes = pl.ds(pl.multiple_of(col * tile_size, 128), tile_size)
         depth = out_refs[0].shape[0]
         for i, out_ref in enumerate(out_refs):
-            out_ref[:, lanes] += product[depth * i : depth * (i + 1)]
-        return carry
-
-    lax.fori_loop(0, count, step, 0)
-
-
-def forward_kernel(outs, count_ref, rows_ref, cols_ref, tiles_ref, *refs):
+            out_ref[:, lanes] += value[depth * i : depth * (i + 1)]
+
+    for_each_tile(layout_ref, tiles_ref, tile_buf, sems, multiply, add)
+
+
+def forward_kernel(outs, layout_ref, tiles_ref, *refs):
     column_buf, total, tile_buf, sems = refs[-4:]
     pieces, out_refs = refs[: -4 - outs], refs[-4 - outs : -4]
-    count = count_ref[0, 0]
+    count = layout_ref[0]
     fetch_tiles(count, tiles_ref, tile_buf, sems)
     row_index, col_index = lax.axis_index("row"), lax.axis_index("col")
     tile_size = tiles_ref.shape[1]
@@ -96,16 +120,16 @@
             column_buf[...] = piece[...]
     total[...] = jnp.zeros_like(total)
 
-    def step(slot, carry):
-        wait_tile(slot, tiles_ref, tile_buf, sems)
-        block = column_buf[:, pl.ds(pl.multiple_of(cols_ref[0, 0, slot] * tile_size, 128), tile_size)]
-        product = lax.dot_general(
+    def multiply(slot, col):
+        block = column_buf[:, pl.ds(pl.multiple_of(col * tile_size, 128), tile_size)]
+        return lax.dot_general(
             tile_buf[slot], block, (((1,), (1,)), ((), ())), preferred_element_type=jnp.float32
         )
-        total[pl.ds(pl.multiple_of(rows_ref[0, 0, slot] * tile_size, 128), tile_size), :] += product
-        return carry
-
-    lax.fori_loop(0, count, step, 0)
+
+    def add(row, value):
+        total[pl.ds(pl.multiple_of(row * tile_size, 128), tile_size), :] += value
+
+    for_each_tile(layout_ref, tiles_ref, tile_buf, sems, multiply, add, forward=True)
     for offset, out_ref in enumerate(out_refs):
         width = out_ref.shape[0]
         if outs == 1:
@@ -115,14 +139,14 @@
             out_ref[...] = total[pl.ds(start, width), :].astype(out_ref.dtype)
 
 
-def tile_call(kernel, out_shape, scratch, counts, rows, cols, tiles, pieces):
+def tile_call(kernel, out_shape, scratch, layout, tiles, pieces):
     slots, tile_size, _ = tiles.shape
     smem = pl.BlockSpec(memory_space=pltpu.SMEM)
     vmem = pl.BlockSpec(memory_space=pltpu.VMEM)
     return pl.pallas_call(
         kernel,
         out_shape=out_shape,
-        in_specs=[smem, smem, smem, pl.BlockSpec(memory_space=pl.ANY)] + [vmem] * len(pieces),
+        in_specs=[smem, pl.BlockSpec(memory_space=pl.ANY)] + [vmem] * len(pieces),
         out_specs=jax.tree.map(lambda _: vmem, out_shape),
         scratch_shapes=scratch
         + [
@@ -131,7 +155,7 @@
         ],
         compiler_params=pltpu.CompilerParams(vmem_limit_bytes=VMEM_LIMIT),
         cost_estimate=NO_COST,
-    )(counts, rows, cols, tiles, *pieces)
+    )(layout, tiles, *pieces)
 
 
 def after(value, token):
@@ -228,7 +252,7 @@
     mine, other = call_transposed(pieces, None)
     arrived = swap(after(other, a.near), "row", 1)
     a.gather_far()
-    b.shard = after(b.shard, [piece[2] for piece in a.pieces[5:]])
+    b.shard = after(b.shard, a.near)
     b.gather_near()
     sent = half(mine + arrived)
     far = swap(sent, "row", 2)
@@ -368,6 +392,7 @@
 
 def body(tiles, tile_rows, tile_cols, tile_counts, sketch):
     tiles = tiles[0, 0]
+    layout = jnp.concatenate([tile_counts[0], tile_rows[0, 0], tile_cols[0, 0]])
     slots, tile_size, _ = tiles.shape
     width, sketch_width = sketch.shape
     group_rows, group_cols = BR * tile_size, BC * tile_size
@@ -381,7 +406,7 @@
             functools.partial(transposed_kernel, [piece[:2] for piece in pieces]),
             [jax.ShapeDtypeStruct((depth // outs, group_cols), jnp.float32)] * outs,
             [pltpu.VMEM((depth, group_rows), jnp.bfloat16)],
-            tile_counts, tile_rows, tile_cols, tiles, after([piece[2] for piece in pieces], token),
+            layout, tiles, after([piece[2] for piece in pieces], token),
         )
 
     def call_forward(columns, outs=cols_axis):
@@ -393,7 +418,7 @@
                 for offset in range(outs)
             ],
             [pltpu.VMEM((depth, group_cols), jnp.bfloat16), pltpu.VMEM((group_rows, depth), jnp.float32)],
-            tile_counts, tile_rows, tile_cols, tiles, columns,
+            layout, tiles, columns,
         )
 
     paired = rows_axis == 8 and cols_axis == 4 and sketch_width == 2 * GROUP * rows_axis

time: 172 us -> 166 us (0.965)
  waiting for transfers between devices: 70.1 us -> 64.7 us
  Pallas kernels: 52.8 us -> 48.5 us
  starting transfers between devices: 41.1 us -> 45.1 us
    ppermute x57, waiting for transfers between devices: 70.1 us -> 64.7 us  [swap(): return lax.ppermute(value, axis, [(i, i ^ offset) for i in range(size)])]
    pallas_call x5, Pallas kernels: 35.2 us -> 30.9 us  [tile_call(): pl.pallas_call(kernel, out_shape=out_shape, in_specs=[smem, pl.BlockSpec(...]
    ppermute x57, starting transfers between devices: 41.1 us -> 45.1 us  [swap(): return lax.ppermute(value, axis, [(i, i ^ offset) for i in range(size)])]
  transfers between devices with their start and end apart: 57 -> 57, of which waited for: 24 -> 25; matrix products, arithmetic and copies ran while one was open for 1% -> 1% of each run, Pallas kernels for 26% -> 25%
where the time goes in v4:
time: 166 us; the launch traced here: 165 us
  waiting for transfers between devices  64.7 us (39%)
  Pallas kernels  48.5 us (29%)
  starting transfers between devices  45.1 us (27%)
  other arithmetic  3 us (2%)
  local copies, waits for them, and re-layouts  2.08 us (1%)
  between operations  1.79 us (1%)
    ppermute x57, waiting for transfers between devices, swap(): return lax.ppermute(value, axis, [(i, i ^ offset) for i in range(size)])  64.7 us
    ppermute x57, starting transfers between devices, swap(): return lax.ppermute(value, axis, [(i, i ^ offset) for i in range(size)])  45.1 us
    pallas_call x5, Pallas kernels, tile_call(): pl.pallas_call(kernel, out_shape=out_shape, in_specs=[smem, pl.BlockSpec(...  30.9 us
    pallas_call x1, Pallas kernels, body(): pl.pallas_call(functools.partial(second_factor_kernel, total_rows), out_s...  7.39 us
    pallas_call x2, Pallas kernels, finish_call(): pl.pallas_call(functools.partial(finish_kernel, len(parts)), out_shape=(j...  4.98 us
    pallas_call x1, Pallas kernels, body(): pl.pallas_call(functools.partial(first_factor_kernel, total_rows), out_sh...  4.88 us
  transfers between devices with their start and end apart: 57, of which 25 were waited for; matrix products, arithmetic and copies ran while one was open for 1% of the time, Pallas kernels for 25%

profile of v4, /device:TPU:0, one launch (start us, length us, event | category | flops | bytes accessed | tf_op | source)
XLA Modules:
  0.0 165.2 jit_solution(3808770033235053804)
XLA Ops:
  0.6 1.1 copy-done.3
  2.1 4.0 %collective-permute-start.8 = (bf16[64,1536]{1,0:T(8,128)(2,1)S(1)}, bf16[64,1536]{1,0:T(8,128)(2,1)S(1)}, u32[]{:S(2)}, u32[]{:S(2)}) collective-permute-start(bf16[64,1536]{1,0:T(8,128)(2,1)S(1)} %get-tuple-element.66.refs_0_), channel_id=1, source_target_pairs={{0,3},{1,2},{2,1},{3,0},{4,7},{5,6},{6,5},{7,4},{8,11},{9,10},{10,... | collective-permute-start | bytes 589832 | tf_op jit(solution)/shard_map/ppermute | solution.py:19
  6.7 2.0 %collective-permute-start.3 = (bf16[48,1536]{1,0:T(8,128)(2,1)S(1)}, bf16[48,1536]{1,0:T(8,128)(2,1)S(1)}, u32[]{:S(2)}, u32[]{:S(2)}) collective-permute-start(bf16[48,1536]{1,0:T(8,128)(2,1)S(1)} %get-tuple-element.134), channel_id=1, source_target_pairs={{0,2},{1,3},{2,0},{3,1},{4,6},{5,7},{6,4},{7,5},{8,10},{9,11},{10,... | collective-permute-start | bytes 442376 | tf_op jit(solution)/shard_map/ppermute | solution.py:19
  8.7 1.5 collective-permute-start.1
  10.2 1.6 collective-permute-done.8.refs_3_
  11.8 2.0 %collective-permute-start.2 = (bf16[48,1536]{1,0:T(8,128)(2,1)S(1)}, bf16[48,1536]{1,0:T(8,128)(2,1)S(1)}, u32[]{:S(2)}, u32[]{:S(2)}) collective-permute-start(bf16[48,1536]{1,0:T(8,128)(2,1)S(1)} %get-tuple-element.135), channel_id=1, source_target_pairs={{0,2},{1,3},{2,0},{3,1},{4,6},{5,7},{6,4},{7,5},{8,10},{9,11},{10,... | collective-permute-start | bytes 442376 | tf_op jit(solution)/shard_map/ppermute | solution.py:19
  13.8 1.4 collective-permute-done.7.refs_2_
  15.3 1.7 %collective-permute-start = (bf16[48,1536]{1,0:T(8,128)(2,1)S(1)}, bf16[48,1536]{1,0:T(8,128)(2,1)S(1)}, u32[]{:S(2)}, u32[]{:S(2)}) collective-permute-start(bf16[48,1536]{1,0:T(8,128)(2,1)S(1)} %get-tuple-element.135), channel_id=1, source_target_pairs={{0,1},{1,0},{2,3},{3,2},{4,5},{5,4},{6,7},{7,6},{8,9},{9,8},{10,11... | collective-permute-start | bytes 442376 | tf_op jit(solution)/shard_map/ppermute | solution.py:19
  17.7 5.3 %shard_map.69 = (f32[32,6144]{1,0:T(8,128)S(1)}, f32[32,6144]{1,0:T(8,128)}) custom-call(s32[33]{0:T(128)S(1)} %pad_add_fusion.layout_ref, bf16[16,512,512]{2,1,0:T(8,128)(2,1)} %bitcast.17, bf16[64,1536]{1,0:T(8,128)(2,1)S(1)} %get-tuple-element.66.refs_0_, bf16[64,1536]{1,0:T(8,128)(2,1)S(1)} %collective-permute-done.6.refs_1_, ...), custom_call_target="tpu_custom_call" | custom-call | tf_op jit(solution)/shard_map/pallas_call | solution.py:146
  24.4 1.1 collective-permute-done.9
  25.6 1.6 collective-permute-start.14
  30.3 1.2 collective-permute-start.10
  31.4 5.9 %shard_map.70 = (f32[48,6144]{1,0:T(8,128)}, f32[48,6144]{1,0:T(8,128)}) custom-call(s32[33]{0:T(128)S(1)} %pad_add_fusion.layout_ref, bf16[16,512,512]{2,1,0:T(8,128)(2,1)} %bitcast.18, bf16[96,1536]{1,0:T(8,128)(2,1)S(1)} %get-tuple-element.70.refs_0_, bf16[48,1536]{1,0:T(8,128)(2,1)S(1)} %collective-permute-done.refs_1_, ...), custom_call_target="tpu_custom_call" | custom-call | tf_op jit(solution)/shard_map/pallas_call | solution.py:146
  37.4 3.0 %collective-permute-done.15 = f32[48,6144]{1,0:T(8,128)S(1)} collective-permute-done((f32[48,6144]{1,0:T(8,128)}, f32[48,6144]{1,0:T(8,128)S(1)}, u32[]{:S(2)}, u32[]{:S(2)}) %collective-permute-start.15) | collective-permute-done | bytes 1179680 | tf_op jit(solution)/shard_map/ppermute | solution.py:19
  40.5 1.3 slice_add_fusion.3
  41.7 2.9 %collective-permute-start.16 = (f16[16,6144]{1,0:T(8,128)(2,1)S(1)}, f16[16,6144]{1,0:T(8,128)(2,1)S(1)}, u32[]{:S(2)}, u32[]{:S(2)}) collective-permute-start(f16[16,6144]{1,0:T(8,128)(2,1)S(1)} %get-tuple-element.131), channel_id=1, source_target_pairs={{0,16},{4,20},{8,24},{12,28},{16,0},{20,4},{24,8},{28,12},{1,17},{... | collective-permute-start | bytes 589832 | tf_op jit(solution)/shard_map/ppermute | solution.py:19
  45.0 1.5 collective-permute-start.19
  46.8 3.6 %collective-permute-done.19.refs_6_ = bf16[48,1536]{1,0:T(8,128)(2,1)S(1)} collective-permute-done((bf16[48,1536]{1,0:T(8,128)(2,1)S(1)}, bf16[48,1536]{1,0:T(8,128)(2,1)S(1)}, u32[]{:S(2)}, u32[]{:S(2)}) %collective-permute-start.19) | collective-permute-done | bytes 147488 | tf_op jit(solution)/shard_map/ppermute | solution.py:19
  50.4 1.2 collective-permute-done.18.refs_5_
  51.6 5.8 %shard_map.71 = (f32[48,6144]{1,0:T(8,128)}, f32[48,6144]{1,0:T(8,128)}) custom-call(s32[33]{0:T(128)S(1)} %pad_add_fusion.layout_ref, bf16[16,512,512]{2,1,0:T(8,128)(2,1)} %bitcast.19, bf16[96,1536]{1,0:T(8,128)(2,1)S(1)} %get-tuple-element.83.refs_0_, bf16[48,1536]{1,0:T(8,128)(2,1)S(1)} %collective-permute-done.10.refs_1_, ...), custom_call_target="tpu_custom_call" | custom-call | tf_op jit(solution)/shard_map/pallas_call | solution.py:146
  57.5 1.2 fusion.9.refs_0_
  60.7 10.4 %collective-permute-done.21.refs_2_ = bf16[16,6144]{1,0:T(8,128)(2,1)S(1)} collective-permute-done((bf16[16,6144]{1,0:T(8,128)(2,1)S(1)}, bf16[16,6144]{1,0:T(8,128)(2,1)S(1)}, u32[]{:S(2)}, u32[]{:S(2)}) %collective-permute-start.21) | collective-permute-done | bytes 196640 | tf_op jit(solution)/shard_map/ppermute | solution.py:19
  71.7 1.1 collective-permute-start.31
  72.8 6.4 %collective-permute-done.23.refs_3_ = bf16[16,6144]{1,0:T(8,128)(2,1)S(1)} collective-permute-done((bf16[16,6144]{1,0:T(8,128)(2,1)S(1)}, bf16[16,6144]{1,0:T(8,128)(2,1)S(1)}, u32[]{:S(2)}, u32[]{:S(2)}) %collective-permute-start.23) | collective-permute-done | bytes 196640 | tf_op jit(solution)/shard_map/ppermute | solution.py:19
  79.4 1.3 collective-permute-done.27.refs_7_
  80.7 6.9 %shard_map.72 = (f32[1536,128]{1,0:T(8,128)}, bf16[1536,128]{1,0:T(8,128)(2,1)S(1)}, bf16[1536,128]{1,0:T(8,128)(2,1)}, bf16[1536,128]{1,0:T(8,128)(2,1)}) custom-call(s32[33]{0:T(128)S(1)} %pad_add_fusion.layout_ref, bf16[16,512,512]{2,1,0:T(8,128)(2,1)} %bitcast.20, bf16[16,6144]{1,0:T(8,128)(2,1)S(1)} %fusion.9.refs_0_, ...), custom_call_target="tpu_custom_call" | custom-call | tf_op jit(solution)/shard_map/pallas_call | solution.py:146
  88.4 1.2 collective-permute-start.34
  90.5 9.1 %collective-permute-done.34.refs_2_ = bf16[16,6144]{1,0:T(8,128)(2,1)S(1)} collective-permute-done((bf16[16,6144]{1,0:T(8,128)(2,1)S(1)}, bf16[16,6144]{1,0:T(8,128)(2,1)S(1)}, u32[]{:S(2)}, u32[]{:S(2)}) %collective-permute-start.34) | collective-permute-done | bytes 196640 | tf_op jit(solution)/shard_map/ppermute | solution.py:19
  99.7 2.0 %collective-permute-start.30 = (bf16[1536,128]{1,0:T(8,128)(2,1)S(1)}, bf16[1536,128]{1,0:T(8,128)(2,1)S(1)}, u32[]{:S(2)}, u32[]{:S(2)}) collective-permute-start(bf16[1536,128]{1,0:T(8,128)(2,1)S(1)} %copy-done.8), channel_id=1, source_target_pairs={{0,3},{1,2},{2,1},{3,0},{4,7},{5,6},{6,5},{7,4},{8,11},{9,10},{10,... | collective-permute-start | bytes 1179656 | tf_op jit(solution)/shard_map/ppermute | solution.py:19
  102.2 4.2 %collective-permute-done.35.refs_3_ = bf16[16,6144]{1,0:T(8,128)(2,1)S(1)} collective-permute-done((bf16[16,6144]{1,0:T(8,128)(2,1)S(1)}, bf16[16,6144]{1,0:T(8,128)(2,1)S(1)}, u32[]{:S(2)}, u32[]{:S(2)}) %collective-permute-start.35) | collective-permute-done | bytes 196640 | tf_op jit(solution)/shard_map/ppermute | solution.py:19
  106.5 1.4 collective-permute-done.39.refs_7_
  107.9 7.1 %shard_map.73 = (f32[1536,128]{1,0:T(8,128)}, bf16[1536,128]{1,0:T(8,128)(2,1)S(1)}, bf16[1536,128]{1,0:T(8,128)(2,1)}, bf16[1536,128]{1,0:T(8,128)(2,1)}) custom-call(s32[33]{0:T(128)S(1)} %pad_add_fusion.layout_ref, bf16[16,512,512]{2,1,0:T(8,128)(2,1)} %bitcast.21, bf16[16,6144]{1,0:T(8,128)(2,1)S(1)} %fusion.2.refs_0_, ...), custom_call_target="tpu_custom_call" | custom-call | tf_op jit(solution)/shard_map/pallas_call | solution.py:146
  115.9 2.6 %collective-permute-start.42 = (bf16[1536,128]{1,0:T(8,128)(2,1)}, bf16[1536,128]{1,0:T(8,128)(2,1)S(1)}, u32[]{:S(2)}, u32[]{:S(2)}) collective-permute-start(bf16[1536,128]{1,0:T(8,128)(2,1)} %get-tuple-element.111), channel_id=1, source_target_pairs={{0,3},{1,2},{2,1},{3,0},{4,7},{5,6},{6,5},{7,4},{8,11},{9,10},{10,... | collective-permute-start | bytes 1179656 | tf_op jit(solution)/shard_map/ppermute | solution.py:19
  118.6 2.0 %shard_map.74 = (f32[1536,128]{1,0:T(8,128)S(1)}, f32[128,128]{1,0:T(8,128)S(1)}) custom-call(f32[1536,128]{1,0:T(8,128)} %get-tuple-element.97.refs_0_, bf16[1536,128]{1,0:T(8,128)(2,1)S(1)} %collective-permute-done.28.refs_1_, bf16[1536,128]{1,0:T(8,128)(2,1)S(1)} %collective-permute-done.29.refs_2_, bf16[1536,128]{1,0:T(8,128)(2,1)S(1)} %collective-permute-done.30.refs_3_), custom_call_target="tpu_custom_call" | custom-call | tf_op jit(solution)/shard_map/pallas_call | solution.py:238
  121.5 1.2 collective-permute-done.43
  123.0 3.6 %collective-permute-done.44 = f32[64,128]{1,0:T(8,128)S(1)} collective-permute-done((f32[64,128]{1,0:T(8,128)S(1)}, f32[64,128]{1,0:T(8,128)S(1)}, u32[]{:S(2)}, u32[]{:S(2)}) %collective-permute-start.44) | collective-permute-done | bytes 32800 | tf_op jit(solution)/shard_map/ppermute | solution.py:19
  128.0 4.0 %collective-permute-done.45 = f32[64,128]{1,0:T(8,128)S(1)} collective-permute-done((f32[64,128]{1,0:T(8,128)S(1)}, f32[64,128]{1,0:T(8,128)S(1)}, u32[]{:S(2)}, u32[]{:S(2)}) %collective-permute-start.45) | collective-permute-done | bytes 32800 | tf_op jit(solution)/shard_map/ppermute | solution.py:19
  132.3 1.9 %collective-permute-start.50 = (f32[64,128]{1,0:T(8,128)S(1)}, f32[64,128]{1,0:T(8,128)S(1)}, u32[]{:S(2)}, u32[]{:S(2)}) collective-permute-start(f32[64,128]{1,0:T(8,128)S(1)} %add.138), channel_id=1, source_target_pairs={{0,2},{1,3},{2,0},{3,1},{4,6},{5,7},{6,4},{7,5},{8,10},{9,11},{10,... | collective-permute-start | bytes 98312 | tf_op jit(solution)/shard_map/ppermute | solution.py:19
  134.2 1.3 collective-permute-start.49
  135.5 2.9 %shard_map.75 = (f32[1536,128]{1,0:T(8,128)}, f32[256,128]{1,0:T(8,128)S(1)}) custom-call(f32[1536,128]{1,0:T(8,128)} %copy-done, f32[1536,128]{1,0:T(8,128)} %get-tuple-element.116.refs_1_, bf16[1536,128]{1,0:T(8,128)(2,1)S(1)} %collective-permute-done.40.refs_2_, bf16[1536,128]{1,0:T(8,128)(2,1)S(1)} %collective-permute-done.41.refs_3_, ...), custom_call_target="tpu_custom_call" | custom-call | tf_op jit(solution)/shard_map/pallas_call | solution.py:238
  138.6 1.2 collective-permute-done.46
  140.4 3.7 %collective-permute-done.47 = f32[128,128]{1,0:T(8,128)S(1)} collective-permute-done((f32[128,128]{1,0:T(8,128)S(1)}, f32[128,128]{1,0:T(8,128)S(1)}, u32[]{:S(2)}, u32[]{:S(2)}) %collective-permute-start.47) | collective-permute-done | bytes 65568 | tf_op jit(solution)/shard_map/ppermute | solution.py:19
  145.1 4.9 %shard_map.76 = (f32[128,128]{1,0:T(8,128)S(1)}, f32[128,128]{1,0:T(8,128)S(1)}, f32[1536,128]{1,0:T(8,128)S(1)}) custom-call(f32[128,128]{1,0:T(8,128)S(1)} %maximum_select_fusion.1.gram_ref, f32[1536,128]{1,0:T(8,128)S(1)} %copy-done.1), custom_call_target="tpu_custom_call" | custom-call | tf_op jit(solution)/shard_map/pallas_call | solution.py:455
  150.0 1.4 collective-permute-start.55
  152.1 1.5 collective-permute-start.53
  153.6 1.7 %collective-permute-done.55 = f32[128,128]{1,0:T(8,128)S(1)} collective-permute-done((f32[128,128]{1,0:T(8,128)S(1)}, f32[128,128]{1,0:T(8,128)S(1)}, u32[]{:S(2)}, u32[]{:S(2)}) %collective-permute-start.55) | collective-permute-done | bytes 65568 | tf_op jit(solution)/shard_map/ppermute | solution.py:19
  156.5 1.2 collective-permute-done.56
  157.8 7.4 %shard_map.77 = (f32[1536,256]{1,0:T(8,128)}, f32[256,256]{1,0:T(8,128)}) custom-call(f32[256,128]{1,0:T(8,128)S(1)} %maximum_select_fusion.gram_ref, f32[128,128]{1,0:T(8,128)S(1)} %get-tuple-element.123.upper_ref, f32[128,128]{1,0:T(8,128)S(1)} %get-tuple-element.125.inverse_ref, f32[1536,128]{1,0:T(8,128)S(1)} %get-tuple-element.126.first_ref, ...), custom_call_target="tpu_custom_call" | custom-call | tf_op jit(solution)/shard_map/pallas_call | solution.py:462
  (120 shorter events, 18.8 us)
Async XLA Ops:
  2.1 9.7 %collective-permute-start.8 = (bf16[64,1536]{1,0:T(8,128)(2,1)S(1)}, bf16[64,1536]{1,0:T(8,128)(2,1)S(1)}, u32[]{:S(2)}, u32[]{:S(2)}) collective-permute-start(bf16[64,1536]{1,0:T(8,128)(2,1)S(1)} %get-tuple-element.66.refs_0_), channel_id=1, source_target_pairs={{0,3},{1,2},{2,1},{3,0},{4,7},{5,6},{6,5},{7,4},{8,11},{9,10},{10,... | collective-permute-start | bytes 589832 | tf_op jit(solution)/shard_map/ppermute | solution.py:19
  6.0 9.2 %collective-permute-start.7 = (bf16[64,1536]{1,0:T(8,128)(2,1)S(1)}, bf16[64,1536]{1,0:T(8,128)(2,1)S(1)}, u32[]{:S(2)}, u32[]{:S(2)}) collective-permute-start(bf16[64,1536]{1,0:T(8,128)(2,1)S(1)} %get-tuple-element.66.refs_0_), channel_id=1, source_target_pairs={{0,2},{1,3},{2,0},{3,1},{4,6},{5,7},{6,4},{7,5},{8,10},{9,11},{10,... | collective-permute-start | bytes 589832 | tf_op jit(solution)/shard_map/ppermute | solution.py:19
  6.5 11.1 %collective-permute-start.6 = (bf16[64,1536]{1,0:T(8,128)(2,1)S(1)}, bf16[64,1536]{1,0:T(8,128)(2,1)S(1)}, u32[]{:S(2)}, u32[]{:S(2)}) collective-permute-start(bf16[64,1536]{1,0:T(8,128)(2,1)S(1)} %get-tuple-element.66.refs_0_), channel_id=1, source_target_pairs={{0,1},{1,0},{2,3},{3,2},{4,5},{5,4},{6,7},{7,6},{8,9},{9,8},{10,11... | collective-permute-start | bytes 589832 | tf_op jit(solution)/shard_map/ppermute | solution.py:19
  6.7 16.3 %collective-permute-start.3 = (bf16[48,1536]{1,0:T(8,128)(2,1)S(1)}, bf16[48,1536]{1,0:T(8,128)(2,1)S(1)}, u32[]{:S(2)}, u32[]{:S(2)}) collective-permute-start(bf16[48,1536]{1,0:T(8,128)(2,1)S(1)} %get-tuple-element.134), channel_id=1, source_target_pairs={{0,2},{1,3},{2,0},{3,1},{4,6},{5,7},{6,4},{7,5},{8,10},{9,11},{10,... | collective-permute-start | bytes 442376 | tf_op jit(solution)/shard_map/ppermute | solution.py:19
  8.7 14.3 %collective-permute-start.1 = (bf16[48,1536]{1,0:T(8,128)(2,1)S(1)}, bf16[48,1536]{1,0:T(8,128)(2,1)S(1)}, u32[]{:S(2)}, u32[]{:S(2)}) collective-permute-start(bf16[48,1536]{1,0:T(8,128)(2,1)S(1)} %get-tuple-element.134), channel_id=1, source_target_pairs={{0,1},{1,0},{2,3},{3,2},{4,5},{5,4},{6,7},{7,6},{8,9},{9,8},{10,11... | collective-permute-start | bytes 442376 | tf_op jit(solution)/shard_map/ppermute | solution.py:19
  11.8 11.2 %collective-permute-start.2 = (bf16[48,1536]{1,0:T(8,128)(2,1)S(1)}, bf16[48,1536]{1,0:T(8,128)(2,1)S(1)}, u32[]{:S(2)}, u32[]{:S(2)}) collective-permute-start(bf16[48,1536]{1,0:T(8,128)(2,1)S(1)} %get-tuple-element.135), channel_id=1, source_target_pairs={{0,2},{1,3},{2,0},{3,1},{4,6},{5,7},{6,4},{7,5},{8,10},{9,11},{10,... | collective-permute-start | bytes 442376 | tf_op jit(solution)/shard_map/ppermute | solution.py:19
  15.3 7.7 %collective-permute-start = (bf16[48,1536]{1,0:T(8,128)(2,1)S(1)}, bf16[48,1536]{1,0:T(8,128)(2,1)S(1)}, u32[]{:S(2)}, u32[]{:S(2)}) collective-permute-start(bf16[48,1536]{1,0:T(8,128)(2,1)S(1)} %get-tuple-element.135), channel_id=1, source_target_pairs={{0,1},{1,0},{2,3},{3,2},{4,5},{5,4},{6,7},{7,6},{8,9},{9,8},{10,11... | collective-permute-start | bytes 442376 | tf_op jit(solution)/shard_map/ppermute | solution.py:19
  23.1 6.3 %collective-permute-start.5 = (bf16[48,1536]{1,0:T(8,128)(2,1)S(1)}, bf16[48,1536]{1,0:T(8,128)(2,1)S(1)}, u32[]{:S(2)}, u32[]{:S(2)}) collective-permute-start(bf16[48,1536]{1,0:T(8,128)(2,1)S(1)} %collective-permute-done.1.refs_2_), channel_id=1, source_target_pairs={{0,2},{1,3},{2,0},{3,1},{4,6},{5,7},{6,4},{7,5},{8,10},{9,11},{10,... | collective-permute-start | bytes 442376 | tf_op jit(solution)/shard_map/ppermute | solution.py:19
  24.0 6.2 %collective-permute-start.4 = (bf16[48,1536]{1,0:T(8,128)(2,1)S(1)}, bf16[48,1536]{1,0:T(8,128)(2,1)S(1)}, u32[]{:S(2)}, u32[]{:S(2)}) collective-permute-start(bf16[48,1536]{1,0:T(8,128)(2,1)S(1)} %collective-permute-done.2.refs_3_), channel_id=1, source_target_pairs={{0,1},{1,0},{2,3},{3,2},{4,5},{5,4},{6,7},{7,6},{8,9},{9,8},{10,11... | collective-permute-start | bytes 442376 | tf_op jit(solution)/shard_map/ppermute | solution.py:19
  25.6 11.7 %collective-permute-start.14 = (f16[32,6144]{1,0:T(8,128)(2,1)S(1)}, f16[32,6144]{1,0:T(8,128)(2,1)S(1)}, u32[]{:S(2)}, u32[]{:S(2)}) collective-permute-start(f16[32,6144]{1,0:T(8,128)(2,1)S(1)} %add_convert_fusion), channel_id=1, source_target_pairs={{0,8},{4,12},{8,0},{12,4},{16,24},{20,28},{24,16},{28,20},{1,9},{5... | collective-permute-start | bytes 1179656 | tf_op jit(solution)/shard_map/ppermute | solution.py:19
  27.3 10.0 %collective-permute-start.13 = (bf16[48,1536]{1,0:T(8,128)(2,1)S(1)}, bf16[48,1536]{1,0:T(8,128)(2,1)S(1)}, u32[]{:S(2)}, u32[]{:S(2)}) collective-permute-start(bf16[48,1536]{1,0:T(8,128)(2,1)S(1)} %get-tuple-element.132), channel_id=1, source_target_pairs={{0,2},{1,3},{2,0},{3,1},{4,6},{5,7},{6,4},{7,5},{8,10},{9,11},{10,... | collective-permute-start | bytes 442376 | tf_op jit(solution)/shard_map/ppermute | solution.py:19
  28.3 9.0 %collective-permute-start.11 = (bf16[48,1536]{1,0:T(8,128)(2,1)S(1)}, bf16[48,1536]{1,0:T(8,128)(2,1)S(1)}, u32[]{:S(2)}, u32[]{:S(2)}) collective-permute-start(bf16[48,1536]{1,0:T(8,128)(2,1)S(1)} %get-tuple-element.132), channel_id=1, source_target_pairs={{0,1},{1,0},{2,3},{3,2},{4,5},{5,4},{6,7},{7,6},{8,9},{9,8},{10,11... | collective-permute-start | bytes 442376 | tf_op jit(solution)/shard_map/ppermute | solution.py:19
  29.3 8.0 %collective-permute-start.12 = (bf16[48,1536]{1,0:T(8,128)(2,1)S(1)}, bf16[48,1536]{1,0:T(8,128)(2,1)S(1)}, u32[]{:S(2)}, u32[]{:S(2)}) collective-permute-start(bf16[48,1536]{1,0:T(8,128)(2,1)S(1)} %get-tuple-element.133), channel_id=1, source_target_pairs={{0,2},{1,3},{2,0},{3,1},{4,6},{5,7},{6,4},{7,5},{8,10},{9,11},{10,... | collective-permute-start | bytes 442376 | tf_op jit(solution)/shard_map/ppermute | solution.py:19
  30.3 7.1 %collective-permute-start.10 = (bf16[48,1536]{1,0:T(8,128)(2,1)S(1)}, bf16[48,1536]{1,0:T(8,128)(2,1)S(1)}, u32[]{:S(2)}, u32[]{:S(2)}) collective-permute-start(bf16[48,1536]{1,0:T(8,128)(2,1)S(1)} %get-tuple-element.133), channel_id=1, source_target_pairs={{0,1},{1,0},{2,3},{3,2},{4,5},{5,4},{6,7},{7,6},{8,9},{9,8},{10,11... | collective-permute-start | bytes 442376 | tf_op jit(solution)/shard_map/ppermute | solution.py:19
  41.7 15.7 %collective-permute-start.16 = (f16[16,6144]{1,0:T(8,128)(2,1)S(1)}, f16[16,6144]{1,0:T(8,128)(2,1)S(1)}, u32[]{:S(2)}, u32[]{:S(2)}) collective-permute-start(f16[16,6144]{1,0:T(8,128)(2,1)S(1)} %get-tuple-element.131), channel_id=1, source_target_pairs={{0,16},{4,20},{8,24},{12,28},{16,0},{20,4},{24,8},{28,12},{1,17},{... | collective-permute-start | bytes 589832 | tf_op jit(solution)/shard_map/ppermute | solution.py:19
  44.6 12.8 %collective-permute-start.17 = (f16[16,6144]{1,0:T(8,128)(2,1)S(1)}, f16[16,6144]{1,0:T(8,128)(2,1)S(1)}, u32[]{:S(2)}, u32[]{:S(2)}) collective-permute-start(f16[16,6144]{1,0:T(8,128)(2,1)S(1)} %convert_element_type.42), channel_id=1, source_target_pairs={{0,8},{4,12},{8,0},{12,4},{16,24},{20,28},{24,16},{28,20},{1,9},{5... | collective-permute-start | bytes 589832 | tf_op jit(solution)/shard_map/ppermute | solution.py:19
  45.0 5.4 %collective-permute-start.19 = (bf16[48,1536]{1,0:T(8,128)(2,1)S(1)}, bf16[48,1536]{1,0:T(8,128)(2,1)S(1)}, u32[]{:S(2)}, u32[]{:S(2)}) collective-permute-start(bf16[48,1536]{1,0:T(8,128)(2,1)S(1)} %collective-permute-done.11.refs_2_), channel_id=1, source_target_pairs={{0,2},{1,3},{2,0},{3,1},{4,6},{5,7},{6,4},{7,5},{8,10},{9,11},{10,... | collective-permute-start | bytes 442376 | tf_op jit(solution)/shard_map/ppermute | solution.py:19
  46.4 5.1 %collective-permute-start.18 = (bf16[48,1536]{1,0:T(8,128)(2,1)S(1)}, bf16[48,1536]{1,0:T(8,128)(2,1)S(1)}, u32[]{:S(2)}, u32[]{:S(2)}) collective-permute-start(bf16[48,1536]{1,0:T(8,128)(2,1)S(1)} %collective-permute-done.12.refs_3_), channel_id=1, source_target_pairs={{0,1},{1,0},{2,3},{3,2},{4,5},{5,4},{6,7},{7,6},{8,9},{9,8},{10,11... | collective-permute-start | bytes 442376 | tf_op jit(solution)/shard_map/ppermute | solution.py:19
  58.7 12.4 %collective-permute-start.21 = (bf16[16,6144]{1,0:T(8,128)(2,1)S(1)}, bf16[16,6144]{1,0:T(8,128)(2,1)S(1)}, u32[]{:S(2)}, u32[]{:S(2)}) collective-permute-start(bf16[16,6144]{1,0:T(8,128)(2,1)S(1)} %fusion.9.refs_0_), channel_id=1, source_target_pairs={{0,16},{4,20},{8,24},{12,28},{16,0},{20,4},{24,8},{28,12},{1,17},{... | collective-permute-start | bytes 589832 | tf_op jit(solution)/shard_map/ppermute | solution.py:19
  59.1 12.0 %collective-permute-start.20 = (bf16[16,6144]{1,0:T(8,128)(2,1)S(1)}, bf16[16,6144]{1,0:T(8,128)(2,1)S(1)}, u32[]{:S(2)}, u32[]{:S(2)}) collective-permute-start(bf16[16,6144]{1,0:T(8,128)(2,1)S(1)} %fusion.9.refs_0_), channel_id=1, source_target_pairs={{0,8},{4,12},{8,0},{12,4},{16,24},{20,28},{24,16},{28,20},{1,9},{5... | collective-permute-start | bytes 589832 | tf_op jit(solution)/shard_map/ppermute | solution.py:19
  71.1 8.1 %collective-permute-start.23 = (bf16[16,6144]{1,0:T(8,128)(2,1)S(1)}, bf16[16,6144]{1,0:T(8,128)(2,1)S(1)}, u32[]{:S(2)}, u32[]{:S(2)}) collective-permute-start(bf16[16,6144]{1,0:T(8,128)(2,1)S(1)} %collective-permute-done.21.refs_2_), channel_id=1, source_target_pairs={{0,8},{4,12},{8,0},{12,4},{16,24},{20,28},{24,16},{28,20},{1,9},{5... | collective-permute-start | bytes 589832 | tf_op jit(solution)/shard_map/ppermute | solution.py:19
  71.1 8.1 %collective-permute-start.24 = (bf16[16,6144]{1,0:T(8,128)(2,1)S(1)}, bf16[16,6144]{1,0:T(8,128)(2,1)S(1)}, u32[]{:S(2)}, u32[]{:S(2)}) collective-permute-start(bf16[16,6144]{1,0:T(8,128)(2,1)S(1)} %fusion.9.refs_0_), channel_id=1, source_target_pairs={{0,4},{4,0},{8,12},{12,8},{16,20},{20,16},{24,28},{28,24},{1,5},{5... | collective-permute-start | bytes 589832 | tf_op jit(solution)/shard_map/ppermute | solution.py:19
  71.1 8.2 %collective-permute-start.25 = (bf16[16,6144]{1,0:T(8,128)(2,1)S(1)}, bf16[16,6144]{1,0:T(8,128)(2,1)S(1)}, u32[]{:S(2)}, u32[]{:S(2)}) collective-permute-start(bf16[16,6144]{1,0:T(8,128)(2,1)S(1)} %collective-permute-done.20.refs_1_), channel_id=1, source_target_pairs={{0,4},{4,0},{8,12},{12,8},{16,20},{20,16},{24,28},{28,24},{1,5},{5... | collective-permute-start | bytes 589832 | tf_op jit(solution)/shard_map/ppermute | solution.py:19
  71.6 7.7 %collective-permute-start.26 = (bf16[16,6144]{1,0:T(8,128)(2,1)S(1)}, bf16[16,6144]{1,0:T(8,128)(2,1)S(1)}, u32[]{:S(2)}, u32[]{:S(2)}) collective-permute-start(bf16[16,6144]{1,0:T(8,128)(2,1)S(1)} %collective-permute-done.21.refs_2_), channel_id=1, source_target_pairs={{0,4},{4,0},{8,12},{12,8},{16,20},{20,16},{24,28},{28,24},{1,5},{5... | collective-permute-start | bytes 589832 | tf_op jit(solution)/shard_map/ppermute | solution.py:19
  71.7 16.4 %collective-permute-start.31 = (f16[16,6144]{1,0:T(8,128)(2,1)S(1)}, f16[16,6144]{1,0:T(8,128)(2,1)S(1)}, u32[]{:S(2)}, u32[]{:S(2)}) collective-permute-start(f16[16,6144]{1,0:T(8,128)(2,1)S(1)} %get-tuple-element.129), channel_id=1, source_target_pairs={{0,16},{4,20},{8,24},{12,28},{16,0},{20,4},{24,8},{28,12},{1,17},{... | collective-permute-start | bytes 589832 | tf_op jit(solution)/shard_map/ppermute | solution.py:19
  79.3 9.1 %collective-permute-start.32 = (f16[16,6144]{1,0:T(8,128)(2,1)S(1)}, f16[16,6144]{1,0:T(8,128)(2,1)S(1)}, u32[]{:S(2)}, u32[]{:S(2)}) collective-permute-start(f16[16,6144]{1,0:T(8,128)(2,1)S(1)} %convert_element_type.48), channel_id=1, source_target_pairs={{0,8},{4,12},{8,0},{12,4},{16,24},{20,28},{24,16},{28,20},{1,9},{5... | collective-permute-start | bytes 589832 | tf_op jit(solution)/shard_map/ppermute | solution.py:19
  87.6 12.1 %collective-permute-start.28 = (bf16[1536,128]{1,0:T(8,128)(2,1)S(1)}, bf16[1536,128]{1,0:T(8,128)(2,1)S(1)}, u32[]{:S(2)}, u32[]{:S(2)}) collective-permute-start(bf16[1536,128]{1,0:T(8,128)(2,1)S(1)} %get-tuple-element.98), channel_id=1, source_target_pairs={{0,1},{1,0},{2,3},{3,2},{4,5},{5,4},{6,7},{7,6},{8,9},{9,8},{10,11... | collective-permute-start | bytes 1179656 | tf_op jit(solution)/shard_map/ppermute | solution.py:19
  88.1 11.5 %collective-permute-start.29 = (bf16[1536,128]{1,0:T(8,128)(2,1)}, bf16[1536,128]{1,0:T(8,128)(2,1)S(1)}, u32[]{:S(2)}, u32[]{:S(2)}) collective-permute-start(bf16[1536,128]{1,0:T(8,128)(2,1)} %get-tuple-element.99), channel_id=1, source_target_pairs={{0,2},{1,3},{2,0},{3,1},{4,6},{5,7},{6,4},{7,5},{8,10},{9,11},{10,... | collective-permute-start | bytes 1179656 | tf_op jit(solution)/shard_map/ppermute | solution.py:19
  88.4 11.2 %collective-permute-start.34 = (bf16[16,6144]{1,0:T(8,128)(2,1)S(1)}, bf16[16,6144]{1,0:T(8,128)(2,1)S(1)}, u32[]{:S(2)}, u32[]{:S(2)}) collective-permute-start(bf16[16,6144]{1,0:T(8,128)(2,1)S(1)} %fusion.2.refs_0_), channel_id=1, source_target_pairs={{0,16},{4,20},{8,24},{12,28},{16,0},{20,4},{24,8},{28,12},{1,17},{... | collective-permute-start | bytes 589832 | tf_op jit(solution)/shard_map/ppermute | solution.py:19
  89.6 12.1 %collective-permute-start.33 = (bf16[16,6144]{1,0:T(8,128)(2,1)S(1)}, bf16[16,6144]{1,0:T(8,128)(2,1)S(1)}, u32[]{:S(2)}, u32[]{:S(2)}) collective-permute-start(bf16[16,6144]{1,0:T(8,128)(2,1)S(1)} %fusion.2.refs_0_), channel_id=1, source_target_pairs={{0,8},{4,12},{8,0},{12,4},{16,24},{20,28},{24,16},{28,20},{1,9},{5... | collective-permute-start | bytes 589832 | tf_op jit(solution)/shard_map/ppermute | solution.py:19
  99.7 6.8 %collective-permute-start.35 = (bf16[16,6144]{1,0:T(8,128)(2,1)S(1)}, bf16[16,6144]{1,0:T(8,128)(2,1)S(1)}, u32[]{:S(2)}, u32[]{:S(2)}) collective-permute-start(bf16[16,6144]{1,0:T(8,128)(2,1)S(1)} %collective-permute-done.34.refs_2_), channel_id=1, source_target_pairs={{0,8},{4,12},{8,0},{12,4},{16,24},{20,28},{24,16},{28,20},{1,9},{5... | collective-permute-start | bytes 589832 | tf_op jit(solution)/shard_map/ppermute | solution.py:19
  99.7 15.3 %collective-permute-start.30 = (bf16[1536,128]{1,0:T(8,128)(2,1)S(1)}, bf16[1536,128]{1,0:T(8,128)(2,1)S(1)}, u32[]{:S(2)}, u32[]{:S(2)}) collective-permute-start(bf16[1536,128]{1,0:T(8,128)(2,1)S(1)} %copy-done.8), channel_id=1, source_target_pairs={{0,3},{1,2},{2,1},{3,0},{4,7},{5,6},{6,5},{7,4},{8,11},{9,10},{10,... | collective-permute-start | bytes 1179656 | tf_op jit(solution)/shard_map/ppermute | solution.py:19
  101.7 4.7 %collective-permute-start.36 = (bf16[16,6144]{1,0:T(8,128)(2,1)S(1)}, bf16[16,6144]{1,0:T(8,128)(2,1)S(1)}, u32[]{:S(2)}, u32[]{:S(2)}) collective-permute-start(bf16[16,6144]{1,0:T(8,128)(2,1)S(1)} %fusion.2.refs_0_), channel_id=1, source_target_pairs={{0,4},{4,0},{8,12},{12,8},{16,20},{20,16},{24,28},{28,24},{1,5},{5... | collective-permute-start | bytes 589832 | tf_op jit(solution)/shard_map/ppermute | solution.py:19
  101.7 4.7 %collective-permute-start.37 = (bf16[16,6144]{1,0:T(8,128)(2,1)S(1)}, bf16[16,6144]{1,0:T(8,128)(2,1)S(1)}, u32[]{:S(2)}, u32[]{:S(2)}) collective-permute-start(bf16[16,6144]{1,0:T(8,128)(2,1)S(1)} %collective-permute-done.33.refs_1_), channel_id=1, source_target_pairs={{0,4},{4,0},{8,12},{12,8},{16,20},{20,16},{24,28},{28,24},{1,5},{5... | collective-permute-start | bytes 589832 | tf_op jit(solution)/shard_map/ppermute | solution.py:19
  102.2 4.2 %collective-permute-start.38 = (bf16[16,6144]{1,0:T(8,128)(2,1)S(1)}, bf16[16,6144]{1,0:T(8,128)(2,1)S(1)}, u32[]{:S(2)}, u32[]{:S(2)}) collective-permute-start(bf16[16,6144]{1,0:T(8,128)(2,1)S(1)} %collective-permute-done.34.refs_2_), channel_id=1, source_target_pairs={{0,4},{4,0},{8,12},{12,8},{16,20},{20,16},{24,28},{28,24},{1,5},{5... | collective-permute-start | bytes 589832 | tf_op jit(solution)/shard_map/ppermute | solution.py:19
  115.0 12.1 %collective-permute-start.40 = (bf16[1536,128]{1,0:T(8,128)(2,1)S(1)}, bf16[1536,128]{1,0:T(8,128)(2,1)S(1)}, u32[]{:S(2)}, u32[]{:S(2)}) collective-permute-start(bf16[1536,128]{1,0:T(8,128)(2,1)S(1)} %get-tuple-element.109), channel_id=1, source_target_pairs={{0,1},{1,0},{2,3},{3,2},{4,5},{5,4},{6,7},{7,6},{8,9},{9,8},{10,11... | collective-permute-start | bytes 1179656 | tf_op jit(solution)/shard_map/ppermute | solution.py:19
  115.9 19.6 %collective-permute-start.41 = (bf16[1536,128]{1,0:T(8,128)(2,1)}, bf16[1536,128]{1,0:T(8,128)(2,1)S(1)}, u32[]{:S(2)}, u32[]{:S(2)}) collective-permute-start(bf16[1536,128]{1,0:T(8,128)(2,1)} %get-tuple-element.110), channel_id=1, source_target_pairs={{0,2},{1,3},{2,0},{3,1},{4,6},{5,7},{6,4},{7,5},{8,10},{9,11},{10,... | collective-permute-start | bytes 1179656 | tf_op jit(solution)/shard_map/ppermute | solution.py:19
  115.9 19.6 %collective-permute-start.42 = (bf16[1536,128]{1,0:T(8,128)(2,1)}, bf16[1536,128]{1,0:T(8,128)(2,1)S(1)}, u32[]{:S(2)}, u32[]{:S(2)}) collective-permute-start(bf16[1536,128]{1,0:T(8,128)(2,1)} %get-tuple-element.111), channel_id=1, source_target_pairs={{0,3},{1,2},{2,1},{3,0},{4,7},{5,6},{6,5},{7,4},{8,11},{9,10},{10,... | collective-permute-start | bytes 1179656 | tf_op jit(solution)/shard_map/ppermute | solution.py:19
  127.1 4.9 %collective-permute-start.45 = (f32[64,128]{1,0:T(8,128)S(1)}, f32[64,128]{1,0:T(8,128)S(1)}, u32[]{:S(2)}, u32[]{:S(2)}) collective-permute-start(f32[64,128]{1,0:T(8,128)S(1)} %add.137), channel_id=1, source_target_pairs={{0,16},{4,20},{8,24},{12,28},{16,0},{20,4},{24,8},{28,12},{1,17},{... | collective-permute-start | bytes 98312 | tf_op jit(solution)/shard_map/ppermute | solution.py:19
  132.0 6.5 %collective-permute-start.51 = (f32[64,128]{1,0:T(8,128)S(1)}, f32[64,128]{1,0:T(8,128)S(1)}, u32[]{:S(2)}, u32[]{:S(2)}) collective-permute-start(f32[64,128]{1,0:T(8,128)S(1)} %add.138), channel_id=1, source_target_pairs={{0,3},{1,2},{2,1},{3,0},{4,7},{5,6},{6,5},{7,4},{8,11},{9,10},{10,... | collective-permute-start | bytes 98312 | tf_op jit(solution)/shard_map/ppermute | solution.py:19
  132.3 6.2 %collective-permute-start.50 = (f32[64,128]{1,0:T(8,128)S(1)}, f32[64,128]{1,0:T(8,128)S(1)}, u32[]{:S(2)}, u32[]{:S(2)}) collective-permute-start(f32[64,128]{1,0:T(8,128)S(1)} %add.138), channel_id=1, source_target_pairs={{0,2},{1,3},{2,0},{3,1},{4,6},{5,7},{6,4},{7,5},{8,10},{9,11},{10,... | collective-permute-start | bytes 98312 | tf_op jit(solution)/shard_map/ppermute | solution.py:19
  134.2 4.3 %collective-permute-start.49 = (f32[64,128]{1,0:T(8,128)S(1)}, f32[64,128]{1,0:T(8,128)S(1)}, u32[]{:S(2)}, u32[]{:S(2)}) collective-permute-start(f32[64,128]{1,0:T(8,128)S(1)} %add.138), channel_id=1, source_target_pairs={{0,1},{1,0},{2,3},{3,2},{4,5},{5,4},{6,7},{7,6},{8,9},{9,8},{10,11... | collective-permute-start | bytes 98312 | tf_op jit(solution)/shard_map/ppermute | solution.py:19
  139.8 4.3 %collective-permute-start.47 = (f32[128,128]{1,0:T(8,128)S(1)}, f32[128,128]{1,0:T(8,128)S(1)}, u32[]{:S(2)}, u32[]{:S(2)}) collective-permute-start(f32[128,128]{1,0:T(8,128)S(1)} %dynamic-slice_add_fusion), channel_id=1, source_target_pairs={{0,8},{4,12},{8,0},{12,4},{16,24},{20,28},{24,16},{28,20},{1,9},{5... | collective-permute-start | bytes 196616 | tf_op jit(solution)/shard_map/ppermute | solution.py:19
  140.3 4.8 %collective-permute-start.52 = (f32[64,128]{1,0:T(8,128)S(1)}, f32[64,128]{1,0:T(8,128)S(1)}, u32[]{:S(2)}, u32[]{:S(2)}) collective-permute-start(f32[64,128]{1,0:T(8,128)S(1)} %add_bitcast_fusion.1), channel_id=1, source_target_pairs={{0,4},{4,0},{8,12},{12,8},{16,20},{20,16},{24,28},{28,24},{1,5},{5... | collective-permute-start | bytes 98312 | tf_op jit(solution)/shard_map/ppermute | solution.py:19
  144.2 5.8 %collective-permute-start.48 = (f32[128,128]{1,0:T(8,128)S(1)}, f32[128,128]{1,0:T(8,128)S(1)}, u32[]{:S(2)}, u32[]{:S(2)}) collective-permute-start(f32[128,128]{1,0:T(8,128)S(1)} %add.142), channel_id=1, source_target_pairs={{0,16},{4,20},{8,24},{12,28},{16,0},{20,4},{24,8},{28,12},{1,17},{... | collective-permute-start | bytes 196616 | tf_op jit(solution)/shard_map/ppermute | solution.py:19
  150.0 5.3 %collective-permute-start.55 = (f32[128,128]{1,0:T(8,128)S(1)}, f32[128,128]{1,0:T(8,128)S(1)}, u32[]{:S(2)}, u32[]{:S(2)}) collective-permute-start(f32[128,128]{1,0:T(8,128)S(1)} %add.151), channel_id=1, source_target_pairs={{0,3},{1,2},{2,1},{3,0},{4,7},{5,6},{6,5},{7,4},{8,11},{9,10},{10,... | collective-permute-start | bytes 196616 | tf_op jit(solution)/shard_map/ppermute | solution.py:19
  151.4 4.5 %collective-permute-start.54 = (f32[128,128]{1,0:T(8,128)S(1)}, f32[128,128]{1,0:T(8,128)S(1)}, u32[]{:S(2)}, u32[]{:S(2)}) collective-permute-start(f32[128,128]{1,0:T(8,128)S(1)} %add.151), channel_id=1, source_target_pairs={{0,2},{1,3},{2,0},{3,1},{4,6},{5,7},{6,4},{7,5},{8,10},{9,11},{10,... | collective-permute-start | bytes 196616 | tf_op jit(solution)/shard_map/ppermute | solution.py:19
  152.1 4.3 %collective-permute-start.53 = (f32[128,128]{1,0:T(8,128)S(1)}, f32[128,128]{1,0:T(8,128)S(1)}, u32[]{:S(2)}, u32[]{:S(2)}) collective-permute-start(f32[128,128]{1,0:T(8,128)S(1)} %add.151), channel_id=1, source_target_pairs={{0,1},{1,0},{2,3},{3,2},{4,5},{5,4},{6,7},{7,6},{8,9},{9,8},{10,11... | collective-permute-start | bytes 196616 | tf_op jit(solution)/shard_map/ppermute | solution.py:19
  (19 other events, 101.3 us)

commit v5 on v4

--- a/solution.py
+++ b/solution.py
@@ -10,6 +10,7 @@
 BC = 12
 GROUP = 16
 SUBLANES = 8
+SCALE = 16.0
 VMEM_LIMIT = 52 * 1024 * 1024
 NO_COST = pl.CostEstimate(flops=0, bytes_accessed=0, transcendentals=0)
 
@@ -163,11 +164,11 @@
 
 
 def half(value):
-    return value.astype(jnp.float16)
+    return (value * (1.0 / SCALE)).astype(jnp.float16)
 
 
 def full(value):
-    return value.astype(jnp.float32)
+    return value.astype(jnp.float32) * SCALE
 
 
 def gather(shard):
@@ -260,7 +261,7 @@
     a.send_other([b.near, far])
     b.gather_far()
     a.reduce(far[:GROUP])
-    a.reduce_last(a.sent)
+    a.reduce_last([a.sent, [piece[2] for piece in b.pieces[5:]]])
     b.multiply_transposed(a.sent)
     b.send_other(a.arriving[0])
     a.own(b.other)
@@ -271,8 +272,8 @@
     a.multiply_forward()
     b.own(a.forward)
     a.send_rows()
-    b.spread(a.arrived[:2])
-    b.share()
+    b.spread()
+    b.share(a.arrived[:2])
     b.multiply_forward()
     b.send_rows(a.arrived[2:])
 

time: 166 us -> 164 us (0.988)
  waiting for transfers between devices: 64.7 us -> 55.2 us
  starting transfers between devices: 45.1 us -> 53.6 us
    ppermute x57, waiting for transfers between devices: 64.7 us -> 55.2 us  [swap(): return lax.ppermute(value, axis, [(i, i ^ offset) for i in range(size)])]
    ppermute x57, starting transfers between devices: 45.1 us -> 53.6 us  [swap(): return lax.ppermute(value, axis, [(i, i ^ offset) for i in range(size)])]
  transfers between devices with their start and end apart: 57 -> 57, of which waited for: 25 -> 29; matrix products, arithmetic and copies ran while one was open for 1% -> 2% of each run, Pallas kernels for 25% -> 25%
where the time goes in v5:
time: 164 us
  waiting for transfers between devices  55.2 us (34%)
  starting transfers between devices  53.6 us (33%)
  Pallas kernels  48.4 us (30%)
  other arithmetic  2.99 us (2%)
  local copies, waits for them, and re-layouts  2.09 us (1%)
  between operations  1.8 us (1%)
    ppermute x57, waiting for transfers between devices, swap(): return lax.ppermute(value, axis, [(i, i ^ offset) for i in range(size)])  55.2 us
    ppermute x57, starting transfers between devices, swap(): return lax.ppermute(value, axis, [(i, i ^ offset) for i in range(size)])  53.6 us
    pallas_call x5, Pallas kernels, tile_call(): pl.pallas_call(kernel, out_shape=out_shape, in_specs=[smem, pl.BlockSpec(...  30.9 us
    pallas_call x1, Pallas kernels, body(): pl.pallas_call(functools.partial(second_factor_kernel, total_rows), out_s...  7.39 us
    pallas_call x2, Pallas kernels, finish_call(): pl.pallas_call(functools.partial(finish_kernel, len(parts)), out_shape=(j...  4.97 us
    pallas_call x1, Pallas kernels, body(): pl.pallas_call(functools.partial(first_factor_kernel, total_rows), out_sh...  4.88 us
  transfers between devices with their start and end apart: 57, of which 29 were waited for; matrix products, arithmetic and copies ran while one was open for 2% of the time, Pallas kernels for 25%

profile of v5, /device:TPU:0, one launch (start us, length us, event | category | flops | bytes accessed | tf_op | source)
XLA Modules:
  0.0 164.1 jit_solution(17376553987928130664)
XLA Ops:
  2.1 4.0 %collective-permute-start.8 = (bf16[64,1536]{1,0:T(8,128)(2,1)S(1)}, bf16[64,1536]{1,0:T(8,128)(2,1)S(1)}, u32[]{:S(2)}, u32[]{:S(2)}) collective-permute-start(bf16[64,1536]{1,0:T(8,128)(2,1)S(1)} %get-tuple-element.67.refs_0_), channel_id=1, source_target_pairs={{0,3},{1,2},{2,1},{3,0},{4,7},{5,6},{6,5},{7,4},{8,11},{9,10},{10,... | collective-permute-start | bytes 589832 | tf_op jit(solution)/shard_map/ppermute | solution.py:20
  6.7 2.0 %collective-permute-start.3 = (bf16[48,1536]{1,0:T(8,128)(2,1)S(1)}, bf16[48,1536]{1,0:T(8,128)(2,1)S(1)}, u32[]{:S(2)}, u32[]{:S(2)}) collective-permute-start(bf16[48,1536]{1,0:T(8,128)(2,1)S(1)} %get-tuple-element.136), channel_id=1, source_target_pairs={{0,2},{1,3},{2,0},{3,1},{4,6},{5,7},{6,4},{7,5},{8,10},{9,11},{10,... | collective-permute-start | bytes 442376 | tf_op jit(solution)/shard_map/ppermute | solution.py:20
  8.7 1.5 collective-permute-start.1
  10.2 1.6 collective-permute-done.8.refs_3_
  11.8 2.0 %collective-permute-start.2 = (bf16[48,1536]{1,0:T(8,128)(2,1)S(1)}, bf16[48,1536]{1,0:T(8,128)(2,1)S(1)}, u32[]{:S(2)}, u32[]{:S(2)}) collective-permute-start(bf16[48,1536]{1,0:T(8,128)(2,1)S(1)} %get-tuple-element.137), channel_id=1, source_target_pairs={{0,2},{1,3},{2,0},{3,1},{4,6},{5,7},{6,4},{7,5},{8,10},{9,11},{10,... | collective-permute-start | bytes 442376 | tf_op jit(solution)/shard_map/ppermute | solution.py:20
  13.8 1.4 collective-permute-done.7.refs_2_
  15.3 1.7 %collective-permute-start = (bf16[48,1536]{1,0:T(8,128)(2,1)S(1)}, bf16[48,1536]{1,0:T(8,128)(2,1)S(1)}, u32[]{:S(2)}, u32[]{:S(2)}) collective-permute-start(bf16[48,1536]{1,0:T(8,128)(2,1)S(1)} %get-tuple-element.137), channel_id=1, source_target_pairs={{0,1},{1,0},{2,3},{3,2},{4,5},{5,4},{6,7},{7,6},{8,9},{9,8},{10,11... | collective-permute-start | bytes 442376 | tf_op jit(solution)/shard_map/ppermute | solution.py:20
  17.7 5.3 %shard_map.69 = (f32[32,6144]{1,0:T(8,128)S(1)}, f32[32,6144]{1,0:T(8,128)}) custom-call(s32[33]{0:T(128)S(1)} %pad_add_fusion.layout_ref, bf16[16,512,512]{2,1,0:T(8,128)(2,1)} %bitcast.17, bf16[64,1536]{1,0:T(8,128)(2,1)S(1)} %get-tuple-element.67.refs_0_, bf16[64,1536]{1,0:T(8,128)(2,1)S(1)} %collective-permute-done.6.refs_1_, ...), custom_call_target="tpu_custom_call" | custom-call | tf_op jit(solution)/shard_map/pallas_call | solution.py:147
  23.7 1.5 collective-permute-start.4
  25.7 1.3 collective-permute-start.14
  27.0 1.3 collective-permute-start.13
  30.0 1.4 collective-permute-start.10
  31.4 5.9 %shard_map.70 = (f32[48,6144]{1,0:T(8,128)}, f32[48,6144]{1,0:T(8,128)}) custom-call(s32[33]{0:T(128)S(1)} %pad_add_fusion.layout_ref, bf16[16,512,512]{2,1,0:T(8,128)(2,1)} %bitcast.18, bf16[96,1536]{1,0:T(8,128)(2,1)S(1)} %get-tuple-element.71.refs_0_, bf16[48,1536]{1,0:T(8,128)(2,1)S(1)} %collective-permute-done.refs_1_, ...), custom_call_target="tpu_custom_call" | custom-call | tf_op jit(solution)/shard_map/pallas_call | solution.py:147
  37.7 1.8 %collective-permute-start.17 = (bf16[48,1536]{1,0:T(8,128)(2,1)S(1)}, bf16[48,1536]{1,0:T(8,128)(2,1)S(1)}, u32[]{:S(2)}, u32[]{:S(2)}) collective-permute-start(bf16[48,1536]{1,0:T(8,128)(2,1)S(1)} %collective-permute-done.12.refs_3_), channel_id=1, source_target_pairs={{0,1},{1,0},{2,3},{3,2},{4,5},{5,4},{6,7},{7,6},{8,9},{9,8},{10,11... | collective-permute-start | bytes 442376 | tf_op jit(solution)/shard_map/ppermute | solution.py:20
  40.5 1.2 slice_add_fusion.3
  41.7 2.1 %collective-permute-start.16 = (f16[16,6144]{1,0:T(8,128)(2,1)S(1)}, f16[16,6144]{1,0:T(8,128)(2,1)S(1)}, u32[]{:S(2)}, u32[]{:S(2)}) collective-permute-start(f16[16,6144]{1,0:T(8,128)(2,1)S(1)} %get-tuple-element.133), channel_id=1, source_target_pairs={{0,16},{4,20},{8,24},{12,28},{16,0},{20,4},{24,8},{28,12},{1,17},{... | collective-permute-start | bytes 589832 | tf_op jit(solution)/shard_map/ppermute | solution.py:20
  43.8 1.8 %collective-permute-start.19 = (f16[16,6144]{1,0:T(8,128)(2,1)S(1)}, f16[16,6144]{1,0:T(8,128)(2,1)S(1)}, u32[]{:S(2)}, u32[]{:S(2)}) collective-permute-start(f16[16,6144]{1,0:T(8,128)(2,1)S(1)} %multiply_convert_fusion.2), channel_id=1, source_target_pairs={{0,8},{4,12},{8,0},{12,4},{16,24},{20,28},{24,16},{28,20},{1,9},{5... | collective-permute-start | bytes 589832 | tf_op jit(solution)/shard_map/ppermute | solution.py:20
  45.6 5.8 %shard_map.71 = (f32[48,6144]{1,0:T(8,128)}, f32[48,6144]{1,0:T(8,128)}) custom-call(s32[33]{0:T(128)S(1)} %pad_add_fusion.layout_ref, bf16[16,512,512]{2,1,0:T(8,128)(2,1)} %bitcast.19, bf16[96,1536]{1,0:T(8,128)(2,1)S(1)} %get-tuple-element.84.refs_0_, bf16[48,1536]{1,0:T(8,128)(2,1)S(1)} %collective-permute-done.10.refs_1_, ...), custom_call_target="tpu_custom_call" | custom-call | tf_op jit(solution)/shard_map/pallas_call | solution.py:147
  51.5 2.5 %collective-permute-done.16 = f16[16,6144]{1,0:T(8,128)(2,1)S(1)} collective-permute-done((f16[16,6144]{1,0:T(8,128)(2,1)S(1)}, f16[16,6144]{1,0:T(8,128)(2,1)S(1)}, u32[]{:S(2)}, u32[]{:S(2)}) %collective-permute-start.16) | collective-permute-done | bytes 196640 | tf_op jit(solution)/shard_map/ppermute | solution.py:20
  55.1 2.0 %collective-permute-start.21 = (bf16[16,6144]{1,0:T(8,128)(2,1)S(1)}, bf16[16,6144]{1,0:T(8,128)(2,1)S(1)}, u32[]{:S(2)}, u32[]{:S(2)}) collective-permute-start(bf16[16,6144]{1,0:T(8,128)(2,1)S(1)} %fusion.11.refs_0_), channel_id=1, source_target_pairs={{0,16},{4,20},{8,24},{12,28},{16,0},{20,4},{24,8},{28,12},{1,17},{... | collective-permute-start | bytes 589832 | tf_op jit(solution)/shard_map/ppermute | solution.py:20
  57.1 2.5 %collective-permute-start.20 = (bf16[16,6144]{1,0:T(8,128)(2,1)S(1)}, bf16[16,6144]{1,0:T(8,128)(2,1)S(1)}, u32[]{:S(2)}, u32[]{:S(2)}) collective-permute-start(bf16[16,6144]{1,0:T(8,128)(2,1)S(1)} %fusion.11.refs_0_), channel_id=1, source_target_pairs={{0,8},{4,12},{8,0},{12,4},{16,24},{20,28},{24,16},{28,20},{1,9},{5... | collective-permute-start | bytes 589832 | tf_op jit(solution)/shard_map/ppermute | solution.py:20
  59.8 8.0 %collective-permute-done.21.refs_2_ = bf16[16,6144]{1,0:T(8,128)(2,1)S(1)} collective-permute-done((bf16[16,6144]{1,0:T(8,128)(2,1)S(1)}, bf16[16,6144]{1,0:T(8,128)(2,1)S(1)}, u32[]{:S(2)}, u32[]{:S(2)}) %collective-permute-start.21) | collective-permute-done | bytes 196640 | tf_op jit(solution)/shard_map/ppermute | solution.py:20
  68.3 3.3 %collective-permute-start.31 = (f16[16,6144]{1,0:T(8,128)(2,1)S(1)}, f16[16,6144]{1,0:T(8,128)(2,1)S(1)}, u32[]{:S(2)}, u32[]{:S(2)}) collective-permute-start(f16[16,6144]{1,0:T(8,128)(2,1)S(1)} %get-tuple-element.131), channel_id=1, source_target_pairs={{0,16},{4,20},{8,24},{12,28},{16,0},{20,4},{24,8},{28,12},{1,17},{... | collective-permute-start | bytes 589832 | tf_op jit(solution)/shard_map/ppermute | solution.py:20
  71.6 5.2 %collective-permute-done.23.refs_3_ = bf16[16,6144]{1,0:T(8,128)(2,1)S(1)} collective-permute-done((bf16[16,6144]{1,0:T(8,128)(2,1)S(1)}, bf16[16,6144]{1,0:T(8,128)(2,1)S(1)}, u32[]{:S(2)}, u32[]{:S(2)}) %collective-permute-start.23) | collective-permute-done | bytes 196640 | tf_op jit(solution)/shard_map/ppermute | solution.py:20
  77.0 1.3 collective-permute-done.27.refs_7_
  78.3 6.9 %shard_map.72 = (f32[1536,128]{1,0:T(8,128)}, bf16[1536,128]{1,0:T(8,128)(2,1)S(1)}, bf16[1536,128]{1,0:T(8,128)(2,1)}, bf16[1536,128]{1,0:T(8,128)(2,1)}) custom-call(s32[33]{0:T(128)S(1)} %pad_add_fusion.layout_ref, bf16[16,512,512]{2,1,0:T(8,128)(2,1)} %bitcast.20, bf16[16,6144]{1,0:T(8,128)(2,1)S(1)} %fusion.11.refs_0_, ...), custom_call_target="tpu_custom_call" | custom-call | tf_op jit(solution)/shard_map/pallas_call | solution.py:147
  86.1 2.0 %collective-permute-start.28 = (bf16[1536,128]{1,0:T(8,128)(2,1)S(1)}, bf16[1536,128]{1,0:T(8,128)(2,1)S(1)}, u32[]{:S(2)}, u32[]{:S(2)}) collective-permute-start(bf16[1536,128]{1,0:T(8,128)(2,1)S(1)} %get-tuple-element.99), channel_id=1, source_target_pairs={{0,1},{1,0},{2,3},{3,2},{4,5},{5,4},{6,7},{7,6},{8,9},{9,8},{10,11... | collective-permute-start | bytes 1179656 | tf_op jit(solution)/shard_map/ppermute | solution.py:20
  88.7 1.9 %collective-permute-start.33 = (bf16[16,6144]{1,0:T(8,128)(2,1)S(1)}, bf16[16,6144]{1,0:T(8,128)(2,1)S(1)}, u32[]{:S(2)}, u32[]{:S(2)}) collective-permute-start(bf16[16,6144]{1,0:T(8,128)(2,1)S(1)} %fusion.2.refs_0_), channel_id=1, source_target_pairs={{0,8},{4,12},{8,0},{12,4},{16,24},{20,28},{24,16},{28,20},{1,9},{5... | collective-permute-start | bytes 589832 | tf_op jit(solution)/shard_map/ppermute | solution.py:20
  90.5 6.9 %collective-permute-done.34.refs_2_ = bf16[16,6144]{1,0:T(8,128)(2,1)S(1)} collective-permute-done((bf16[16,6144]{1,0:T(8,128)(2,1)S(1)}, bf16[16,6144]{1,0:T(8,128)(2,1)S(1)}, u32[]{:S(2)}, u32[]{:S(2)}) %collective-permute-start.34) | collective-permute-done | bytes 196640 | tf_op jit(solution)/shard_map/ppermute | solution.py:20
  97.4 1.4 collective-permute-start.30
  98.9 5.3 %collective-permute-done.35.refs_3_ = bf16[16,6144]{1,0:T(8,128)(2,1)S(1)} collective-permute-done((bf16[16,6144]{1,0:T(8,128)(2,1)S(1)}, bf16[16,6144]{1,0:T(8,128)(2,1)S(1)}, u32[]{:S(2)}, u32[]{:S(2)}) %collective-permute-start.35) | collective-permute-done | bytes 196640 | tf_op jit(solution)/shard_map/ppermute | solution.py:20
  106.2 7.1 %shard_map.73 = (f32[1536,128]{1,0:T(8,128)}, bf16[1536,128]{1,0:T(8,128)(2,1)S(1)}, bf16[1536,128]{1,0:T(8,128)(2,1)}, bf16[1536,128]{1,0:T(8,128)(2,1)}) custom-call(s32[33]{0:T(128)S(1)} %pad_add_fusion.layout_ref, bf16[16,512,512]{2,1,0:T(8,128)(2,1)} %bitcast.21, bf16[16,6144]{1,0:T(8,128)(2,1)S(1)} %fusion.2.refs_0_, ...), custom_call_target="tpu_custom_call" | custom-call | tf_op jit(solution)/shard_map/pallas_call | solution.py:147
  113.3 1.3 collective-permute-start.40
  115.4 1.5 collective-permute-start.42
  116.9 2.0 %shard_map.74 = (f32[1536,128]{1,0:T(8,128)S(1)}, f32[128,128]{1,0:T(8,128)S(1)}) custom-call(f32[1536,128]{1,0:T(8,128)} %get-tuple-element.98.refs_0_, bf16[1536,128]{1,0:T(8,128)(2,1)S(1)} %collective-permute-done.28.refs_1_, bf16[1536,128]{1,0:T(8,128)(2,1)S(1)} %collective-permute-done.29.refs_2_, bf16[1536,128]{1,0:T(8,128)(2,1)S(1)} %collective-permute-done.30.refs_3_), custom_call_target="tpu_custom_call" | custom-call | tf_op jit(solution)/shard_map/pallas_call | solution.py:239
  119.8 1.2 collective-permute-done.43
  121.0 3.9 %collective-permute-done.44 = f32[64,128]{1,0:T(8,128)S(1)} collective-permute-done((f32[64,128]{1,0:T(8,128)S(1)}, f32[64,128]{1,0:T(8,128)S(1)}, u32[]{:S(2)}, u32[]{:S(2)}) %collective-permute-start.44) | collective-permute-done | bytes 32800 | tf_op jit(solution)/shard_map/ppermute | solution.py:20
  125.5 4.8 %collective-permute-done.45 = f32[64,128]{1,0:T(8,128)S(1)} collective-permute-done((f32[64,128]{1,0:T(8,128)S(1)}, f32[64,128]{1,0:T(8,128)S(1)}, u32[]{:S(2)}, u32[]{:S(2)}) %collective-permute-start.45) | collective-permute-done | bytes 32800 | tf_op jit(solution)/shard_map/ppermute | solution.py:20
  130.2 1.4 collective-permute-start.51
  131.6 1.3 collective-permute-start.50
  133.7 2.9 %shard_map.75 = (f32[1536,128]{1,0:T(8,128)}, f32[256,128]{1,0:T(8,128)S(1)}) custom-call(f32[1536,128]{1,0:T(8,128)} %copy-done, f32[1536,128]{1,0:T(8,128)} %get-tuple-element.118.refs_1_, bf16[1536,128]{1,0:T(8,128)(2,1)S(1)} %collective-permute-done.40.refs_2_, bf16[1536,128]{1,0:T(8,128)(2,1)S(1)} %collective-permute-done.41.refs_3_, ...), custom_call_target="tpu_custom_call" | custom-call | tf_op jit(solution)/shard_map/pallas_call | solution.py:239
  138.3 4.0 %collective-permute-done.47 = f32[128,128]{1,0:T(8,128)S(1)} collective-permute-done((f32[128,128]{1,0:T(8,128)S(1)}, f32[128,128]{1,0:T(8,128)S(1)}, u32[]{:S(2)}, u32[]{:S(2)}) %collective-permute-start.47) | collective-permute-done | bytes 65568 | tf_op jit(solution)/shard_map/ppermute | solution.py:20
  142.4 2.0 %collective-permute-start.48 = (f32[128,128]{1,0:T(8,128)S(1)}, f32[128,128]{1,0:T(8,128)S(1)}, u32[]{:S(2)}, u32[]{:S(2)}) collective-permute-start(f32[128,128]{1,0:T(8,128)S(1)} %add.142), channel_id=1, source_target_pairs={{0,16},{4,20},{8,24},{12,28},{16,0},{20,4},{24,8},{28,12},{1,17},{... | collective-permute-start | bytes 196616 | tf_op jit(solution)/shard_map/ppermute | solution.py:20
  144.4 4.9 %shard_map.76 = (f32[128,128]{1,0:T(8,128)S(1)}, f32[128,128]{1,0:T(8,128)S(1)}, f32[1536,128]{1,0:T(8,128)S(1)}) custom-call(f32[128,128]{1,0:T(8,128)S(1)} %maximum_select_fusion.1.gram_ref, f32[1536,128]{1,0:T(8,128)S(1)} %copy-done.1), custom_call_target="tpu_custom_call" | custom-call | tf_op jit(solution)/shard_map/pallas_call | solution.py:456
  151.1 1.7 %collective-permute-start.53 = (f32[128,128]{1,0:T(8,128)S(1)}, f32[128,128]{1,0:T(8,128)S(1)}, u32[]{:S(2)}, u32[]{:S(2)}) collective-permute-start(f32[128,128]{1,0:T(8,128)S(1)} %add.151), channel_id=1, source_target_pairs={{0,1},{1,0},{2,3},{3,2},{4,5},{5,4},{6,7},{7,6},{8,9},{9,8},{10,11... | collective-permute-start | bytes 196616 | tf_op jit(solution)/shard_map/ppermute | solution.py:20
  152.8 1.8 %collective-permute-done.55 = f32[128,128]{1,0:T(8,128)S(1)} collective-permute-done((f32[128,128]{1,0:T(8,128)S(1)}, f32[128,128]{1,0:T(8,128)S(1)}, u32[]{:S(2)}, u32[]{:S(2)}) %collective-permute-start.55) | collective-permute-done | bytes 65568 | tf_op jit(solution)/shard_map/ppermute | solution.py:20
  155.5 1.2 collective-permute-done.56
  156.8 7.4 %shard_map.77 = (f32[1536,256]{1,0:T(8,128)}, f32[256,256]{1,0:T(8,128)}) custom-call(f32[256,128]{1,0:T(8,128)S(1)} %maximum_select_fusion.gram_ref, f32[128,128]{1,0:T(8,128)S(1)} %get-tuple-element.125.upper_ref, f32[128,128]{1,0:T(8,128)S(1)} %get-tuple-element.127.inverse_ref, f32[1536,128]{1,0:T(8,128)S(1)} %get-tuple-element.128.first_ref, ...), custom_call_target="tpu_custom_call" | custom-call | tf_op jit(solution)/shard_map/pallas_call | solution.py:463
  (122 shorter events, 19.3 us)
Async XLA Ops:
  2.1 9.7 %collective-permute-start.8 = (bf16[64,1536]{1,0:T(8,128)(2,1)S(1)}, bf16[64,1536]{1,0:T(8,128)(2,1)S(1)}, u32[]{:S(2)}, u32[]{:S(2)}) collective-permute-start(bf16[64,1536]{1,0:T(8,128)(2,1)S(1)} %get-tuple-element.67.refs_0_), channel_id=1, source_target_pairs={{0,3},{1,2},{2,1},{3,0},{4,7},{5,6},{6,5},{7,4},{8,11},{9,10},{10,... | collective-permute-start | bytes 589832 | tf_op jit(solution)/shard_map/ppermute | solution.py:20
  6.0 9.2 %collective-permute-start.7 = (bf16[64,1536]{1,0:T(8,128)(2,1)S(1)}, bf16[64,1536]{1,0:T(8,128)(2,1)S(1)}, u32[]{:S(2)}, u32[]{:S(2)}) collective-permute-start(bf16[64,1536]{1,0:T(8,128)(2,1)S(1)} %get-tuple-element.67.refs_0_), channel_id=1, source_target_pairs={{0,2},{1,3},{2,0},{3,1},{4,6},{5,7},{6,4},{7,5},{8,10},{9,11},{10,... | collective-permute-start | bytes 589832 | tf_op jit(solution)/shard_map/ppermute | solution.py:20
  6.5 11.1 %collective-permute-start.6 = (bf16[64,1536]{1,0:T(8,128)(2,1)S(1)}, bf16[64,1536]{1,0:T(8,128)(2,1)S(1)}, u32[]{:S(2)}, u32[]{:S(2)}) collective-permute-start(bf16[64,1536]{1,0:T(8,128)(2,1)S(1)} %get-tuple-element.67.refs_0_), channel_id=1, source_target_pairs={{0,1},{1,0},{2,3},{3,2},{4,5},{5,4},{6,7},{7,6},{8,9},{9,8},{10,11... | collective-permute-start | bytes 589832 | tf_op jit(solution)/shard_map/ppermute | solution.py:20
  6.7 16.3 %collective-permute-start.3 = (bf16[48,1536]{1,0:T(8,128)(2,1)S(1)}, bf16[48,1536]{1,0:T(8,128)(2,1)S(1)}, u32[]{:S(2)}, u32[]{:S(2)}) collective-permute-start(bf16[48,1536]{1,0:T(8,128)(2,1)S(1)} %get-tuple-element.136), channel_id=1, source_target_pairs={{0,2},{1,3},{2,0},{3,1},{4,6},{5,7},{6,4},{7,5},{8,10},{9,11},{10,... | collective-permute-start | bytes 442376 | tf_op jit(solution)/shard_map/ppermute | solution.py:20
  8.7 14.3 %collective-permute-start.1 = (bf16[48,1536]{1,0:T(8,128)(2,1)S(1)}, bf16[48,1536]{1,0:T(8,128)(2,1)S(1)}, u32[]{:S(2)}, u32[]{:S(2)}) collective-permute-start(bf16[48,1536]{1,0:T(8,128)(2,1)S(1)} %get-tuple-element.136), channel_id=1, source_target_pairs={{0,1},{1,0},{2,3},{3,2},{4,5},{5,4},{6,7},{7,6},{8,9},{9,8},{10,11... | collective-permute-start | bytes 442376 | tf_op jit(solution)/shard_map/ppermute | solution.py:20
  11.8 11.2 %collective-permute-start.2 = (bf16[48,1536]{1,0:T(8,128)(2,1)S(1)}, bf16[48,1536]{1,0:T(8,128)(2,1)S(1)}, u32[]{:S(2)}, u32[]{:S(2)}) collective-permute-start(bf16[48,1536]{1,0:T(8,128)(2,1)S(1)} %get-tuple-element.137), channel_id=1, source_target_pairs={{0,2},{1,3},{2,0},{3,1},{4,6},{5,7},{6,4},{7,5},{8,10},{9,11},{10,... | collective-permute-start | bytes 442376 | tf_op jit(solution)/shard_map/ppermute | solution.py:20
  15.3 7.7 %collective-permute-start = (bf16[48,1536]{1,0:T(8,128)(2,1)S(1)}, bf16[48,1536]{1,0:T(8,128)(2,1)S(1)}, u32[]{:S(2)}, u32[]{:S(2)}) collective-permute-start(bf16[48,1536]{1,0:T(8,128)(2,1)S(1)} %get-tuple-element.137), channel_id=1, source_target_pairs={{0,1},{1,0},{2,3},{3,2},{4,5},{5,4},{6,7},{7,6},{8,9},{9,8},{10,11... | collective-permute-start | bytes 442376 | tf_op jit(solution)/shard_map/ppermute | solution.py:20
  23.1 6.3 %collective-permute-start.5 = (bf16[48,1536]{1,0:T(8,128)(2,1)S(1)}, bf16[48,1536]{1,0:T(8,128)(2,1)S(1)}, u32[]{:S(2)}, u32[]{:S(2)}) collective-permute-start(bf16[48,1536]{1,0:T(8,128)(2,1)S(1)} %collective-permute-done.1.refs_2_), channel_id=1, source_target_pairs={{0,2},{1,3},{2,0},{3,1},{4,6},{5,7},{6,4},{7,5},{8,10},{9,11},{10,... | collective-permute-start | bytes 442376 | tf_op jit(solution)/shard_map/ppermute | solution.py:20
  23.7 6.2 %collective-permute-start.4 = (bf16[48,1536]{1,0:T(8,128)(2,1)S(1)}, bf16[48,1536]{1,0:T(8,128)(2,1)S(1)}, u32[]{:S(2)}, u32[]{:S(2)}) collective-permute-start(bf16[48,1536]{1,0:T(8,128)(2,1)S(1)} %collective-permute-done.2.refs_3_), channel_id=1, source_target_pairs={{0,1},{1,0},{2,3},{3,2},{4,5},{5,4},{6,7},{7,6},{8,9},{9,8},{10,11... | collective-permute-start | bytes 442376 | tf_op jit(solution)/shard_map/ppermute | solution.py:20
  25.7 11.7 %collective-permute-start.14 = (f16[32,6144]{1,0:T(8,128)(2,1)S(1)}, f16[32,6144]{1,0:T(8,128)(2,1)S(1)}, u32[]{:S(2)}, u32[]{:S(2)}) collective-permute-start(f16[32,6144]{1,0:T(8,128)(2,1)S(1)} %multiply_convert_fusion), channel_id=1, source_target_pairs={{0,8},{4,12},{8,0},{12,4},{16,24},{20,28},{24,16},{28,20},{1,9},{5... | collective-permute-start | bytes 1179656 | tf_op jit(solution)/shard_map/ppermute | solution.py:20
  27.0 10.2 %collective-permute-start.13 = (bf16[48,1536]{1,0:T(8,128)(2,1)S(1)}, bf16[48,1536]{1,0:T(8,128)(2,1)S(1)}, u32[]{:S(2)}, u32[]{:S(2)}) collective-permute-start(bf16[48,1536]{1,0:T(8,128)(2,1)S(1)} %get-tuple-element.134), channel_id=1, source_target_pairs={{0,2},{1,3},{2,0},{3,1},{4,6},{5,7},{6,4},{7,5},{8,10},{9,11},{10,... | collective-permute-start | bytes 442376 | tf_op jit(solution)/shard_map/ppermute | solution.py:20
  28.3 9.0 %collective-permute-start.11 = (bf16[48,1536]{1,0:T(8,128)(2,1)S(1)}, bf16[48,1536]{1,0:T(8,128)(2,1)S(1)}, u32[]{:S(2)}, u32[]{:S(2)}) collective-permute-start(bf16[48,1536]{1,0:T(8,128)(2,1)S(1)} %get-tuple-element.134), channel_id=1, source_target_pairs={{0,1},{1,0},{2,3},{3,2},{4,5},{5,4},{6,7},{7,6},{8,9},{9,8},{10,11... | collective-permute-start | bytes 442376 | tf_op jit(solution)/shard_map/ppermute | solution.py:20
  29.3 7.9 %collective-permute-start.12 = (bf16[48,1536]{1,0:T(8,128)(2,1)S(1)}, bf16[48,1536]{1,0:T(8,128)(2,1)S(1)}, u32[]{:S(2)}, u32[]{:S(2)}) collective-permute-start(bf16[48,1536]{1,0:T(8,128)(2,1)S(1)} %get-tuple-element.135), channel_id=1, source_target_pairs={{0,2},{1,3},{2,0},{3,1},{4,6},{5,7},{6,4},{7,5},{8,10},{9,11},{10,... | collective-permute-start | bytes 442376 | tf_op jit(solution)/shard_map/ppermute | solution.py:20
  30.0 7.3 %collective-permute-start.10 = (bf16[48,1536]{1,0:T(8,128)(2,1)S(1)}, bf16[48,1536]{1,0:T(8,128)(2,1)S(1)}, u32[]{:S(2)}, u32[]{:S(2)}) collective-permute-start(bf16[48,1536]{1,0:T(8,128)(2,1)S(1)} %get-tuple-element.135), channel_id=1, source_target_pairs={{0,1},{1,0},{2,3},{3,2},{4,5},{5,4},{6,7},{7,6},{8,9},{9,8},{10,11... | collective-permute-start | bytes 442376 | tf_op jit(solution)/shard_map/ppermute | solution.py:20
  37.4 6.4 %collective-permute-start.18 = (bf16[48,1536]{1,0:T(8,128)(2,1)S(1)}, bf16[48,1536]{1,0:T(8,128)(2,1)S(1)}, u32[]{:S(2)}, u32[]{:S(2)}) collective-permute-start(bf16[48,1536]{1,0:T(8,128)(2,1)S(1)} %collective-permute-done.11.refs_2_), channel_id=1, source_target_pairs={{0,2},{1,3},{2,0},{3,1},{4,6},{5,7},{6,4},{7,5},{8,10},{9,11},{10,... | collective-permute-start | bytes 442376 | tf_op jit(solution)/shard_map/ppermute | solution.py:20
  37.7 6.1 %collective-permute-start.17 = (bf16[48,1536]{1,0:T(8,128)(2,1)S(1)}, bf16[48,1536]{1,0:T(8,128)(2,1)S(1)}, u32[]{:S(2)}, u32[]{:S(2)}) collective-permute-start(bf16[48,1536]{1,0:T(8,128)(2,1)S(1)} %collective-permute-done.12.refs_3_), channel_id=1, source_target_pairs={{0,1},{1,0},{2,3},{3,2},{4,5},{5,4},{6,7},{7,6},{8,9},{9,8},{10,11... | collective-permute-start | bytes 442376 | tf_op jit(solution)/shard_map/ppermute | solution.py:20
  41.7 12.2 %collective-permute-start.16 = (f16[16,6144]{1,0:T(8,128)(2,1)S(1)}, f16[16,6144]{1,0:T(8,128)(2,1)S(1)}, u32[]{:S(2)}, u32[]{:S(2)}) collective-permute-start(f16[16,6144]{1,0:T(8,128)(2,1)S(1)} %get-tuple-element.133), channel_id=1, source_target_pairs={{0,16},{4,20},{8,24},{12,28},{16,0},{20,4},{24,8},{28,12},{1,17},{... | collective-permute-start | bytes 589832 | tf_op jit(solution)/shard_map/ppermute | solution.py:20
  43.8 10.2 %collective-permute-start.19 = (f16[16,6144]{1,0:T(8,128)(2,1)S(1)}, f16[16,6144]{1,0:T(8,128)(2,1)S(1)}, u32[]{:S(2)}, u32[]{:S(2)}) collective-permute-start(f16[16,6144]{1,0:T(8,128)(2,1)S(1)} %multiply_convert_fusion.2), channel_id=1, source_target_pairs={{0,8},{4,12},{8,0},{12,4},{16,24},{20,28},{24,16},{28,20},{1,9},{5... | collective-permute-start | bytes 589832 | tf_op jit(solution)/shard_map/ppermute | solution.py:20
  54.0 5.6 %collective-permute-start.22 = (f32[48,6144]{1,0:T(8,128)}, f32[48,6144]{1,0:T(8,128)S(1)}, u32[]{:S(2)}, u32[]{:S(2)}) collective-permute-start(f32[48,6144]{1,0:T(8,128)} %get-tuple-element.95), channel_id=1, source_target_pairs={{0,4},{4,0},{8,12},{12,8},{16,20},{20,16},{24,28},{28,24},{1,5},{5... | collective-permute-start | bytes 3538952 | tf_op jit(solution)/shard_map/ppermute | solution.py:20
  55.1 12.6 %collective-permute-start.21 = (bf16[16,6144]{1,0:T(8,128)(2,1)S(1)}, bf16[16,6144]{1,0:T(8,128)(2,1)S(1)}, u32[]{:S(2)}, u32[]{:S(2)}) collective-permute-start(bf16[16,6144]{1,0:T(8,128)(2,1)S(1)} %fusion.11.refs_0_), channel_id=1, source_target_pairs={{0,16},{4,20},{8,24},{12,28},{16,0},{20,4},{24,8},{28,12},{1,17},{... | collective-permute-start | bytes 589832 | tf_op jit(solution)/shard_map/ppermute | solution.py:20
  57.1 10.7 %collective-permute-start.20 = (bf16[16,6144]{1,0:T(8,128)(2,1)S(1)}, bf16[16,6144]{1,0:T(8,128)(2,1)S(1)}, u32[]{:S(2)}, u32[]{:S(2)}) collective-permute-start(bf16[16,6144]{1,0:T(8,128)(2,1)S(1)} %fusion.11.refs_0_), channel_id=1, source_target_pairs={{0,8},{4,12},{8,0},{12,4},{16,24},{20,28},{24,16},{28,20},{1,9},{5... | collective-permute-start | bytes 589832 | tf_op jit(solution)/shard_map/ppermute | solution.py:20
  67.7 9.2 %collective-permute-start.23 = (bf16[16,6144]{1,0:T(8,128)(2,1)S(1)}, bf16[16,6144]{1,0:T(8,128)(2,1)S(1)}, u32[]{:S(2)}, u32[]{:S(2)}) collective-permute-start(bf16[16,6144]{1,0:T(8,128)(2,1)S(1)} %collective-permute-done.21.refs_2_), channel_id=1, source_target_pairs={{0,8},{4,12},{8,0},{12,4},{16,24},{20,28},{24,16},{28,20},{1,9},{5... | collective-permute-start | bytes 589832 | tf_op jit(solution)/shard_map/ppermute | solution.py:20
  67.7 9.2 %collective-permute-start.24 = (bf16[16,6144]{1,0:T(8,128)(2,1)S(1)}, bf16[16,6144]{1,0:T(8,128)(2,1)S(1)}, u32[]{:S(2)}, u32[]{:S(2)}) collective-permute-start(bf16[16,6144]{1,0:T(8,128)(2,1)S(1)} %fusion.11.refs_0_), channel_id=1, source_target_pairs={{0,4},{4,0},{8,12},{12,8},{16,20},{20,16},{24,28},{28,24},{1,5},{5... | collective-permute-start | bytes 589832 | tf_op jit(solution)/shard_map/ppermute | solution.py:20
  67.8 9.2 %collective-permute-start.25 = (bf16[16,6144]{1,0:T(8,128)(2,1)S(1)}, bf16[16,6144]{1,0:T(8,128)(2,1)S(1)}, u32[]{:S(2)}, u32[]{:S(2)}) collective-permute-start(bf16[16,6144]{1,0:T(8,128)(2,1)S(1)} %collective-permute-done.20.refs_1_), channel_id=1, source_target_pairs={{0,4},{4,0},{8,12},{12,8},{16,20},{20,16},{24,28},{28,24},{1,5},{5... | collective-permute-start | bytes 589832 | tf_op jit(solution)/shard_map/ppermute | solution.py:20
  68.2 8.8 %collective-permute-start.26 = (bf16[16,6144]{1,0:T(8,128)(2,1)S(1)}, bf16[16,6144]{1,0:T(8,128)(2,1)S(1)}, u32[]{:S(2)}, u32[]{:S(2)}) collective-permute-start(bf16[16,6144]{1,0:T(8,128)(2,1)S(1)} %collective-permute-done.21.refs_2_), channel_id=1, source_target_pairs={{0,4},{4,0},{8,12},{12,8},{16,20},{20,16},{24,28},{28,24},{1,5},{5... | collective-permute-start | bytes 589832 | tf_op jit(solution)/shard_map/ppermute | solution.py:20
  68.3 16.9 %collective-permute-start.31 = (f16[16,6144]{1,0:T(8,128)(2,1)S(1)}, f16[16,6144]{1,0:T(8,128)(2,1)S(1)}, u32[]{:S(2)}, u32[]{:S(2)}) collective-permute-start(f16[16,6144]{1,0:T(8,128)(2,1)S(1)} %get-tuple-element.131), channel_id=1, source_target_pairs={{0,16},{4,20},{8,24},{12,28},{16,0},{20,4},{24,8},{28,12},{1,17},{... | collective-permute-start | bytes 589832 | tf_op jit(solution)/shard_map/ppermute | solution.py:20
  76.9 8.7 %collective-permute-start.32 = (f16[16,6144]{1,0:T(8,128)(2,1)S(1)}, f16[16,6144]{1,0:T(8,128)(2,1)S(1)}, u32[]{:S(2)}, u32[]{:S(2)}) collective-permute-start(f16[16,6144]{1,0:T(8,128)(2,1)S(1)} %multiply_convert_fusion.1), channel_id=1, source_target_pairs={{0,8},{4,12},{8,0},{12,4},{16,24},{20,28},{24,16},{28,20},{1,9},{5... | collective-permute-start | bytes 589832 | tf_op jit(solution)/shard_map/ppermute | solution.py:20
  85.8 11.6 %collective-permute-start.34 = (bf16[16,6144]{1,0:T(8,128)(2,1)S(1)}, bf16[16,6144]{1,0:T(8,128)(2,1)S(1)}, u32[]{:S(2)}, u32[]{:S(2)}) collective-permute-start(bf16[16,6144]{1,0:T(8,128)(2,1)S(1)} %fusion.2.refs_0_), channel_id=1, source_target_pairs={{0,16},{4,20},{8,24},{12,28},{16,0},{20,4},{24,8},{28,12},{1,17},{... | collective-permute-start | bytes 589832 | tf_op jit(solution)/shard_map/ppermute | solution.py:20
  86.1 18.1 %collective-permute-start.28 = (bf16[1536,128]{1,0:T(8,128)(2,1)S(1)}, bf16[1536,128]{1,0:T(8,128)(2,1)S(1)}, u32[]{:S(2)}, u32[]{:S(2)}) collective-permute-start(bf16[1536,128]{1,0:T(8,128)(2,1)S(1)} %get-tuple-element.99), channel_id=1, source_target_pairs={{0,1},{1,0},{2,3},{3,2},{4,5},{5,4},{6,7},{7,6},{8,9},{9,8},{10,11... | collective-permute-start | bytes 1179656 | tf_op jit(solution)/shard_map/ppermute | solution.py:20
  88.0 16.2 %collective-permute-start.29 = (bf16[1536,128]{1,0:T(8,128)(2,1)S(1)}, bf16[1536,128]{1,0:T(8,128)(2,1)S(1)}, u32[]{:S(2)}, u32[]{:S(2)}) collective-permute-start(bf16[1536,128]{1,0:T(8,128)(2,1)S(1)} %copy-done.9), channel_id=1, source_target_pairs={{0,2},{1,3},{2,0},{3,1},{4,6},{5,7},{6,4},{7,5},{8,10},{9,11},{10,... | collective-permute-start | bytes 1179656 | tf_op jit(solution)/shard_map/ppermute | solution.py:20
  88.7 10.3 %collective-permute-start.33 = (bf16[16,6144]{1,0:T(8,128)(2,1)S(1)}, bf16[16,6144]{1,0:T(8,128)(2,1)S(1)}, u32[]{:S(2)}, u32[]{:S(2)}) collective-permute-start(bf16[16,6144]{1,0:T(8,128)(2,1)S(1)} %fusion.2.refs_0_), channel_id=1, source_target_pairs={{0,8},{4,12},{8,0},{12,4},{16,24},{20,28},{24,16},{28,20},{1,9},{5... | collective-permute-start | bytes 589832 | tf_op jit(solution)/shard_map/ppermute | solution.py:20
  97.4 6.8 %collective-permute-start.35 = (bf16[16,6144]{1,0:T(8,128)(2,1)S(1)}, bf16[16,6144]{1,0:T(8,128)(2,1)S(1)}, u32[]{:S(2)}, u32[]{:S(2)}) collective-permute-start(bf16[16,6144]{1,0:T(8,128)(2,1)S(1)} %collective-permute-done.34.refs_2_), channel_id=1, source_target_pairs={{0,8},{4,12},{8,0},{12,4},{16,24},{20,28},{24,16},{28,20},{1,9},{5... | collective-permute-start | bytes 589832 | tf_op jit(solution)/shard_map/ppermute | solution.py:20
  97.4 15.9 %collective-permute-start.30 = (bf16[1536,128]{1,0:T(8,128)(2,1)S(1)}, bf16[1536,128]{1,0:T(8,128)(2,1)S(1)}, u32[]{:S(2)}, u32[]{:S(2)}) collective-permute-start(bf16[1536,128]{1,0:T(8,128)(2,1)S(1)} %copy-done.8), channel_id=1, source_target_pairs={{0,3},{1,2},{2,1},{3,0},{4,7},{5,6},{6,5},{7,4},{8,11},{9,10},{10,... | collective-permute-start | bytes 1179656 | tf_op jit(solution)/shard_map/ppermute | solution.py:20
  98.9 5.9 %collective-permute-start.36 = (bf16[16,6144]{1,0:T(8,128)(2,1)S(1)}, bf16[16,6144]{1,0:T(8,128)(2,1)S(1)}, u32[]{:S(2)}, u32[]{:S(2)}) collective-permute-start(bf16[16,6144]{1,0:T(8,128)(2,1)S(1)} %fusion.2.refs_0_), channel_id=1, source_target_pairs={{0,4},{4,0},{8,12},{12,8},{16,20},{20,16},{24,28},{28,24},{1,5},{5... | collective-permute-start | bytes 589832 | tf_op jit(solution)/shard_map/ppermute | solution.py:20
  113.3 12.1 %collective-permute-start.40 = (bf16[1536,128]{1,0:T(8,128)(2,1)S(1)}, bf16[1536,128]{1,0:T(8,128)(2,1)S(1)}, u32[]{:S(2)}, u32[]{:S(2)}) collective-permute-start(bf16[1536,128]{1,0:T(8,128)(2,1)S(1)} %get-tuple-element.111), channel_id=1, source_target_pairs={{0,1},{1,0},{2,3},{3,2},{4,5},{5,4},{6,7},{7,6},{8,9},{9,8},{10,11... | collective-permute-start | bytes 1179656 | tf_op jit(solution)/shard_map/ppermute | solution.py:20
  114.6 19.1 %collective-permute-start.41 = (bf16[1536,128]{1,0:T(8,128)(2,1)}, bf16[1536,128]{1,0:T(8,128)(2,1)S(1)}, u32[]{:S(2)}, u32[]{:S(2)}) collective-permute-start(bf16[1536,128]{1,0:T(8,128)(2,1)} %get-tuple-element.112), channel_id=1, source_target_pairs={{0,2},{1,3},{2,0},{3,1},{4,6},{5,7},{6,4},{7,5},{8,10},{9,11},{10,... | collective-permute-start | bytes 1179656 | tf_op jit(solution)/shard_map/ppermute | solution.py:20
  115.4 18.4 %collective-permute-start.42 = (bf16[1536,128]{1,0:T(8,128)(2,1)}, bf16[1536,128]{1,0:T(8,128)(2,1)S(1)}, u32[]{:S(2)}, u32[]{:S(2)}) collective-permute-start(bf16[1536,128]{1,0:T(8,128)(2,1)} %get-tuple-element.113), channel_id=1, source_target_pairs={{0,3},{1,2},{2,1},{3,0},{4,7},{5,6},{6,5},{7,4},{8,11},{9,10},{10,... | collective-permute-start | bytes 1179656 | tf_op jit(solution)/shard_map/ppermute | solution.py:20
  121.0 3.9 %collective-permute-start.44 = (f32[64,128]{1,0:T(8,128)S(1)}, f32[64,128]{1,0:T(8,128)S(1)}, u32[]{:S(2)}, u32[]{:S(2)}) collective-permute-start(f32[64,128]{1,0:T(8,128)S(1)} %dynamic-slice_add_fusion.1), channel_id=1, source_target_pairs={{0,8},{4,12},{8,0},{12,4},{16,24},{20,28},{24,16},{28,20},{1,9},{5... | collective-permute-start | bytes 98312 | tf_op jit(solution)/shard_map/ppermute | solution.py:20
  125.4 4.8 %collective-permute-start.45 = (f32[64,128]{1,0:T(8,128)S(1)}, f32[64,128]{1,0:T(8,128)S(1)}, u32[]{:S(2)}, u32[]{:S(2)}) collective-permute-start(f32[64,128]{1,0:T(8,128)S(1)} %add.137), channel_id=1, source_target_pairs={{0,16},{4,20},{8,24},{12,28},{16,0},{20,4},{24,8},{28,12},{1,17},{... | collective-permute-start | bytes 98312 | tf_op jit(solution)/shard_map/ppermute | solution.py:20
  130.2 6.5 %collective-permute-start.51 = (f32[64,128]{1,0:T(8,128)S(1)}, f32[64,128]{1,0:T(8,128)S(1)}, u32[]{:S(2)}, u32[]{:S(2)}) collective-permute-start(f32[64,128]{1,0:T(8,128)S(1)} %add.138), channel_id=1, source_target_pairs={{0,3},{1,2},{2,1},{3,0},{4,7},{5,6},{6,5},{7,4},{8,11},{9,10},{10,... | collective-permute-start | bytes 98312 | tf_op jit(solution)/shard_map/ppermute | solution.py:20
  131.6 5.1 %collective-permute-start.50 = (f32[64,128]{1,0:T(8,128)S(1)}, f32[64,128]{1,0:T(8,128)S(1)}, u32[]{:S(2)}, u32[]{:S(2)}) collective-permute-start(f32[64,128]{1,0:T(8,128)S(1)} %add.138), channel_id=1, source_target_pairs={{0,2},{1,3},{2,0},{3,1},{4,6},{5,7},{6,4},{7,5},{8,10},{9,11},{10,... | collective-permute-start | bytes 98312 | tf_op jit(solution)/shard_map/ppermute | solution.py:20
  132.9 3.9 %collective-permute-start.49 = (f32[64,128]{1,0:T(8,128)S(1)}, f32[64,128]{1,0:T(8,128)S(1)}, u32[]{:S(2)}, u32[]{:S(2)}) collective-permute-start(f32[64,128]{1,0:T(8,128)S(1)} %add.138), channel_id=1, source_target_pairs={{0,1},{1,0},{2,3},{3,2},{4,5},{5,4},{6,7},{7,6},{8,9},{9,8},{10,11... | collective-permute-start | bytes 98312 | tf_op jit(solution)/shard_map/ppermute | solution.py:20
  138.0 4.3 %collective-permute-start.47 = (f32[128,128]{1,0:T(8,128)S(1)}, f32[128,128]{1,0:T(8,128)S(1)}, u32[]{:S(2)}, u32[]{:S(2)}) collective-permute-start(f32[128,128]{1,0:T(8,128)S(1)} %dynamic-slice_add_fusion), channel_id=1, source_target_pairs={{0,8},{4,12},{8,0},{12,4},{16,24},{20,28},{24,16},{28,20},{1,9},{5... | collective-permute-start | bytes 196616 | tf_op jit(solution)/shard_map/ppermute | solution.py:20
  138.1 6.2 %collective-permute-start.52 = (f32[64,128]{1,0:T(8,128)S(1)}, f32[64,128]{1,0:T(8,128)S(1)}, u32[]{:S(2)}, u32[]{:S(2)}) collective-permute-start(f32[64,128]{1,0:T(8,128)S(1)} %add_bitcast_fusion.1), channel_id=1, source_target_pairs={{0,4},{4,0},{8,12},{12,8},{16,20},{20,16},{24,28},{28,24},{1,5},{5... | collective-permute-start | bytes 98312 | tf_op jit(solution)/shard_map/ppermute | solution.py:20
  142.4 6.9 %collective-permute-start.48 = (f32[128,128]{1,0:T(8,128)S(1)}, f32[128,128]{1,0:T(8,128)S(1)}, u32[]{:S(2)}, u32[]{:S(2)}) collective-permute-start(f32[128,128]{1,0:T(8,128)S(1)} %add.142), channel_id=1, source_target_pairs={{0,16},{4,20},{8,24},{12,28},{16,0},{20,4},{24,8},{28,12},{1,17},{... | collective-permute-start | bytes 196616 | tf_op jit(solution)/shard_map/ppermute | solution.py:20
  149.3 5.3 %collective-permute-start.55 = (f32[128,128]{1,0:T(8,128)S(1)}, f32[128,128]{1,0:T(8,128)S(1)}, u32[]{:S(2)}, u32[]{:S(2)}) collective-permute-start(f32[128,128]{1,0:T(8,128)S(1)} %add.151), channel_id=1, source_target_pairs={{0,3},{1,2},{2,1},{3,0},{4,7},{5,6},{6,5},{7,4},{8,11},{9,10},{10,... | collective-permute-start | bytes 196616 | tf_op jit(solution)/shard_map/ppermute | solution.py:20
  150.0 5.0 %collective-permute-start.54 = (f32[128,128]{1,0:T(8,128)S(1)}, f32[128,128]{1,0:T(8,128)S(1)}, u32[]{:S(2)}, u32[]{:S(2)}) collective-permute-start(f32[128,128]{1,0:T(8,128)S(1)} %add.151), channel_id=1, source_target_pairs={{0,2},{1,3},{2,0},{3,1},{4,6},{5,7},{6,4},{7,5},{8,10},{9,11},{10,... | collective-permute-start | bytes 196616 | tf_op jit(solution)/shard_map/ppermute | solution.py:20
  151.1 4.3 %collective-permute-start.53 = (f32[128,128]{1,0:T(8,128)S(1)}, f32[128,128]{1,0:T(8,128)S(1)}, u32[]{:S(2)}, u32[]{:S(2)}) collective-permute-start(f32[128,128]{1,0:T(8,128)S(1)} %add.151), channel_id=1, source_target_pairs={{0,1},{1,0},{2,3},{3,2},{4,5},{5,4},{6,7},{7,6},{8,9},{9,8},{10,11... | collective-permute-start | bytes 196616 | tf_op jit(solution)/shard_map/ppermute | solution.py:20
  (20 other events, 111.0 us)

commit v6 on v5

--- a/solution.py
+++ b/solution.py
@@ -386,9 +386,9 @@
     factor_ref[split:, split:] = upper
     first = first_ref[...]
     basis_ref[:, :split] = first
-    basis_ref[:, split:] = product(rows_ref[...], inverse, 1, 1) - product(
-        first, product(corner, inverse, 1, 1), 1, 0
-    )
+    rows = jnp.concatenate([rows_ref[...], first], axis=1)
+    blocks = jnp.concatenate([inverse, -product(inverse, corner, 1, 1)], axis=1)
+    basis_ref[:, split:] = product(rows, blocks, 1, 1)
 
 
 def body(tiles, tile_rows, tile_cols, tile_counts, sketch):

time: 164 us -> 165 us (level)
  Pallas kernels: 48.4 us -> 43 us
  starting transfers between devices: 53.6 us -> 58.1 us
    pallas_call x5, Pallas kernels: 30.9 us -> 25.3 us  [tile_call(): pl.pallas_call(kernel, out_shape=out_shape, in_specs=[smem, pl.BlockSpec(...]
    ppermute x57, starting transfers between devices: 53.6 us -> 58.1 us  [swap(): return lax.ppermute(value, axis, [(i, i ^ offset) for i in range(size)])]
    ppermute x57, waiting for transfers between devices: 55.2 us -> 56.8 us  [swap(): return lax.ppermute(value, axis, [(i, i ^ offset) for i in range(size)])]
  transfers between devices with their start and end apart: 57 -> 57, of which waited for: 29 -> 27; matrix products, arithmetic and copies ran while one was open for 2% -> 2% of each run, Pallas kernels for 25% -> 21%
where the time goes in v6:
time: 165 us
  starting transfers between devices  58.1 us (35%)
  waiting for transfers between devices  56.8 us (34%)
  Pallas kernels  43 us (26%)
  other arithmetic  2.99 us (2%)
  local copies, waits for them, and re-layouts  2.09 us (1%)
  between operations  1.77 us (1%)
    ppermute x57, starting transfers between devices, swap(): return lax.ppermute(value, axis, [(i, i ^ offset) for i in range(size)])  58.1 us
    ppermute x57, waiting for transfers between devices, swap(): return lax.ppermute(value, axis, [(i, i ^ offset) for i in range(size)])  56.8 us
    pallas_call x5, Pallas kernels, tile_call(): pl.pallas_call(kernel, out_shape=out_shape, in_specs=[smem, pl.BlockSpec(...  25.3 us
    pallas_call x1, Pallas kernels, body(): pl.pallas_call(functools.partial(second_factor_kernel, total_rows), out_s...  7.55 us
    pallas_call x2, Pallas kernels, finish_call(): pl.pallas_call(functools.partial(finish_kernel, len(parts)), out_shape=(j...  4.97 us
    pallas_call x1, Pallas kernels, body(): pl.pallas_call(functools.partial(first_factor_kernel, total_rows), out_sh...  4.88 us
  transfers between devices with their start and end apart: 57, of which 27 were waited for; matrix products, arithmetic and copies ran while one was open for 2% of the time, Pallas kernels for 21%

profile of v6, /device:TPU:0, one launch (start us, length us, event | category | flops | bytes accessed | tf_op | source)
XLA Modules:
  0.0 164.8 jit_solution(17341490299486751574)
XLA Ops:
  2.1 4.0 %collective-permute-start.8 = (bf16[64,1536]{1,0:T(8,128)(2,1)S(1)}, bf16[64,1536]{1,0:T(8,128)(2,1)S(1)}, u32[]{:S(2)}, u32[]{:S(2)}) collective-permute-start(bf16[64,1536]{1,0:T(8,128)(2,1)S(1)} %get-tuple-element.67.refs_0_), channel_id=1, source_target_pairs={{0,3},{1,2},{2,1},{3,0},{4,7},{5,6},{6,5},{7,4},{8,11},{9,10},{10,... | collective-permute-start | bytes 589832 | tf_op jit(solution)/shard_map/ppermute | solution.py:20
  6.7 2.0 %collective-permute-start.3 = (bf16[48,1536]{1,0:T(8,128)(2,1)S(1)}, bf16[48,1536]{1,0:T(8,128)(2,1)S(1)}, u32[]{:S(2)}, u32[]{:S(2)}) collective-permute-start(bf16[48,1536]{1,0:T(8,128)(2,1)S(1)} %get-tuple-element.136), channel_id=1, source_target_pairs={{0,2},{1,3},{2,0},{3,1},{4,6},{5,7},{6,4},{7,5},{8,10},{9,11},{10,... | collective-permute-start | bytes 442376 | tf_op jit(solution)/shard_map/ppermute | solution.py:20
  8.7 1.5 collective-permute-start.1
  10.2 1.6 collective-permute-done.8.refs_3_
  11.8 2.0 %collective-permute-start.2 = (bf16[48,1536]{1,0:T(8,128)(2,1)S(1)}, bf16[48,1536]{1,0:T(8,128)(2,1)S(1)}, u32[]{:S(2)}, u32[]{:S(2)}) collective-permute-start(bf16[48,1536]{1,0:T(8,128)(2,1)S(1)} %get-tuple-element.137), channel_id=1, source_target_pairs={{0,2},{1,3},{2,0},{3,1},{4,6},{5,7},{6,4},{7,5},{8,10},{9,11},{10,... | collective-permute-start | bytes 442376 | tf_op jit(solution)/shard_map/ppermute | solution.py:20
  13.8 1.4 collective-permute-done.7.refs_2_
  15.3 1.7 %collective-permute-start = (bf16[48,1536]{1,0:T(8,128)(2,1)S(1)}, bf16[48,1536]{1,0:T(8,128)(2,1)S(1)}, u32[]{:S(2)}, u32[]{:S(2)}) collective-permute-start(bf16[48,1536]{1,0:T(8,128)(2,1)S(1)} %get-tuple-element.137), channel_id=1, source_target_pairs={{0,1},{1,0},{2,3},{3,2},{4,5},{5,4},{6,7},{7,6},{8,9},{9,8},{10,11... | collective-permute-start | bytes 442376 | tf_op jit(solution)/shard_map/ppermute | solution.py:20
  17.7 4.3 %shard_map.69 = (f32[32,6144]{1,0:T(8,128)S(1)}, f32[32,6144]{1,0:T(8,128)}) custom-call(s32[33]{0:T(128)S(1)} %pad_add_fusion.layout_ref, bf16[16,512,512]{2,1,0:T(8,128)(2,1)} %bitcast.17, bf16[64,1536]{1,0:T(8,128)(2,1)S(1)} %get-tuple-element.67.refs_0_, bf16[64,1536]{1,0:T(8,128)(2,1)S(1)} %collective-permute-done.6.refs_1_, ...), custom_call_target="tpu_custom_call" | custom-call | tf_op jit(solution)/shard_map/pallas_call | solution.py:147
  22.1 1.6 collective-permute-start.5
  23.7 1.5 collective-permute-start.4
  26.0 1.7 %collective-permute-start.13 = (bf16[48,1536]{1,0:T(8,128)(2,1)S(1)}, bf16[48,1536]{1,0:T(8,128)(2,1)S(1)}, u32[]{:S(2)}, u32[]{:S(2)}) collective-permute-start(bf16[48,1536]{1,0:T(8,128)(2,1)S(1)} %get-tuple-element.134), channel_id=1, source_target_pairs={{0,2},{1,3},{2,0},{3,1},{4,6},{5,7},{6,4},{7,5},{8,10},{9,11},{10,... | collective-permute-start | bytes 442376 | tf_op jit(solution)/shard_map/ppermute | solution.py:20
  28.4 1.5 collective-permute-start.12
  30.0 1.9 %collective-permute-start.10 = (bf16[48,1536]{1,0:T(8,128)(2,1)S(1)}, bf16[48,1536]{1,0:T(8,128)(2,1)S(1)}, u32[]{:S(2)}, u32[]{:S(2)}) collective-permute-start(bf16[48,1536]{1,0:T(8,128)(2,1)S(1)} %get-tuple-element.135), channel_id=1, source_target_pairs={{0,1},{1,0},{2,3},{3,2},{4,5},{5,4},{6,7},{7,6},{8,9},{9,8},{10,11... | collective-permute-start | bytes 442376 | tf_op jit(solution)/shard_map/ppermute | solution.py:20
  31.9 4.9 %shard_map.70 = (f32[48,6144]{1,0:T(8,128)}, f32[48,6144]{1,0:T(8,128)}) custom-call(s32[33]{0:T(128)S(1)} %pad_add_fusion.layout_ref, bf16[16,512,512]{2,1,0:T(8,128)(2,1)} %bitcast.18, bf16[96,1536]{1,0:T(8,128)(2,1)S(1)} %get-tuple-element.71.refs_0_, bf16[48,1536]{1,0:T(8,128)(2,1)S(1)} %collective-permute-done.refs_1_, ...), custom_call_target="tpu_custom_call" | custom-call | tf_op jit(solution)/shard_map/pallas_call | solution.py:147
  37.5 1.5 collective-permute-start.17
  41.2 2.9 %collective-permute-start.16 = (f16[16,6144]{1,0:T(8,128)(2,1)S(1)}, f16[16,6144]{1,0:T(8,128)(2,1)S(1)}, u32[]{:S(2)}, u32[]{:S(2)}) collective-permute-start(f16[16,6144]{1,0:T(8,128)(2,1)S(1)} %get-tuple-element.133), channel_id=1, source_target_pairs={{0,16},{4,20},{8,24},{12,28},{16,0},{20,4},{24,8},{28,12},{1,17},{... | collective-permute-start | bytes 589832 | tf_op jit(solution)/shard_map/ppermute | solution.py:20
  44.2 1.3 collective-permute-start.19
  45.4 4.9 %shard_map.71 = (f32[48,6144]{1,0:T(8,128)}, f32[48,6144]{1,0:T(8,128)}) custom-call(s32[33]{0:T(128)S(1)} %pad_add_fusion.layout_ref, bf16[16,512,512]{2,1,0:T(8,128)(2,1)} %bitcast.19, bf16[96,1536]{1,0:T(8,128)(2,1)S(1)} %get-tuple-element.84.refs_0_, bf16[48,1536]{1,0:T(8,128)(2,1)S(1)} %collective-permute-done.10.refs_1_, ...), custom_call_target="tpu_custom_call" | custom-call | tf_op jit(solution)/shard_map/pallas_call | solution.py:147
  50.3 3.3 %collective-permute-done.16 = f16[16,6144]{1,0:T(8,128)(2,1)S(1)} collective-permute-done((f16[16,6144]{1,0:T(8,128)(2,1)S(1)}, f16[16,6144]{1,0:T(8,128)(2,1)S(1)}, u32[]{:S(2)}, u32[]{:S(2)}) %collective-permute-start.16) | collective-permute-done | bytes 196640 | tf_op jit(solution)/shard_map/ppermute | solution.py:20
  55.5 1.7 %collective-permute-start.21 = (bf16[16,6144]{1,0:T(8,128)(2,1)S(1)}, bf16[16,6144]{1,0:T(8,128)(2,1)S(1)}, u32[]{:S(2)}, u32[]{:S(2)}) collective-permute-start(bf16[16,6144]{1,0:T(8,128)(2,1)S(1)} %fusion.11.refs_0_), channel_id=1, source_target_pairs={{0,16},{4,20},{8,24},{12,28},{16,0},{20,4},{24,8},{28,12},{1,17},{... | collective-permute-start | bytes 589832 | tf_op jit(solution)/shard_map/ppermute | solution.py:20
  57.2 2.5 %collective-permute-start.20 = (bf16[16,6144]{1,0:T(8,128)(2,1)S(1)}, bf16[16,6144]{1,0:T(8,128)(2,1)S(1)}, u32[]{:S(2)}, u32[]{:S(2)}) collective-permute-start(bf16[16,6144]{1,0:T(8,128)(2,1)S(1)} %fusion.11.refs_0_), channel_id=1, source_target_pairs={{0,8},{4,12},{8,0},{12,4},{16,24},{20,28},{24,16},{28,20},{1,9},{5... | collective-permute-start | bytes 589832 | tf_op jit(solution)/shard_map/ppermute | solution.py:20
  59.8 8.2 %collective-permute-done.21.refs_2_ = bf16[16,6144]{1,0:T(8,128)(2,1)S(1)} collective-permute-done((bf16[16,6144]{1,0:T(8,128)(2,1)S(1)}, bf16[16,6144]{1,0:T(8,128)(2,1)S(1)}, u32[]{:S(2)}, u32[]{:S(2)}) %collective-permute-start.21) | collective-permute-done | bytes 196640 | tf_op jit(solution)/shard_map/ppermute | solution.py:20
  68.7 3.0 %collective-permute-start.31 = (f16[16,6144]{1,0:T(8,128)(2,1)S(1)}, f16[16,6144]{1,0:T(8,128)(2,1)S(1)}, u32[]{:S(2)}, u32[]{:S(2)}) collective-permute-start(f16[16,6144]{1,0:T(8,128)(2,1)S(1)} %get-tuple-element.131), channel_id=1, source_target_pairs={{0,16},{4,20},{8,24},{12,28},{16,0},{20,4},{24,8},{28,12},{1,17},{... | collective-permute-start | bytes 589832 | tf_op jit(solution)/shard_map/ppermute | solution.py:20
  71.7 5.5 %collective-permute-done.23.refs_3_ = bf16[16,6144]{1,0:T(8,128)(2,1)S(1)} collective-permute-done((bf16[16,6144]{1,0:T(8,128)(2,1)S(1)}, bf16[16,6144]{1,0:T(8,128)(2,1)S(1)}, u32[]{:S(2)}, u32[]{:S(2)}) %collective-permute-start.23) | collective-permute-done | bytes 196640 | tf_op jit(solution)/shard_map/ppermute | solution.py:20
  77.4 1.3 collective-permute-done.27.refs_7_
  78.7 5.5 %shard_map.72 = (f32[1536,128]{1,0:T(8,128)}, bf16[1536,128]{1,0:T(8,128)(2,1)S(1)}, bf16[1536,128]{1,0:T(8,128)(2,1)}, bf16[1536,128]{1,0:T(8,128)(2,1)}) custom-call(s32[33]{0:T(128)S(1)} %pad_add_fusion.layout_ref, bf16[16,512,512]{2,1,0:T(8,128)(2,1)} %bitcast.20, bf16[16,6144]{1,0:T(8,128)(2,1)S(1)} %fusion.11.refs_0_, ...), custom_call_target="tpu_custom_call" | custom-call | tf_op jit(solution)/shard_map/pallas_call | solution.py:147
  84.2 1.6 collective-permute-done.32
  86.3 1.8 %collective-permute-start.28 = (bf16[1536,128]{1,0:T(8,128)(2,1)S(1)}, bf16[1536,128]{1,0:T(8,128)(2,1)S(1)}, u32[]{:S(2)}, u32[]{:S(2)}) collective-permute-start(bf16[1536,128]{1,0:T(8,128)(2,1)S(1)} %get-tuple-element.99), channel_id=1, source_target_pairs={{0,1},{1,0},{2,3},{3,2},{4,5},{5,4},{6,7},{7,6},{8,9},{9,8},{10,11... | collective-permute-start | bytes 1179656 | tf_op jit(solution)/shard_map/ppermute | solution.py:20
  89.1 2.4 %collective-permute-start.33 = (bf16[16,6144]{1,0:T(8,128)(2,1)S(1)}, bf16[16,6144]{1,0:T(8,128)(2,1)S(1)}, u32[]{:S(2)}, u32[]{:S(2)}) collective-permute-start(bf16[16,6144]{1,0:T(8,128)(2,1)S(1)} %fusion.2.refs_0_), channel_id=1, source_target_pairs={{0,8},{4,12},{8,0},{12,4},{16,24},{20,28},{24,16},{28,20},{1,9},{5... | collective-permute-start | bytes 589832 | tf_op jit(solution)/shard_map/ppermute | solution.py:20
  91.6 5.9 %collective-permute-done.34.refs_2_ = bf16[16,6144]{1,0:T(8,128)(2,1)S(1)} collective-permute-done((bf16[16,6144]{1,0:T(8,128)(2,1)S(1)}, bf16[16,6144]{1,0:T(8,128)(2,1)S(1)}, u32[]{:S(2)}, u32[]{:S(2)}) %collective-permute-start.34) | collective-permute-done | bytes 196640 | tf_op jit(solution)/shard_map/ppermute | solution.py:20
  97.5 1.9 %collective-permute-start.30 = (bf16[1536,128]{1,0:T(8,128)(2,1)S(1)}, bf16[1536,128]{1,0:T(8,128)(2,1)S(1)}, u32[]{:S(2)}, u32[]{:S(2)}) collective-permute-start(bf16[1536,128]{1,0:T(8,128)(2,1)S(1)} %copy-done.8), channel_id=1, source_target_pairs={{0,3},{1,2},{2,1},{3,0},{4,7},{5,6},{6,5},{7,4},{8,11},{9,10},{10,... | collective-permute-start | bytes 1179656 | tf_op jit(solution)/shard_map/ppermute | solution.py:20
  100.0 4.3 %collective-permute-done.35.refs_3_ = bf16[16,6144]{1,0:T(8,128)(2,1)S(1)} collective-permute-done((bf16[16,6144]{1,0:T(8,128)(2,1)S(1)}, bf16[16,6144]{1,0:T(8,128)(2,1)S(1)}, u32[]{:S(2)}, u32[]{:S(2)}) %collective-permute-start.35) | collective-permute-done | bytes 196640 | tf_op jit(solution)/shard_map/ppermute | solution.py:20
  106.3 5.7 %shard_map.73 = (f32[1536,128]{1,0:T(8,128)}, bf16[1536,128]{1,0:T(8,128)(2,1)S(1)}, bf16[1536,128]{1,0:T(8,128)(2,1)}, bf16[1536,128]{1,0:T(8,128)(2,1)}) custom-call(s32[33]{0:T(128)S(1)} %pad_add_fusion.layout_ref, bf16[16,512,512]{2,1,0:T(8,128)(2,1)} %bitcast.21, bf16[16,6144]{1,0:T(8,128)(2,1)S(1)} %fusion.2.refs_0_, ...), custom_call_target="tpu_custom_call" | custom-call | tf_op jit(solution)/shard_map/pallas_call | solution.py:147
  112.0 1.6 collective-permute-start.40
  113.6 1.7 %collective-permute-start.41 = (bf16[1536,128]{1,0:T(8,128)(2,1)}, bf16[1536,128]{1,0:T(8,128)(2,1)S(1)}, u32[]{:S(2)}, u32[]{:S(2)}) collective-permute-start(bf16[1536,128]{1,0:T(8,128)(2,1)} %get-tuple-element.112), channel_id=1, source_target_pairs={{0,2},{1,3},{2,0},{3,1},{4,6},{5,7},{6,4},{7,5},{8,10},{9,11},{10,... | collective-permute-start | bytes 1179656 | tf_op jit(solution)/shard_map/ppermute | solution.py:20
  115.5 2.0 %shard_map.74 = (f32[1536,128]{1,0:T(8,128)S(1)}, f32[128,128]{1,0:T(8,128)S(1)}) custom-call(f32[1536,128]{1,0:T(8,128)} %get-tuple-element.98.refs_0_, bf16[1536,128]{1,0:T(8,128)(2,1)S(1)} %collective-permute-done.28.refs_1_, bf16[1536,128]{1,0:T(8,128)(2,1)S(1)} %collective-permute-done.29.refs_2_, bf16[1536,128]{1,0:T(8,128)(2,1)S(1)} %collective-permute-done.30.refs_3_), custom_call_target="tpu_custom_call" | custom-call | tf_op jit(solution)/shard_map/pallas_call | solution.py:239
  120.2 3.4 %collective-permute-done.44 = f32[64,128]{1,0:T(8,128)S(1)} collective-permute-done((f32[64,128]{1,0:T(8,128)S(1)}, f32[64,128]{1,0:T(8,128)S(1)}, u32[]{:S(2)}, u32[]{:S(2)}) %collective-permute-start.44) | collective-permute-done | bytes 32800 | tf_op jit(solution)/shard_map/ppermute | solution.py:20
  124.0 1.4 collective-permute-start.45
  125.4 3.4 %collective-permute-done.45 = f32[64,128]{1,0:T(8,128)S(1)} collective-permute-done((f32[64,128]{1,0:T(8,128)S(1)}, f32[64,128]{1,0:T(8,128)S(1)}, u32[]{:S(2)}, u32[]{:S(2)}) %collective-permute-start.45) | collective-permute-done | bytes 32800 | tf_op jit(solution)/shard_map/ppermute | solution.py:20
  128.9 2.8 %collective-permute-start.51 = (f32[64,128]{1,0:T(8,128)S(1)}, f32[64,128]{1,0:T(8,128)S(1)}, u32[]{:S(2)}, u32[]{:S(2)}) collective-permute-start(f32[64,128]{1,0:T(8,128)S(1)} %add.138), channel_id=1, source_target_pairs={{0,3},{1,2},{2,1},{3,0},{4,7},{5,6},{6,5},{7,4},{8,11},{9,10},{10,... | collective-permute-start | bytes 98312 | tf_op jit(solution)/shard_map/ppermute | solution.py:20
  132.3 2.4 %collective-permute-done.41.refs_3_ = bf16[1536,128]{1,0:T(8,128)(2,1)S(1)} collective-permute-done((bf16[1536,128]{1,0:T(8,128)(2,1)}, bf16[1536,128]{1,0:T(8,128)(2,1)S(1)}, u32[]{:S(2)}, u32[]{:S(2)}) %collective-permute-start.41) | collective-permute-done | bytes 393248 | tf_op jit(solution)/shard_map/ppermute | solution.py:20
  134.7 2.9 %shard_map.75 = (f32[1536,128]{1,0:T(8,128)}, f32[256,128]{1,0:T(8,128)S(1)}) custom-call(f32[1536,128]{1,0:T(8,128)} %copy-done, f32[1536,128]{1,0:T(8,128)} %get-tuple-element.118.refs_1_, bf16[1536,128]{1,0:T(8,128)(2,1)S(1)} %collective-permute-done.40.refs_2_, bf16[1536,128]{1,0:T(8,128)(2,1)S(1)} %collective-permute-done.41.refs_3_, ...), custom_call_target="tpu_custom_call" | custom-call | tf_op jit(solution)/shard_map/pallas_call | solution.py:239
  139.3 4.0 %collective-permute-done.47 = f32[128,128]{1,0:T(8,128)S(1)} collective-permute-done((f32[128,128]{1,0:T(8,128)S(1)}, f32[128,128]{1,0:T(8,128)S(1)}, u32[]{:S(2)}, u32[]{:S(2)}) %collective-permute-start.47) | collective-permute-done | bytes 65568 | tf_op jit(solution)/shard_map/ppermute | solution.py:20
  143.4 1.5 collective-permute-start.48
  144.9 4.9 %shard_map.76 = (f32[128,128]{1,0:T(8,128)S(1)}, f32[128,128]{1,0:T(8,128)S(1)}, f32[1536,128]{1,0:T(8,128)S(1)}) custom-call(f32[128,128]{1,0:T(8,128)S(1)} %maximum_select_fusion.1.gram_ref, f32[1536,128]{1,0:T(8,128)S(1)} %copy-done.1), custom_call_target="tpu_custom_call" | custom-call | tf_op jit(solution)/shard_map/pallas_call | solution.py:456
  151.4 2.0 %collective-permute-start.53 = (f32[128,128]{1,0:T(8,128)S(1)}, f32[128,128]{1,0:T(8,128)S(1)}, u32[]{:S(2)}, u32[]{:S(2)}) collective-permute-start(f32[128,128]{1,0:T(8,128)S(1)} %add.151), channel_id=1, source_target_pairs={{0,1},{1,0},{2,3},{3,2},{4,5},{5,4},{6,7},{7,6},{8,9},{9,8},{10,11... | collective-permute-start | bytes 196616 | tf_op jit(solution)/shard_map/ppermute | solution.py:20
  153.4 1.9 %collective-permute-done.55 = f32[128,128]{1,0:T(8,128)S(1)} collective-permute-done((f32[128,128]{1,0:T(8,128)S(1)}, f32[128,128]{1,0:T(8,128)S(1)}, u32[]{:S(2)}, u32[]{:S(2)}) %collective-permute-start.55) | collective-permute-done | bytes 65568 | tf_op jit(solution)/shard_map/ppermute | solution.py:20
  157.2 7.6 %shard_map.77 = (f32[1536,256]{1,0:T(8,128)}, f32[256,256]{1,0:T(8,128)}) custom-call(f32[256,128]{1,0:T(8,128)S(1)} %maximum_select_fusion.gram_ref, f32[128,128]{1,0:T(8,128)S(1)} %get-tuple-element.125.upper_ref, f32[128,128]{1,0:T(8,128)S(1)} %get-tuple-element.127.inverse_ref, f32[1536,128]{1,0:T(8,128)S(1)} %get-tuple-element.128.first_ref, ...), custom_call_target="tpu_custom_call" | custom-call | tf_op jit(solution)/shard_map/pallas_call | solution.py:463
  (122 shorter events, 22.7 us)
Async XLA Ops:
  2.1 9.7 %collective-permute-start.8 = (bf16[64,1536]{1,0:T(8,128)(2,1)S(1)}, bf16[64,1536]{1,0:T(8,128)(2,1)S(1)}, u32[]{:S(2)}, u32[]{:S(2)}) collective-permute-start(bf16[64,1536]{1,0:T(8,128)(2,1)S(1)} %get-tuple-element.67.refs_0_), channel_id=1, source_target_pairs={{0,3},{1,2},{2,1},{3,0},{4,7},{5,6},{6,5},{7,4},{8,11},{9,10},{10,... | collective-permute-start | bytes 589832 | tf_op jit(solution)/shard_map/ppermute | solution.py:20
  6.0 9.2 %collective-permute-start.7 = (bf16[64,1536]{1,0:T(8,128)(2,1)S(1)}, bf16[64,1536]{1,0:T(8,128)(2,1)S(1)}, u32[]{:S(2)}, u32[]{:S(2)}) collective-permute-start(bf16[64,1536]{1,0:T(8,128)(2,1)S(1)} %get-tuple-element.67.refs_0_), channel_id=1, source_target_pairs={{0,2},{1,3},{2,0},{3,1},{4,6},{5,7},{6,4},{7,5},{8,10},{9,11},{10,... | collective-permute-start | bytes 589832 | tf_op jit(solution)/shard_map/ppermute | solution.py:20
  6.5 11.1 %collective-permute-start.6 = (bf16[64,1536]{1,0:T(8,128)(2,1)S(1)}, bf16[64,1536]{1,0:T(8,128)(2,1)S(1)}, u32[]{:S(2)}, u32[]{:S(2)}) collective-permute-start(bf16[64,1536]{1,0:T(8,128)(2,1)S(1)} %get-tuple-element.67.refs_0_), channel_id=1, source_target_pairs={{0,1},{1,0},{2,3},{3,2},{4,5},{5,4},{6,7},{7,6},{8,9},{9,8},{10,11... | collective-permute-start | bytes 589832 | tf_op jit(solution)/shard_map/ppermute | solution.py:20
  6.7 15.3 %collective-permute-start.3 = (bf16[48,1536]{1,0:T(8,128)(2,1)S(1)}, bf16[48,1536]{1,0:T(8,128)(2,1)S(1)}, u32[]{:S(2)}, u32[]{:S(2)}) collective-permute-start(bf16[48,1536]{1,0:T(8,128)(2,1)S(1)} %get-tuple-element.136), channel_id=1, source_target_pairs={{0,2},{1,3},{2,0},{3,1},{4,6},{5,7},{6,4},{7,5},{8,10},{9,11},{10,... | collective-permute-start | bytes 442376 | tf_op jit(solution)/shard_map/ppermute | solution.py:20
  8.7 13.3 %collective-permute-start.1 = (bf16[48,1536]{1,0:T(8,128)(2,1)S(1)}, bf16[48,1536]{1,0:T(8,128)(2,1)S(1)}, u32[]{:S(2)}, u32[]{:S(2)}) collective-permute-start(bf16[48,1536]{1,0:T(8,128)(2,1)S(1)} %get-tuple-element.136), channel_id=1, source_target_pairs={{0,1},{1,0},{2,3},{3,2},{4,5},{5,4},{6,7},{7,6},{8,9},{9,8},{10,11... | collective-permute-start | bytes 442376 | tf_op jit(solution)/shard_map/ppermute | solution.py:20
  11.8 10.2 %collective-permute-start.2 = (bf16[48,1536]{1,0:T(8,128)(2,1)S(1)}, bf16[48,1536]{1,0:T(8,128)(2,1)S(1)}, u32[]{:S(2)}, u32[]{:S(2)}) collective-permute-start(bf16[48,1536]{1,0:T(8,128)(2,1)S(1)} %get-tuple-element.137), channel_id=1, source_target_pairs={{0,2},{1,3},{2,0},{3,1},{4,6},{5,7},{6,4},{7,5},{8,10},{9,11},{10,... | collective-permute-start | bytes 442376 | tf_op jit(solution)/shard_map/ppermute | solution.py:20
  15.3 6.8 %collective-permute-start = (bf16[48,1536]{1,0:T(8,128)(2,1)S(1)}, bf16[48,1536]{1,0:T(8,128)(2,1)S(1)}, u32[]{:S(2)}, u32[]{:S(2)}) collective-permute-start(bf16[48,1536]{1,0:T(8,128)(2,1)S(1)} %get-tuple-element.137), channel_id=1, source_target_pairs={{0,1},{1,0},{2,3},{3,2},{4,5},{5,4},{6,7},{7,6},{8,9},{9,8},{10,11... | collective-permute-start | bytes 442376 | tf_op jit(solution)/shard_map/ppermute | solution.py:20
  22.1 6.3 %collective-permute-start.5 = (bf16[48,1536]{1,0:T(8,128)(2,1)S(1)}, bf16[48,1536]{1,0:T(8,128)(2,1)S(1)}, u32[]{:S(2)}, u32[]{:S(2)}) collective-permute-start(bf16[48,1536]{1,0:T(8,128)(2,1)S(1)} %collective-permute-done.1.refs_2_), channel_id=1, source_target_pairs={{0,2},{1,3},{2,0},{3,1},{4,6},{5,7},{6,4},{7,5},{8,10},{9,11},{10,... | collective-permute-start | bytes 442376 | tf_op jit(solution)/shard_map/ppermute | solution.py:20
  23.7 6.2 %collective-permute-start.4 = (bf16[48,1536]{1,0:T(8,128)(2,1)S(1)}, bf16[48,1536]{1,0:T(8,128)(2,1)S(1)}, u32[]{:S(2)}, u32[]{:S(2)}) collective-permute-start(bf16[48,1536]{1,0:T(8,128)(2,1)S(1)} %collective-permute-done.2.refs_3_), channel_id=1, source_target_pairs={{0,1},{1,0},{2,3},{3,2},{4,5},{5,4},{6,7},{7,6},{8,9},{9,8},{10,11... | collective-permute-start | bytes 442376 | tf_op jit(solution)/shard_map/ppermute | solution.py:20
  25.3 11.5 %collective-permute-start.14 = (f16[32,6144]{1,0:T(8,128)(2,1)S(1)}, f16[32,6144]{1,0:T(8,128)(2,1)S(1)}, u32[]{:S(2)}, u32[]{:S(2)}) collective-permute-start(f16[32,6144]{1,0:T(8,128)(2,1)S(1)} %multiply_convert_fusion), channel_id=1, source_target_pairs={{0,8},{4,12},{8,0},{12,4},{16,24},{20,28},{24,16},{28,20},{1,9},{5... | collective-permute-start | bytes 1179656 | tf_op jit(solution)/shard_map/ppermute | solution.py:20
  26.0 10.8 %collective-permute-start.13 = (bf16[48,1536]{1,0:T(8,128)(2,1)S(1)}, bf16[48,1536]{1,0:T(8,128)(2,1)S(1)}, u32[]{:S(2)}, u32[]{:S(2)}) collective-permute-start(bf16[48,1536]{1,0:T(8,128)(2,1)S(1)} %get-tuple-element.134), channel_id=1, source_target_pairs={{0,2},{1,3},{2,0},{3,1},{4,6},{5,7},{6,4},{7,5},{8,10},{9,11},{10,... | collective-permute-start | bytes 442376 | tf_op jit(solution)/shard_map/ppermute | solution.py:20
  27.7 9.1 %collective-permute-start.11 = (bf16[48,1536]{1,0:T(8,128)(2,1)S(1)}, bf16[48,1536]{1,0:T(8,128)(2,1)S(1)}, u32[]{:S(2)}, u32[]{:S(2)}) collective-permute-start(bf16[48,1536]{1,0:T(8,128)(2,1)S(1)} %get-tuple-element.134), channel_id=1, source_target_pairs={{0,1},{1,0},{2,3},{3,2},{4,5},{5,4},{6,7},{7,6},{8,9},{9,8},{10,11... | collective-permute-start | bytes 442376 | tf_op jit(solution)/shard_map/ppermute | solution.py:20
  28.4 8.4 %collective-permute-start.12 = (bf16[48,1536]{1,0:T(8,128)(2,1)S(1)}, bf16[48,1536]{1,0:T(8,128)(2,1)S(1)}, u32[]{:S(2)}, u32[]{:S(2)}) collective-permute-start(bf16[48,1536]{1,0:T(8,128)(2,1)S(1)} %get-tuple-element.135), channel_id=1, source_target_pairs={{0,2},{1,3},{2,0},{3,1},{4,6},{5,7},{6,4},{7,5},{8,10},{9,11},{10,... | collective-permute-start | bytes 442376 | tf_op jit(solution)/shard_map/ppermute | solution.py:20
  30.0 6.9 %collective-permute-start.10 = (bf16[48,1536]{1,0:T(8,128)(2,1)S(1)}, bf16[48,1536]{1,0:T(8,128)(2,1)S(1)}, u32[]{:S(2)}, u32[]{:S(2)}) collective-permute-start(bf16[48,1536]{1,0:T(8,128)(2,1)S(1)} %get-tuple-element.135), channel_id=1, source_target_pairs={{0,1},{1,0},{2,3},{3,2},{4,5},{5,4},{6,7},{7,6},{8,9},{9,8},{10,11... | collective-permute-start | bytes 442376 | tf_op jit(solution)/shard_map/ppermute | solution.py:20
  36.9 7.2 %collective-permute-start.18 = (bf16[48,1536]{1,0:T(8,128)(2,1)S(1)}, bf16[48,1536]{1,0:T(8,128)(2,1)S(1)}, u32[]{:S(2)}, u32[]{:S(2)}) collective-permute-start(bf16[48,1536]{1,0:T(8,128)(2,1)S(1)} %collective-permute-done.11.refs_2_), channel_id=1, source_target_pairs={{0,2},{1,3},{2,0},{3,1},{4,6},{5,7},{6,4},{7,5},{8,10},{9,11},{10,... | collective-permute-start | bytes 442376 | tf_op jit(solution)/shard_map/ppermute | solution.py:20
  37.5 6.6 %collective-permute-start.17 = (bf16[48,1536]{1,0:T(8,128)(2,1)S(1)}, bf16[48,1536]{1,0:T(8,128)(2,1)S(1)}, u32[]{:S(2)}, u32[]{:S(2)}) collective-permute-start(bf16[48,1536]{1,0:T(8,128)(2,1)S(1)} %collective-permute-done.12.refs_3_), channel_id=1, source_target_pairs={{0,1},{1,0},{2,3},{3,2},{4,5},{5,4},{6,7},{7,6},{8,9},{9,8},{10,11... | collective-permute-start | bytes 442376 | tf_op jit(solution)/shard_map/ppermute | solution.py:20
  41.2 12.4 %collective-permute-start.16 = (f16[16,6144]{1,0:T(8,128)(2,1)S(1)}, f16[16,6144]{1,0:T(8,128)(2,1)S(1)}, u32[]{:S(2)}, u32[]{:S(2)}) collective-permute-start(f16[16,6144]{1,0:T(8,128)(2,1)S(1)} %get-tuple-element.133), channel_id=1, source_target_pairs={{0,16},{4,20},{8,24},{12,28},{16,0},{20,4},{24,8},{28,12},{1,17},{... | collective-permute-start | bytes 589832 | tf_op jit(solution)/shard_map/ppermute | solution.py:20
  44.2 10.2 %collective-permute-start.19 = (f16[16,6144]{1,0:T(8,128)(2,1)S(1)}, f16[16,6144]{1,0:T(8,128)(2,1)S(1)}, u32[]{:S(2)}, u32[]{:S(2)}) collective-permute-start(f16[16,6144]{1,0:T(8,128)(2,1)S(1)} %multiply_convert_fusion.2), channel_id=1, source_target_pairs={{0,8},{4,12},{8,0},{12,4},{16,24},{20,28},{24,16},{28,20},{1,9},{5... | collective-permute-start | bytes 589832 | tf_op jit(solution)/shard_map/ppermute | solution.py:20
  54.4 5.3 %collective-permute-start.22 = (f32[48,6144]{1,0:T(8,128)}, f32[48,6144]{1,0:T(8,128)S(1)}, u32[]{:S(2)}, u32[]{:S(2)}) collective-permute-start(f32[48,6144]{1,0:T(8,128)} %get-tuple-element.95), channel_id=1, source_target_pairs={{0,4},{4,0},{8,12},{12,8},{16,20},{20,16},{24,28},{28,24},{1,5},{5... | collective-permute-start | bytes 3538952 | tf_op jit(solution)/shard_map/ppermute | solution.py:20
  55.5 12.6 %collective-permute-start.21 = (bf16[16,6144]{1,0:T(8,128)(2,1)S(1)}, bf16[16,6144]{1,0:T(8,128)(2,1)S(1)}, u32[]{:S(2)}, u32[]{:S(2)}) collective-permute-start(bf16[16,6144]{1,0:T(8,128)(2,1)S(1)} %fusion.11.refs_0_), channel_id=1, source_target_pairs={{0,16},{4,20},{8,24},{12,28},{16,0},{20,4},{24,8},{28,12},{1,17},{... | collective-permute-start | bytes 589832 | tf_op jit(solution)/shard_map/ppermute | solution.py:20
  57.2 11.0 %collective-permute-start.20 = (bf16[16,6144]{1,0:T(8,128)(2,1)S(1)}, bf16[16,6144]{1,0:T(8,128)(2,1)S(1)}, u32[]{:S(2)}, u32[]{:S(2)}) collective-permute-start(bf16[16,6144]{1,0:T(8,128)(2,1)S(1)} %fusion.11.refs_0_), channel_id=1, source_target_pairs={{0,8},{4,12},{8,0},{12,4},{16,24},{20,28},{24,16},{28,20},{1,9},{5... | collective-permute-start | bytes 589832 | tf_op jit(solution)/shard_map/ppermute | solution.py:20
  68.1 9.2 %collective-permute-start.23 = (bf16[16,6144]{1,0:T(8,128)(2,1)S(1)}, bf16[16,6144]{1,0:T(8,128)(2,1)S(1)}, u32[]{:S(2)}, u32[]{:S(2)}) collective-permute-start(bf16[16,6144]{1,0:T(8,128)(2,1)S(1)} %collective-permute-done.21.refs_2_), channel_id=1, source_target_pairs={{0,8},{4,12},{8,0},{12,4},{16,24},{20,28},{24,16},{28,20},{1,9},{5... | collective-permute-start | bytes 589832 | tf_op jit(solution)/shard_map/ppermute | solution.py:20
  68.1 9.2 %collective-permute-start.24 = (bf16[16,6144]{1,0:T(8,128)(2,1)S(1)}, bf16[16,6144]{1,0:T(8,128)(2,1)S(1)}, u32[]{:S(2)}, u32[]{:S(2)}) collective-permute-start(bf16[16,6144]{1,0:T(8,128)(2,1)S(1)} %fusion.11.refs_0_), channel_id=1, source_target_pairs={{0,4},{4,0},{8,12},{12,8},{16,20},{20,16},{24,28},{28,24},{1,5},{5... | collective-permute-start | bytes 589832 | tf_op jit(solution)/shard_map/ppermute | solution.py:20
  68.1 9.2 %collective-permute-start.25 = (bf16[16,6144]{1,0:T(8,128)(2,1)S(1)}, bf16[16,6144]{1,0:T(8,128)(2,1)S(1)}, u32[]{:S(2)}, u32[]{:S(2)}) collective-permute-start(bf16[16,6144]{1,0:T(8,128)(2,1)S(1)} %collective-permute-done.20.refs_1_), channel_id=1, source_target_pairs={{0,4},{4,0},{8,12},{12,8},{16,20},{20,16},{24,28},{28,24},{1,5},{5... | collective-permute-start | bytes 589832 | tf_op jit(solution)/shard_map/ppermute | solution.py:20
  68.6 8.8 %collective-permute-start.26 = (bf16[16,6144]{1,0:T(8,128)(2,1)S(1)}, bf16[16,6144]{1,0:T(8,128)(2,1)S(1)}, u32[]{:S(2)}, u32[]{:S(2)}) collective-permute-start(bf16[16,6144]{1,0:T(8,128)(2,1)S(1)} %collective-permute-done.21.refs_2_), channel_id=1, source_target_pairs={{0,4},{4,0},{8,12},{12,8},{16,20},{20,16},{24,28},{28,24},{1,5},{5... | collective-permute-start | bytes 589832 | tf_op jit(solution)/shard_map/ppermute | solution.py:20
  68.7 15.5 %collective-permute-start.31 = (f16[16,6144]{1,0:T(8,128)(2,1)S(1)}, f16[16,6144]{1,0:T(8,128)(2,1)S(1)}, u32[]{:S(2)}, u32[]{:S(2)}) collective-permute-start(f16[16,6144]{1,0:T(8,128)(2,1)S(1)} %get-tuple-element.131), channel_id=1, source_target_pairs={{0,16},{4,20},{8,24},{12,28},{16,0},{20,4},{24,8},{28,12},{1,17},{... | collective-permute-start | bytes 589832 | tf_op jit(solution)/shard_map/ppermute | solution.py:20
  77.3 8.5 %collective-permute-start.32 = (f16[16,6144]{1,0:T(8,128)(2,1)S(1)}, f16[16,6144]{1,0:T(8,128)(2,1)S(1)}, u32[]{:S(2)}, u32[]{:S(2)}) collective-permute-start(f16[16,6144]{1,0:T(8,128)(2,1)S(1)} %multiply_convert_fusion.1), channel_id=1, source_target_pairs={{0,8},{4,12},{8,0},{12,4},{16,24},{20,28},{24,16},{28,20},{1,9},{5... | collective-permute-start | bytes 589832 | tf_op jit(solution)/shard_map/ppermute | solution.py:20
  85.9 11.6 %collective-permute-start.34 = (bf16[16,6144]{1,0:T(8,128)(2,1)S(1)}, bf16[16,6144]{1,0:T(8,128)(2,1)S(1)}, u32[]{:S(2)}, u32[]{:S(2)}) collective-permute-start(bf16[16,6144]{1,0:T(8,128)(2,1)S(1)} %fusion.2.refs_0_), channel_id=1, source_target_pairs={{0,16},{4,20},{8,24},{12,28},{16,0},{20,4},{24,8},{28,12},{1,17},{... | collective-permute-start | bytes 589832 | tf_op jit(solution)/shard_map/ppermute | solution.py:20
  86.3 18.0 %collective-permute-start.28 = (bf16[1536,128]{1,0:T(8,128)(2,1)S(1)}, bf16[1536,128]{1,0:T(8,128)(2,1)S(1)}, u32[]{:S(2)}, u32[]{:S(2)}) collective-permute-start(bf16[1536,128]{1,0:T(8,128)(2,1)S(1)} %get-tuple-element.99), channel_id=1, source_target_pairs={{0,1},{1,0},{2,3},{3,2},{4,5},{5,4},{6,7},{7,6},{8,9},{9,8},{10,11... | collective-permute-start | bytes 1179656 | tf_op jit(solution)/shard_map/ppermute | solution.py:20
  88.1 16.2 %collective-permute-start.29 = (bf16[1536,128]{1,0:T(8,128)(2,1)S(1)}, bf16[1536,128]{1,0:T(8,128)(2,1)S(1)}, u32[]{:S(2)}, u32[]{:S(2)}) collective-permute-start(bf16[1536,128]{1,0:T(8,128)(2,1)S(1)} %copy-done.9), channel_id=1, source_target_pairs={{0,2},{1,3},{2,0},{3,1},{4,6},{5,7},{6,4},{7,5},{8,10},{9,11},{10,... | collective-permute-start | bytes 1179656 | tf_op jit(solution)/shard_map/ppermute | solution.py:20
  89.1 10.9 %collective-permute-start.33 = (bf16[16,6144]{1,0:T(8,128)(2,1)S(1)}, bf16[16,6144]{1,0:T(8,128)(2,1)S(1)}, u32[]{:S(2)}, u32[]{:S(2)}) collective-permute-start(bf16[16,6144]{1,0:T(8,128)(2,1)S(1)} %fusion.2.refs_0_), channel_id=1, source_target_pairs={{0,8},{4,12},{8,0},{12,4},{16,24},{20,28},{24,16},{28,20},{1,9},{5... | collective-permute-start | bytes 589832 | tf_op jit(solution)/shard_map/ppermute | solution.py:20
  97.5 6.8 %collective-permute-start.35 = (bf16[16,6144]{1,0:T(8,128)(2,1)S(1)}, bf16[16,6144]{1,0:T(8,128)(2,1)S(1)}, u32[]{:S(2)}, u32[]{:S(2)}) collective-permute-start(bf16[16,6144]{1,0:T(8,128)(2,1)S(1)} %collective-permute-done.34.refs_2_), channel_id=1, source_target_pairs={{0,8},{4,12},{8,0},{12,4},{16,24},{20,28},{24,16},{28,20},{1,9},{5... | collective-permute-start | bytes 589832 | tf_op jit(solution)/shard_map/ppermute | solution.py:20
  97.5 14.5 %collective-permute-start.30 = (bf16[1536,128]{1,0:T(8,128)(2,1)S(1)}, bf16[1536,128]{1,0:T(8,128)(2,1)S(1)}, u32[]{:S(2)}, u32[]{:S(2)}) collective-permute-start(bf16[1536,128]{1,0:T(8,128)(2,1)S(1)} %copy-done.8), channel_id=1, source_target_pairs={{0,3},{1,2},{2,1},{3,0},{4,7},{5,6},{6,5},{7,4},{8,11},{9,10},{10,... | collective-permute-start | bytes 1179656 | tf_op jit(solution)/shard_map/ppermute | solution.py:20
  100.0 4.9 %collective-permute-start.36 = (bf16[16,6144]{1,0:T(8,128)(2,1)S(1)}, bf16[16,6144]{1,0:T(8,128)(2,1)S(1)}, u32[]{:S(2)}, u32[]{:S(2)}) collective-permute-start(bf16[16,6144]{1,0:T(8,128)(2,1)S(1)} %fusion.2.refs_0_), channel_id=1, source_target_pairs={{0,4},{4,0},{8,12},{12,8},{16,20},{20,16},{24,28},{28,24},{1,5},{5... | collective-permute-start | bytes 589832 | tf_op jit(solution)/shard_map/ppermute | solution.py:20
  112.0 12.1 %collective-permute-start.40 = (bf16[1536,128]{1,0:T(8,128)(2,1)S(1)}, bf16[1536,128]{1,0:T(8,128)(2,1)S(1)}, u32[]{:S(2)}, u32[]{:S(2)}) collective-permute-start(bf16[1536,128]{1,0:T(8,128)(2,1)S(1)} %get-tuple-element.111), channel_id=1, source_target_pairs={{0,1},{1,0},{2,3},{3,2},{4,5},{5,4},{6,7},{7,6},{8,9},{9,8},{10,11... | collective-permute-start | bytes 1179656 | tf_op jit(solution)/shard_map/ppermute | solution.py:20
  113.6 21.1 %collective-permute-start.41 = (bf16[1536,128]{1,0:T(8,128)(2,1)}, bf16[1536,128]{1,0:T(8,128)(2,1)S(1)}, u32[]{:S(2)}, u32[]{:S(2)}) collective-permute-start(bf16[1536,128]{1,0:T(8,128)(2,1)} %get-tuple-element.112), channel_id=1, source_target_pairs={{0,2},{1,3},{2,0},{3,1},{4,6},{5,7},{6,4},{7,5},{8,10},{9,11},{10,... | collective-permute-start | bytes 1179656 | tf_op jit(solution)/shard_map/ppermute | solution.py:20
  115.3 19.4 %collective-permute-start.42 = (bf16[1536,128]{1,0:T(8,128)(2,1)}, bf16[1536,128]{1,0:T(8,128)(2,1)S(1)}, u32[]{:S(2)}, u32[]{:S(2)}) collective-permute-start(bf16[1536,128]{1,0:T(8,128)(2,1)} %get-tuple-element.113), channel_id=1, source_target_pairs={{0,3},{1,2},{2,1},{3,0},{4,7},{5,6},{6,5},{7,4},{8,11},{9,10},{10,... | collective-permute-start | bytes 1179656 | tf_op jit(solution)/shard_map/ppermute | solution.py:20
  119.7 3.9 %collective-permute-start.44 = (f32[64,128]{1,0:T(8,128)S(1)}, f32[64,128]{1,0:T(8,128)S(1)}, u32[]{:S(2)}, u32[]{:S(2)}) collective-permute-start(f32[64,128]{1,0:T(8,128)S(1)} %dynamic-slice_add_fusion.1), channel_id=1, source_target_pairs={{0,8},{4,12},{8,0},{12,4},{16,24},{20,28},{24,16},{28,20},{1,9},{5... | collective-permute-start | bytes 98312 | tf_op jit(solution)/shard_map/ppermute | solution.py:20
  124.0 4.8 %collective-permute-start.45 = (f32[64,128]{1,0:T(8,128)S(1)}, f32[64,128]{1,0:T(8,128)S(1)}, u32[]{:S(2)}, u32[]{:S(2)}) collective-permute-start(f32[64,128]{1,0:T(8,128)S(1)} %add.137), channel_id=1, source_target_pairs={{0,16},{4,20},{8,24},{12,28},{16,0},{20,4},{24,8},{28,12},{1,17},{... | collective-permute-start | bytes 98312 | tf_op jit(solution)/shard_map/ppermute | solution.py:20
  128.9 8.9 %collective-permute-start.51 = (f32[64,128]{1,0:T(8,128)S(1)}, f32[64,128]{1,0:T(8,128)S(1)}, u32[]{:S(2)}, u32[]{:S(2)}) collective-permute-start(f32[64,128]{1,0:T(8,128)S(1)} %add.138), channel_id=1, source_target_pairs={{0,3},{1,2},{2,1},{3,0},{4,7},{5,6},{6,5},{7,4},{8,11},{9,10},{10,... | collective-permute-start | bytes 98312 | tf_op jit(solution)/shard_map/ppermute | solution.py:20
  131.6 6.1 %collective-permute-start.50 = (f32[64,128]{1,0:T(8,128)S(1)}, f32[64,128]{1,0:T(8,128)S(1)}, u32[]{:S(2)}, u32[]{:S(2)}) collective-permute-start(f32[64,128]{1,0:T(8,128)S(1)} %add.138), channel_id=1, source_target_pairs={{0,2},{1,3},{2,0},{3,1},{4,6},{5,7},{6,4},{7,5},{8,10},{9,11},{10,... | collective-permute-start | bytes 98312 | tf_op jit(solution)/shard_map/ppermute | solution.py:20
  131.9 5.9 %collective-permute-start.49 = (f32[64,128]{1,0:T(8,128)S(1)}, f32[64,128]{1,0:T(8,128)S(1)}, u32[]{:S(2)}, u32[]{:S(2)}) collective-permute-start(f32[64,128]{1,0:T(8,128)S(1)} %add.138), channel_id=1, source_target_pairs={{0,1},{1,0},{2,3},{3,2},{4,5},{5,4},{6,7},{7,6},{8,9},{9,8},{10,11... | collective-permute-start | bytes 98312 | tf_op jit(solution)/shard_map/ppermute | solution.py:20
  139.0 4.3 %collective-permute-start.47 = (f32[128,128]{1,0:T(8,128)S(1)}, f32[128,128]{1,0:T(8,128)S(1)}, u32[]{:S(2)}, u32[]{:S(2)}) collective-permute-start(f32[128,128]{1,0:T(8,128)S(1)} %dynamic-slice_add_fusion), channel_id=1, source_target_pairs={{0,8},{4,12},{8,0},{12,4},{16,24},{20,28},{24,16},{28,20},{1,9},{5... | collective-permute-start | bytes 196616 | tf_op jit(solution)/shard_map/ppermute | solution.py:20
  139.1 5.8 %collective-permute-start.52 = (f32[64,128]{1,0:T(8,128)S(1)}, f32[64,128]{1,0:T(8,128)S(1)}, u32[]{:S(2)}, u32[]{:S(2)}) collective-permute-start(f32[64,128]{1,0:T(8,128)S(1)} %add_bitcast_fusion.1), channel_id=1, source_target_pairs={{0,4},{4,0},{8,12},{12,8},{16,20},{20,16},{24,28},{28,24},{1,5},{5... | collective-permute-start | bytes 98312 | tf_op jit(solution)/shard_map/ppermute | solution.py:20
  143.4 6.5 %collective-permute-start.48 = (f32[128,128]{1,0:T(8,128)S(1)}, f32[128,128]{1,0:T(8,128)S(1)}, u32[]{:S(2)}, u32[]{:S(2)}) collective-permute-start(f32[128,128]{1,0:T(8,128)S(1)} %add.142), channel_id=1, source_target_pairs={{0,16},{4,20},{8,24},{12,28},{16,0},{20,4},{24,8},{28,12},{1,17},{... | collective-permute-start | bytes 196616 | tf_op jit(solution)/shard_map/ppermute | solution.py:20
  149.9 5.4 %collective-permute-start.55 = (f32[128,128]{1,0:T(8,128)S(1)}, f32[128,128]{1,0:T(8,128)S(1)}, u32[]{:S(2)}, u32[]{:S(2)}) collective-permute-start(f32[128,128]{1,0:T(8,128)S(1)} %add.151), channel_id=1, source_target_pairs={{0,3},{1,2},{2,1},{3,0},{4,7},{5,6},{6,5},{7,4},{8,11},{9,10},{10,... | collective-permute-start | bytes 196616 | tf_op jit(solution)/shard_map/ppermute | solution.py:20
  150.9 4.9 %collective-permute-start.54 = (f32[128,128]{1,0:T(8,128)S(1)}, f32[128,128]{1,0:T(8,128)S(1)}, u32[]{:S(2)}, u32[]{:S(2)}) collective-permute-start(f32[128,128]{1,0:T(8,128)S(1)} %add.151), channel_id=1, source_target_pairs={{0,2},{1,3},{2,0},{3,1},{4,6},{5,7},{6,4},{7,5},{8,10},{9,11},{10,... | collective-permute-start | bytes 196616 | tf_op jit(solution)/shard_map/ppermute | solution.py:20
  151.4 4.4 %collective-permute-start.53 = (f32[128,128]{1,0:T(8,128)S(1)}, f32[128,128]{1,0:T(8,128)S(1)}, u32[]{:S(2)}, u32[]{:S(2)}) collective-permute-start(f32[128,128]{1,0:T(8,128)S(1)} %add.151), channel_id=1, source_target_pairs={{0,1},{1,0},{2,3},{3,2},{4,5},{5,4},{6,7},{7,6},{8,9},{9,8},{10,11... | collective-permute-start | bytes 196616 | tf_op jit(solution)/shard_map/ppermute | solution.py:20
  (20 other events, 115.5 us)
